TPU v7x, 32 devices: a whole 2x2x4 slice. The times are simulated.
32 devices in a mesh: dp: 16 (over z, y, x), shard: 2 (over core).
Axes of the slice: x: 2, y: 2, z: 4, core: 2. Of those that a mesh axis runs over, the one named last changes fastest.
Arguments:
- features: bfloat16 [65536, 100], P(('dp', 'shard')), may hold values from -6 to 6
- neighbors: int32 [65536, 8], P(('dp', 'shard')), may hold values from 0 to 1023
- label_mask: int32 [65536], P(('dp', 'shard')), may hold values from 0 to 1
- labels: int32 [65536], P(('dp', 'shard')), may hold values from 0 to 46
- w_first: float32 [100, 2048], P(None, ('dp', 'shard')), may hold values from -0.625 to 0.625
- w_second: float32 [2048, 47], P(('dp', 'shard')), may hold values from -0.125 to 0.125
- b_first: float32 [2048], P(('dp', 'shard')), may hold values from -0.6 to 0.6
- b_second: float32 [47], replicated, may hold values from -1.8 to 1.8
- l_first: float32 [100, 100], replicated
- r_first: float32 [2048, 2048], P(None, ('dp', 'shard'))
- l_second: float32 [2048, 2048], P(('dp', 'shard'))
- r_second: float32 [47, 47], replicated
- l_first_root: float32 [100, 100], replicated
- r_first_root: float32 [2048, 2048], P(None, ('dp', 'shard'))
- l_second_root: float32 [2048, 2048], P(('dp', 'shard'))
- r_second_root: float32 [47, 47], replicated
- m_first: float32 [2048], P(('dp', 'shard'))
- v_first: float32 [2048], P(('dp', 'shard')), as said below
- m_second: float32 [47], replicated
- v_second: float32 [47], replicated, as said below
Outputs:
- loss_sum: float32 [], replicated
- label_count: float32 [], replicated
- clip_norm: float32 [], replicated
- grad_first: float32 [100, 2048], P(None, ('dp', 'shard'))
- grad_second: float32 [2048, 47], P(('dp', 'shard'))
- new_w_first: float32 [100, 2048], P(None, ('dp', 'shard'))
- new_w_second: float32 [2048, 47], P(('dp', 'shard'))
- new_l_first: float32 [100, 100], replicated
- new_r_first: float32 [2048, 2048], P(None, ('dp', 'shard'))
- new_l_second: float32 [2048, 2048], P(('dp', 'shard'))
- new_r_second: float32 [47, 47], replicated
- new_m_first: float32 [2048], P(('dp', 'shard'))
- new_v_first: float32 [2048], P(('dp', 'shard'))
- new_b_first: float32 [2048], P(('dp', 'shard'))
- new_m_second: float32 [47], replicated
- new_v_second: float32 [47], replicated
- new_b_second: float32 [47], replicated
Inputs may be any that keep to these rules, and one draw needn't show every extreme that they name: `neighbors`: each entry is a row within the node's own block of 1024 consecutive rows. `v_first`: positive. `v_second`: positive.
All inputs are finite; a program needn't handle non-finite values.
Results may differ from a plain program's by a relative error of at most 0.0057.
Values may be sent and summed in bfloat16 or wider, within the bound.
No kernel may reach another device: no remote copies, remote signals or barrier semaphores. Data moves between devices by JAX's collectives and lax.ppermute only.
A program may use at most 128 MiB of HBM per device.

v0:
```python
import jax
import jax.numpy as jnp
from jax import lax
from jax.sharding import PartitionSpec as P

MB = 2
STEP = 10


clip_limit = 0.05
beta_stat = 0.95
beta_one = 0.9
beta_two = 0.999
adam_eps = 1e-08
decay_rate = 0.01
rate_bias = 0.2
rate_first = 1000.0
rate_second = 300.0
highest = lax.Precision.HIGHEST


def adjacency(neighbors):
    node_count = neighbors.shape[0]
    columns = jnp.arange(node_count, dtype=jnp.int32)
    counts = jnp.sum((neighbors[:, :, None] == columns[None, None, :]).astype(jnp.float32), axis=1)
    identity = jnp.eye(node_count, dtype=jnp.float32)
    self_count = jnp.sum(counts * identity, axis=1)
    return (counts + identity * (2.0 + self_count)[:, None]).astype(jnp.bfloat16)


def forward(feature_rows, neighbor_rows, first_full, second_full, bias_full, bias_two):
    matrix = adjacency(neighbor_rows)
    scale_in = 1.0 / (neighbor_rows.shape[1] + 1)
    pooled_one = (
        jnp.dot(matrix, feature_rows, preferred_element_type=jnp.float32) * scale_in
    ).astype(jnp.bfloat16)
    hidden_pre = jnp.dot(
        pooled_one, first_full, preferred_element_type=jnp.float32
    ) + bias_full.astype(jnp.float32)
    hidden = jax.nn.gelu(hidden_pre).astype(jnp.bfloat16)
    pooled_two = (jnp.dot(matrix, hidden, preferred_element_type=jnp.float32) * scale_in).astype(
        jnp.bfloat16
    )
    logits = jnp.dot(pooled_two, second_full, preferred_element_type=jnp.float32) + bias_two
    return (matrix, pooled_one, hidden_pre, pooled_two, logits)


def backward(saved, mask_rows, label_rows, second_full, denom, scale_in):
    matrix, pooled_one, hidden_pre, pooled_two, logits = saved
    log_prob = jax.nn.log_softmax(logits, axis=-1)
    onehot = (label_rows[:, None] == jnp.arange(logits.shape[1], dtype=jnp.int32)[None, :]).astype(
        jnp.float32
    )
    weight = mask_rows.astype(jnp.float32)
    loss_part = jnp.sum(-jnp.sum(log_prob * onehot, axis=-1) * weight)
    grad_logits = ((jnp.exp(log_prob) - onehot) * (weight / denom)[:, None]).astype(jnp.bfloat16)
    grad_second = jnp.einsum(
        "nh,nc->hc", pooled_two, grad_logits, preferred_element_type=jnp.float32
    )
    grad_bias_two = jnp.sum(grad_logits.astype(jnp.float32), axis=0)
    grad_pooled = jnp.einsum(
        "nc,hc->nh", grad_logits, second_full, preferred_element_type=jnp.float32
    ).astype(jnp.bfloat16)
    grad_hidden = (
        jnp.einsum("nm,nh->mh", matrix, grad_pooled, preferred_element_type=jnp.float32) * scale_in
    )
    grad_pre = jax.vjp(jax.nn.gelu, hidden_pre)[1](grad_hidden)[0].astype(jnp.bfloat16)
    grad_first = jnp.einsum("nf,nh->fh", pooled_one, grad_pre, preferred_element_type=jnp.float32)
    grad_bias_one = jnp.sum(grad_pre.astype(jnp.float32), axis=0)
    return (loss_part, grad_first, grad_second, grad_bias_one, grad_bias_two)


def fetch_weights(w_first, w_second, b_first):
    return (
        lax.all_gather(w_first.astype(jnp.bfloat16), ("dp", "shard"), axis=1, tiled=True),
        lax.all_gather(w_second.astype(jnp.bfloat16), ("dp", "shard"), axis=0, tiled=True),
        lax.all_gather(b_first.astype(jnp.bfloat16), ("dp", "shard"), axis=0, tiled=True),
    )


def adam_step(param, grad, first, second):
    first_new = beta_one * first + (1.0 - beta_one) * grad
    second_new = beta_two * second + (1.0 - beta_two) * grad * grad
    corr_one = 1.0 - beta_one**STEP
    corr_two = 1.0 - beta_two**STEP
    update = (
        first_new / corr_one / (jnp.sqrt(second_new / corr_two) + adam_eps) + decay_rate * param
    )
    return (first_new, second_new, param - rate_bias * update)


def per_device(
    features,
    neighbors,
    label_mask,
    labels,
    w_first,
    w_second,
    b_first,
    b_second,
    l_first,
    r_first,
    l_second,
    r_second,
    l_first_root,
    r_first_root,
    l_second_root,
    r_second_root,
    m_first,
    v_first,
    m_second,
    v_second,
):
    block_rows = features.shape[0] // MB
    scale_in = 1.0 / (neighbors.shape[1] + 1)
    label_count = lax.psum(jnp.sum(label_mask).astype(jnp.float32), ("dp", "shard"))
    denom = jnp.maximum(label_count, 1.0)
    acc_first = jnp.zeros(
        (w_first.shape[0], w_first.shape[1] * lax.axis_size(("dp", "shard"))), jnp.float32
    )
    acc_second = jnp.zeros(
        (w_second.shape[0] * lax.axis_size(("dp", "shard")), w_second.shape[1]), jnp.float32
    )
    acc_bias_one = jnp.zeros((b_first.shape[0] * lax.axis_size(("dp", "shard")),), jnp.float32)
    acc_bias_two = jnp.zeros_like(b_second)
    loss_local = jnp.zeros((), jnp.float32)
    for batch_index in range(MB):
        start = batch_index * block_rows
        first_full, second_full, bias_full = fetch_weights(w_first, w_second, b_first)
        saved = forward(
            features[start : start + block_rows],
            neighbors[start : start + block_rows],
            first_full,
            second_full,
            bias_full,
            b_second,
        )
        second_back = lax.all_gather(
            w_second.astype(jnp.bfloat16), ("dp", "shard"), axis=0, tiled=True
        )
        loss_part, grad_one, grad_two, grad_bias_one, grad_bias_two = backward(
            saved,
            label_mask[start : start + block_rows],
            labels[start : start + block_rows],
            second_back,
            denom,
            scale_in,
        )
        loss_local = loss_local + loss_part
        acc_first = acc_first + grad_one
        acc_second = acc_second + grad_two
        acc_bias_one = acc_bias_one + grad_bias_one
        acc_bias_two = acc_bias_two + grad_bias_two
    shard_one, shard_two, shard_bias_one = (
        lax.psum_scatter(acc_first, ("dp", "shard"), scatter_dimension=1, tiled=True),
        lax.psum_scatter(acc_second, ("dp", "shard"), scatter_dimension=0, tiled=True),
        lax.psum_scatter(acc_bias_one, ("dp", "shard"), scatter_dimension=0, tiled=True),
    )
    local_squares = (
        jnp.sum(shard_one * shard_one)
        + jnp.sum(shard_two * shard_two)
        + jnp.sum(shard_bias_one * shard_bias_one)
    )
    loss_sum, bias_two_grad, total_squares = lax.psum(
        (loss_local, acc_bias_two, local_squares), ("dp", "shard")
    )
    clip_norm = jnp.sqrt(total_squares + jnp.sum(bias_two_grad * bias_two_grad))
    factor = jnp.minimum(1.0, clip_limit / (clip_norm + 1e-06))
    own_one = shard_one * factor
    own_two = shard_two * factor
    own_bias_one = shard_bias_one * factor
    full_one, full_two = (
        lax.all_gather(own_one, ("dp", "shard"), axis=1, tiled=True),
        lax.all_gather(own_two, ("dp", "shard"), axis=0, tiled=True),
    )
    new_l_first = beta_stat * l_first + (1.0 - beta_stat) * jnp.dot(
        full_one, full_one.T, precision=highest
    )
    new_r_first = beta_stat * r_first + (1.0 - beta_stat) * jnp.dot(
        full_one.T, own_one, precision=highest
    )
    new_w_first = w_first - rate_first * jnp.dot(
        jnp.dot(l_first_root, full_one, precision=highest), r_first_root, precision=highest
    )
    new_l_second = beta_stat * l_second + (1.0 - beta_stat) * jnp.dot(
        own_two, full_two.T, precision=highest
    )
    new_r_second = beta_stat * r_second + (1.0 - beta_stat) * jnp.dot(
        full_two.T, full_two, precision=highest
    )
    new_w_second = w_second - rate_second * jnp.dot(
        jnp.dot(l_second_root, full_two, precision=highest), r_second_root, precision=highest
    )
    new_m_first, new_v_first, new_b_first = adam_step(b_first, own_bias_one, m_first, v_first)
    new_m_second, new_v_second, new_b_second = adam_step(
        b_second, bias_two_grad * factor, m_second, v_second
    )
    return (
        loss_sum,
        label_count,
        clip_norm,
        own_one,
        own_two,
        new_w_first,
        new_w_second,
        new_l_first,
        new_r_first,
        new_l_second,
        new_r_second,
        new_m_first,
        new_v_first,
        new_b_first,
        new_m_second,
        new_v_second,
        new_b_second,
    )


def solution(mesh):
    placed = (
        P(("dp", "shard"), None),
        P(("dp", "shard"), None),
        P(("dp", "shard")),
        P(("dp", "shard")),
        P(None, ("dp", "shard")),
        P(("dp", "shard"), None),
        P(("dp", "shard")),
        P(),
        P(),
        P(None, ("dp", "shard")),
        P(("dp", "shard"), None),
        P(),
        P(),
        P(None, ("dp", "shard")),
        P(("dp", "shard"), None),
        P(),
        P(("dp", "shard")),
        P(("dp", "shard")),
        P(),
        P(),
    )
    return jax.shard_map(
        per_device,
        mesh=mesh,
        in_specs=placed,
        out_specs=(
            P(),
            P(),
            P(),
            P(None, ("dp", "shard")),
            P(("dp", "shard"), None),
            P(None, ("dp", "shard")),
            P(("dp", "shard"), None),
            P(),
            P(None, ("dp", "shard")),
            P(("dp", "shard"), None),
            P(),
            P(("dp", "shard")),
            P(("dp", "shard")),
            P(("dp", "shard")),
            P(),
            P(),
            P(),
        ),
        check_vma=False,
    )
```

profile of v0, /device:TPU:0, one launch (start us, length us, event | category | flops | bytes accessed | tf_op | source)
XLA Modules:
  0.0 640.5 jit_solution(14413394267436363561)
XLA Ops:
  7.3 1.4 reduce_sum.170
  9.3 42.0 %psum.29 = f32[]{:T(128)} all-reduce(f32[]{:T(128)S(6)} %convert_element_type.111), channel_id=1, replica_groups=mesh['dp'=16,'shard'=2] {'dp','shard'}, use_global_device_ids=true, to_apply=%region_12.0 | all-reduce | flops 1 | bytes 8 | tf_op jit(solution)/shard_map/psum | solution.py:116
  54.6 1.4 fusion.42
  56.2 10.6 %convert_reduce_fusion = f32[1024,1024]{1,0:T(8,128)S(1)} fusion(s32[1024,8]{1,0:T(8,128)S(1)} %copy.49), kind=kLoop, calls=%fused_computation | loop fusion | flops 24117248 | bytes 4227072 | tf_op jit(solution)/shard_map/reduce_sum | solution.py:25
  67.5 41.9 %all_gather.20 = bf16[100,2048]{0,1:T(8,128)(2,1)S(1)} all-gather(bf16[100,64]{0,1:T(8,128)(2,1)S(1)} %convert_element_type.98), channel_id=1, replica_groups=mesh['dp'=16,'shard'=2] {'dp','shard'}, dimensions={1}, use_global_device_ids=true | all-gather | bytes 422400 | tf_op jit(solution)/shard_map/all_gather | solution.py:75
  109.6 36.9 %all-reduce = bf16[2048]{0:T(1024)(128)(2,1)S(1)} all-reduce(bf16[2048]{0:T(1024)(128)(2,1)S(1)} %dynamic-update-slice), channel_id=1, replica_groups=mesh['dp'=16,'shard'=2] {'dp','shard'}, use_global_device_ids=true, to_apply=%add | all-reduce | flops 2048 | bytes 8192
  147.1 41.3 %all-gather = bf16[32,64,47]{1,2,0:T(8,128)(2,1)S(1)} all-gather(bf16[1,64,47]{1,2,0:T(8,128)(2,1)S(1)} %convert_bitcast_fusion), channel_id=1, replica_groups=mesh['dp'=16,'shard'=2] {'dp','shard'}, dimensions={0}, use_global_device_ids=true | all-gather | bytes 198528 | tf_op jit(solution)/shard_map/all_gather | solution.py:76
  189.3 1.3 reshape.56
  190.7 1.7 fusion.23
  193.7 5.3 multiply_convert_fusion
  199.1 1.9 copy-done.1
  201.0 1.4 fusion.44
  203.4 10.6 %convert_reduce_fusion.1 = f32[1024,1024]{1,0:T(8,128)S(1)} fusion(s32[1024,8]{1,0:T(8,128)S(1)} %copy.47), kind=kLoop, calls=%fused_computation.2 | loop fusion | flops 24117248 | bytes 4227072 | tf_op jit(solution)/shard_map/reduce_sum | solution.py:25
  216.9 5.1 multiply_convert_fusion.2
  222.0 1.4 fusion.45
  226.1 1.4 copy.51
  227.6 17.2 %convert_reduce_fusion.3 = (f32[2048]{0:T(1024)}, bf16[1024,2048]{1,0:T(8,128)(2,1)}) fusion(f32[1024,2048]{1,0:T(8,128)} %copy-done.4, f32[2048]{0:T(1024)S(1)} %copy-done.31, bf16[1024,1024]{1,0:T(8,128)(2,1)} %copy-done.7, bf16[1024,47]{0,1:T(8,128)(2,1)S(1)} %get-tuple-element.51, bf16[2048,47]{0,1:T(8,128)(2,1)S(1)} %reshape.56), kind=kOutput, calls=%fused_computation.23 | convolution fusion | flops 4544526336 | bytes 14985216 | tf_op jit(solution)/shard_map/nm,nh->mh/dot_general | solution.py:65
  244.8 16.1 %convert_reduce_fusion.2 = (f32[2048]{0:T(1024)}, bf16[1024,2048]{1,0:T(8,128)(2,1)}) fusion(f32[1024,2048]{1,0:T(8,128)} %copy-done.3, f32[2048]{0:T(1024)S(1)} %copy-done.31, bf16[1024,1024]{1,0:T(8,128)(2,1)S(1)} %copy-done.6, bf16[1024,47]{0,1:T(8,128)(2,1)S(1)} %get-tuple-element.30, bf16[2048,47]{0,1:T(8,128)(2,1)S(1)} %reshape.56), kind=kOutput, calls=%fused_computation.22 | convolution fusion | flops 4544526336 | bytes 14985216 | tf_op jit(solution)/shard_map/nm,nh->mh/dot_general | solution.py:65
  261.0 4.0 fusion.48
  265.0 4.9 convolution_add_fusion
  272.1 37.2 %all-reduce.1 = f32[2048]{0:T(1024)S(1)} all-reduce(f32[2048]{0:T(1024)S(1)} %add.167), channel_id=4, replica_groups=mesh['dp'=16,'shard'=2] {'dp','shard'}, use_global_device_ids=true, to_apply=%region_19.0.clone | all-reduce | flops 2048 | bytes 16384
  310.0 48.8 %reduce-scatter.7.cloned.1.call-done = f32[64,47]{1,0:T(8,128)} async-done(((f32[2048,47]{1,0:T(8,128)}), f32[64,47]{1,0:T(8,128)}) %reduce-scatter.7.cloned.1.call-update) | async-done | bytes 12048
  360.3 131.6 %reduce-scatter.5.cloned.1.call-done = f32[100,64]{0,1:T(8,128)} async-done(((f32[100,2048]{0,1:T(8,128)}), f32[100,64]{0,1:T(8,128)}) %reduce-scatter.5.cloned.1.call-update) | async-done | bytes 25616 | tf_op jit(solution)/shard_map/reduce_scatter | solution.py:155
  491.9 1.4 multiply_reduce_fusion
  495.2 36.9 %all-reduce.2 = (f32[]{:T(128)}, f32[]{:T(128)}, f32[47]{0:T(128)S(1)}) all-reduce(f32[]{:T(128)S(6)} %add.163, f32[]{:T(128)S(6)} %add.168, f32[47]{0:T(128)S(1)} %add.169), channel_id=1, replica_groups=mesh['dp'=16,'shard'=2] {'dp','shard'}, use_global_device_ids=true, to_apply=%region_10.0 | all-reduce | flops 49 | bytes 392 | tf_op jit(solution)/shard_map/psum | solution.py:164
  534.9 43.0 %all_gather.23 = f32[100,2048]{0,1:T(8,128)S(1)} all-gather(f32[100,64]{0,1:T(8,128)S(1)} %broadcast_multiply_fusion), channel_id=1, replica_groups=mesh['dp'=16,'shard'=2] {'dp','shard'}, dimensions={1}, use_global_device_ids=true | all-gather | bytes 844800 | tf_op jit(solution)/shard_map/all_gather | solution.py:173
  577.8 38.8 %all-gather.1 = f32[32,64,47]{1,2,0:T(8,128)S(1)} all-gather(f32[1,64,47]{1,2,0:T(8,128)S(1)} %fusion.94), channel_id=1, replica_groups=mesh['dp'=16,'shard'=2] {'dp','shard'}, dimensions={0}, use_global_device_ids=true | all-gather | bytes 397056 | tf_op jit(solution)/shard_map/all_gather | solution.py:174
  617.1 2.0 fusion.50
  619.2 3.3 fusion.24
  622.5 3.1 fusion.21
  627.3 1.6 fusion.25
  629.7 1.5 fusion.20
  (129 shorter events, 21.4 us)
Async XLA Ops:
  7.2 620.1 %copy-start = (f32[2048,64]{0,1:T(8,128)S(1)}, f32[2048,64]{0,1:T(8,128)}, u32[]{:S(2)}) copy-start(f32[2048,64]{0,1:T(8,128)} %param.34) | copy-start | bytes 1572868
  7.2 60.2 %copy-start.11 = (f32[100,64]{0,1:T(8,128)S(1)}, f32[100,64]{0,1:T(8,128)}, u32[]{:S(2)}) copy-start(f32[100,64]{0,1:T(8,128)} %param.25) | copy-start | bytes 76804
  7.2 102.1 %copy-start.34 = (f32[64]{0:T(128)S(1)}, f32[64]{0:T(128)}, u32[]{:S(2)}) copy-start(f32[64]{0:T(128)} %param.27) | copy-start | bytes 772
  7.2 139.9 %copy-start.13 = (f32[64,47]{0,1:T(8,128)S(1)}, f32[64,47]{0,1:T(8,128)}, u32[]{:S(2)}) copy-start(f32[64,47]{0,1:T(8,128)} %param.26) | copy-start | bytes 36100
  7.2 351.6 %reduce-scatter.7.cloned.1.call-start = ((), (), s32[]{:S(2)}) async-start(), calls=%async_computation.3 | async-start | bytes 1081344
  67.4 126.3 %copy-start.5 = (bf16[1024,1024]{1,0:T(8,128)(2,1)}, bf16[1024,1024]{1,0:T(8,128)(2,1)S(1)}, u32[]{:S(2)}) copy-start(bf16[1024,1024]{1,0:T(8,128)(2,1)S(1)} %add_convert_fusion) | copy-start | bytes 6291460
  193.7 7.2 %copy-start.25 = (f32[47]{0:T(128)S(1)}, f32[47]{0:T(128)}, u32[]{:S(2)}) copy-start(f32[47]{0:T(128)} %param.28) | copy-start | bytes 568
  202.4 12.3 %copy-start.40 = (bf16[2048,100]{0,1:T(8,128)(2,1)S(1)}, bf16[2048,100]{0,1:T(8,128)(2,1)}, u32[]{:S(2)}) copy-start(bf16[2048,100]{0,1:T(8,128)(2,1)} %param.21) | copy-start | bytes 1228804
  214.7 7.3 %copy-start.7 = (bf16[1024,1024]{1,0:T(8,128)(2,1)}, bf16[1024,1024]{1,0:T(8,128)(2,1)S(1)}, u32[]{:S(2)}) copy-start(bf16[1024,1024]{1,0:T(8,128)(2,1)S(1)} %add_convert_fusion.1) | copy-start | bytes 6291460
  227.6 17.3 %copy-start.6 = (bf16[1024,1024]{1,0:T(8,128)(2,1)S(1)}, bf16[1024,1024]{1,0:T(8,128)(2,1)}, u32[]{:S(2)}) copy-start(bf16[1024,1024]{1,0:T(8,128)(2,1)} %copy-done.5) | copy-start | bytes 6291460
  227.6 264.3 %reduce-scatter.5.cloned.1.call-start = ((), (), s32[]{:S(2)}) async-start(), calls=%async_computation.2 | async-start | bytes 1081344 | tf_op jit(solution)/shard_map/reduce_scatter | solution.py:155
  260.9 9.1 %copy-start.16 = (s32[2048]{0:T(1024)S(1)}, s32[2048]{0:T(1024)}, u32[]{:S(2)}) copy-start(s32[2048]{0:T(1024)} %param.23) | copy-start | bytes 24580
  260.9 9.2 %copy-start.19 = (f32[1024]{0:T(1024)S(1)}, f32[1024]{0:T(1024)}, u32[]{:S(2)}) copy-start(f32[1024]{0:T(1024)} %get-tuple-element.33) | copy-start | bytes 12292
  260.9 9.2 %copy-start.20 = (f32[1024]{0:T(1024)S(1)}, f32[1024]{0:T(1024)}, u32[]{:S(2)}) copy-start(f32[1024]{0:T(1024)} %get-tuple-element.49) | copy-start | bytes 12292
  261.0 11.1 %copy-start.28 = (f32[2048]{0:T(1024)S(1)}, f32[2048]{0:T(1024)}, u32[]{:S(2)}) copy-start(f32[2048]{0:T(1024)} %get-tuple-element.45) | copy-start | bytes 24580
  261.0 11.1 %copy-start.29 = (f32[2048]{0:T(1024)S(1)}, f32[2048]{0:T(1024)}, u32[]{:S(2)}) copy-start(f32[2048]{0:T(1024)} %get-tuple-element.47) | copy-start | bytes 24580
  261.0 11.1 %copy-start.32 = (f32[47]{0:T(128)S(1)}, f32[47]{0:T(128)}, u32[]{:S(2)}) copy-start(f32[47]{0:T(128)} %get-tuple-element.29) | copy-start | bytes 568
  261.0 11.1 %copy-start.33 = (f32[47]{0:T(128)S(1)}, f32[47]{0:T(128)}, u32[]{:S(2)}) copy-start(f32[47]{0:T(128)} %get-tuple-element.50) | copy-start | bytes 568
  265.0 360.6 %copy-start.8 = (f32[64,2048]{1,0:T(8,128)S(1)}, f32[64,2048]{1,0:T(8,128)}, u32[]{:S(2)}) copy-start(f32[64,2048]{1,0:T(8,128)} %param.35) | copy-start | bytes 1572868
  270.0 356.2 %copy-start.17 = (f32[47,47]{1,0:T(8,128)S(1)}, f32[47,47]{1,0:T(8,128)}, u32[]{:S(2)}) copy-start(f32[47,47]{1,0:T(8,128)} %param.32) | copy-start | bytes 26512
  270.0 357.3 %copy-start.12 = (f32[100,64]{0,1:T(8,128)S(1)}, f32[100,64]{0,1:T(8,128)}, u32[]{:S(2)}) copy-start(f32[100,64]{0,1:T(8,128)} %param.25) | copy-start | bytes 76804
  270.0 358.9 %copy-start.14 = (f32[64,47]{0,1:T(8,128)S(1)}, f32[64,47]{0,1:T(8,128)}, u32[]{:S(2)}) copy-start(f32[64,47]{0,1:T(8,128)} %param.26) | copy-start | bytes 36100
  270.0 358.9 %copy-start.18 = (f32[47,47]{1,0:T(8,128)S(1)}, f32[47,47]{1,0:T(8,128)}, u32[]{:S(2)}) copy-start(f32[47,47]{1,0:T(8,128)} %param.36) | copy-start | bytes 26512
  270.0 361.2 %copy-start.35 = (f32[64]{0:T(128)S(1)}, f32[64]{0:T(128)}, u32[]{:S(2)}) copy-start(f32[64]{0:T(128)} %param.27) | copy-start | bytes 772
  270.0 361.2 %copy-start.36 = (f32[64]{0:T(128)S(1)}, f32[64]{0:T(128)}, u32[]{:S(2)}) copy-start(f32[64]{0:T(128)} %param.38) | copy-start | bytes 772
  270.0 361.2 %copy-start.37 = (f32[64]{0:T(128)S(1)}, f32[64]{0:T(128)}, u32[]{:S(2)}) copy-start(f32[64]{0:T(128)} %param.37) | copy-start | bytes 772
  270.0 361.8 %copy-start.27 = (f32[47]{0:T(128)S(1)}, f32[47]{0:T(128)}, u32[]{:S(2)}) copy-start(f32[47]{0:T(128)} %param.28) | copy-start | bytes 568
  270.0 361.8 %copy-start.38 = (f32[47]{0:T(128)S(1)}, f32[47]{0:T(128)}, u32[]{:S(2)}) copy-start(f32[47]{0:T(128)} %param.40) | copy-start | bytes 568
  270.0 361.8 %copy-start.39 = (f32[47]{0:T(128)S(1)}, f32[47]{0:T(128)}, u32[]{:S(2)}) copy-start(f32[47]{0:T(128)} %param.39) | copy-start | bytes 568
  534.1 98.3 %copy-start.15 = (f32[64,47]{0,1:T(8,128)}, f32[64,47]{0,1:T(8,128)S(1)}, u32[]{:S(2)}) copy-start(f32[64,47]{0,1:T(8,128)S(1)} %broadcast_multiply_fusion.1) | copy-start | bytes 36100
  534.9 97.5 %copy-start.10 = (f32[100,64]{0,1:T(8,128)}, f32[100,64]{0,1:T(8,128)S(1)}, u32[]{:S(2)}) copy-start(f32[100,64]{0,1:T(8,128)S(1)} %broadcast_multiply_fusion) | copy-start | bytes 76804
  617.1 12.6 %copy-start.9 = (f32[64,2048]{1,0:T(8,128)S(1)}, f32[64,2048]{1,0:T(8,128)}, u32[]{:S(2)}) copy-start(f32[64,2048]{1,0:T(8,128)} %param.31) | copy-start | bytes 1572868
  (11 other events, 52.6 us)
Sparse Core Ops, SparseCore 0:
  227.7 131.0 reduce-scatter.6
  361.1 130.6 reduce-scatter.4
where the time goes:
time: 647 us; the launch traced here: 641 us
  blocking collectives  318 us (49%)
  waiting for transfers between devices  180 us (28%)
  matrix products  76.2 us (12%)
  other arithmetic  32.5 us (5%)
  between operations  22 us (3%)
  local copies, waits for them, and re-layouts  11.3 us (2%)
    reduce_scatter x1, waiting for transfers between devices, per_device(): lax.psum_scatter(acc_first, ('dp', 'shard'), scatter_dimension=1, tiled=T...  132 us
    unnamed x2, blocking collectives  74.1 us
    unnamed x3, waiting for transfers between devices  48.9 us
    all_gather x1, blocking collectives, per_device(): lax.all_gather(own_one, ('dp', 'shard'), axis=1, tiled=True)  43 us
    psum x1, blocking collectives, per_device(): lax.psum(jnp.sum(label_mask).astype(jnp.float32), ('dp', 'shard'))  42 us
    all_gather x1, blocking collectives, fetch_weights(): lax.all_gather(w_first.astype(jnp.bfloat16), ('dp', 'shard'), axis=1, til...  41.9 us
    all_gather x1, blocking collectives, fetch_weights(): lax.all_gather(w_second.astype(jnp.bfloat16), ('dp', 'shard'), axis=0, ti...  41.3 us
    all_gather x1, blocking collectives, per_device(): lax.all_gather(own_two, ('dp', 'shard'), axis=0, tiled=True)  38.8 us
  transfers between devices with their start and end apart: 2, of which 2 were waited for; matrix products, arithmetic and copies ran while one was open for 7% of the time, Pallas kernels for 0%

commit v1 on v0

v1 whole, which is shorter than its diff:
```python
import functools

import jax
import jax.numpy as jnp
from jax import lax
from jax.experimental import pallas as pl
from jax.experimental.pallas import tpu as pltpu
from jax.sharding import PartitionSpec as P

STEP = 10
BLOCK = 1024
AXES = ("dp", "shard")

clip_limit = 0.05
beta_stat = 0.95
beta_one = 0.9
beta_two = 0.999
adam_eps = 1e-08
decay_rate = 0.01
rate_bias = 0.2
rate_first = 1000.0
rate_second = 300.0
highest = lax.Precision.HIGHEST

f32 = jnp.float32
bf16 = jnp.bfloat16
NN = (((1,), (0,)), ((), ()))
NT = (((1,), (1,)), ((), ()))
TN = (((0,), (0,)), ((), ()))

ROWS = 160
HALF = 80
TOP = 112
LANES = 128


def mm(a, b, dims=NN):
    return lax.dot_general(a, b, dims, preferred_element_type=f32)


def params(limit=56):
    return pltpu.CompilerParams(vmem_limit_bytes=limit * 2**20)


def cost(us):
    return pl.CostEstimate(flops=int(us * 1e9), bytes_accessed=int(us * 2e6), transcendentals=0)


def adam_step(param, grad, first, second):
    first_new = beta_one * first + (1.0 - beta_one) * grad
    second_new = beta_two * second + (1.0 - beta_two) * grad * grad
    corr_one = 1.0 - beta_one**STEP
    corr_two = 1.0 - beta_two**STEP
    update = (
        first_new / corr_one / (jnp.sqrt(second_new / corr_two) + adam_eps) + decay_rate * param
    )
    return (first_new, second_new, param - rate_bias * update)


def pack_kernel(w1t_ref, w2t_ref, b_ref, out_ref, bottom):
    fan_in = w1t_ref.shape[1]
    width = w1t_ref.shape[0]
    classes = w2t_ref.shape[0]
    rows = lax.broadcasted_iota(jnp.int32, (TOP, fan_in), 0)
    cols = lax.broadcasted_iota(jnp.int32, (TOP, fan_in), 1)
    eye = (rows == cols).astype(bf16)
    w1 = mm(eye, w1t_ref[...].astype(bf16), NT)
    rows = lax.broadcasted_iota(jnp.int32, (TOP, width), 0)
    w1 = jnp.where(rows == fan_in, b_ref[...], w1)
    out_ref[:, 0:width] = w1[0:HALF].astype(bf16)
    bottom[...] = jnp.zeros_like(bottom)
    bottom[0 : TOP - HALF, :] = w1[HALF:TOP]
    bottom[TOP - HALF : TOP - HALF + classes, :] = w2t_ref[...]
    out_ref[:, width : 2 * width] = bottom[...].astype(bf16)


def graph_kernel(fan_in, nbr_ref, feat_ref, m_ref, p_ref, pt_ref):
    classes = nbr_ref.shape[0]
    scale_in = 1.0 / (classes + 1)
    base = lax.broadcasted_iota(jnp.int32, (16, LANES), 0).astype(jnp.int16)
    one = jnp.ones((16, LANES), bf16)
    zero = jnp.zeros((16, LANES), bf16)
    row = lax.broadcasted_iota(jnp.int32, (LANES, LANES), 0)
    col = lax.broadcasted_iota(jnp.int32, (LANES, LANES), 1)
    for t in range(BLOCK // LANES):
        at = slice(t * LANES, (t + 1) * LANES)
        slots = [
            jnp.broadcast_to(nbr_ref[k : k + 1, at], (16, LANES)).astype(jnp.int16)
            for k in range(classes)
        ]
        for u in range(BLOCK // 16):
            here = base + jnp.int16(u * 16)
            terms = [jnp.where(s == here, one, zero) for s in slots]
            while len(terms) > 1:
                terms = [sum(terms[a : a + 2][1:], terms[a]) for a in range(0, len(terms), 2)]
            m_ref[u * 16 : (u + 1) * 16, at] = terms[0]
        square = m_ref[at, at].astype(f32)
        m_ref[at, at] = jnp.where(row == col, 2.0 * square + 2.0, square).astype(bf16)
    pooled = mm(feat_ref[...], m_ref[...]) * scale_in
    rest = LANES - fan_in - 1
    pooled = jnp.concatenate(
        [pooled, jnp.ones((1, BLOCK), f32), jnp.zeros((rest, BLOCK), f32)], axis=0
    )
    pt_ref[...] = pooled[0:TOP].astype(bf16)
    p_ref[...] = pooled.T.astype(bf16)


def main_kernel(nblk, classes, degree, *refs):
    own = refs[0:4]
    other = refs[4:8]
    m_hbm = refs[8 : 8 + nblk]
    p_refs = refs[8 + nblk : 8 + 2 * nblk]
    pt_refs = refs[8 + 2 * nblk : 8 + 3 * nblk]
    mask_ref, label_ref, b2_ref = refs[8 + 3 * nblk : 11 + 3 * nblk]
    keep_ref, send_ref = refs[11 + 3 * nblk : 13 + 3 * nblk]
    w, ww, hid, der, m, z, qq, qqt, row_scr, sem = refs[13 + 3 * nblk :]
    hidden = w.shape[1]
    core = lax.axis_index("shard")
    first = core == 0
    scale_in = 1.0 / (degree + 1)
    copies = [
        pltpu.make_async_copy(m_hbm[b], m.at[b], sem.at[b]) for b in range(nblk)
    ]
    for c in copies:
        c.start()

    lane = lax.broadcasted_iota(jnp.int32, (HALF, LANES), 1)
    left = lane < LANES // 2
    for g in range(4):
        for s in range(4):
            at = slice(s * LANES, (s + 1) * LANES)
            to = slice((g * 4 + s) * LANES, (g * 4 + s + 1) * LANES)
            mine = own[g][:, at].astype(f32)
            theirs = other[g][:, at].astype(f32)
            lo = jnp.where(first, mine, theirs)
            hi = jnp.where(first, theirs, mine)
            w[0:HALF, to] = jnp.where(left, lo, pltpu.roll(hi, LANES // 2, 1)).astype(bf16)
            w[HALF:ROWS, to] = jnp.where(left, pltpu.roll(lo, LANES // 2, 1), hi).astype(bf16)
    ww[0:48, :] = w[TOP:ROWS, :]
    ww[48:96, :] = w[TOP:ROWS, :]
    ww[96:128, :] = jnp.zeros((32, hidden), bf16)

    c0 = 0.7978845608028654
    c1 = c0 * 0.044715
    chunk = 512
    sub = 256
    rows = 256

    def forward(n, _):
        n0 = pl.multiple_of(n * chunk, chunk)
        for b in range(nblk):
            for r in range(BLOCK // rows):
                total = None
                for k in range(chunk // sub):
                    at = pl.ds(n0 + k * sub, sub)
                    to = slice(b * BLOCK + r * rows, b * BLOCK + (r + 1) * rows)
                    x = mm(p_refs[b][r * rows : (r + 1) * rows, :], w[0:LANES, at])
                    x2 = x * x
                    t = jnp.tanh(x * (c0 + c1 * x2))
                    p = 0.5 * t + 0.5
                    h = x * p
                    d = p + h * (1.0 - p) * (2.0 * c0 + 6.0 * c1 * x2)
                    hb = h.astype(bf16)
                    hid[to, at] = hb
                    der[to, at] = d.astype(bf16)
                    part = mm(hb, w[TOP:ROWS, at], NT)
                    total = part if total is None else total + part
                z[to, 0:48] += total
        return 0

    z[...] = jnp.zeros_like(z)
    lax.fori_loop(0, hidden // chunk, forward, 0)

    row_scr[...] = jnp.zeros_like(row_scr)
    loss = jnp.zeros((1, 1), f32)
    count = jnp.zeros((1, 1), f32)
    for b in range(nblk):
        copies[b].wait()
        zb = z[b * BLOCK : (b + 1) * BLOCK, :].T
        zb = zb[0:48]
        z_hi = zb.astype(bf16)
        z_lo = (zb - z_hi.astype(f32)).astype(bf16)
        both = mm(jnp.concatenate([z_hi, z_lo], axis=0), m[b])
        logits = (both[0:48] + both[48:96]) * scale_in + b2_ref[...]
        cls = lax.broadcasted_iota(jnp.int32, (48, BLOCK), 0)
        logits = jnp.where(cls < classes, logits, -1e30)
        top = jnp.max(logits, axis=0, keepdims=True)
        e = jnp.exp(logits - top)
        total = jnp.sum(e, axis=0, keepdims=True)
        hit = cls == label_ref[b : b + 1, :]
        weight = mask_ref[b : b + 1, :].astype(f32)
        picked = jnp.sum(jnp.where(hit, logits, 0.0), axis=0, keepdims=True)
        loss += jnp.sum((jnp.log(total) + top - picked) * weight, axis=1, keepdims=True)
        count += jnp.sum(weight, axis=1, keepdims=True)
        grad = ((e / total - hit.astype(f32)) * weight).astype(bf16)
        row_scr[:, 0:48] += mm(jnp.ones((8, BLOCK), bf16), grad, NT)
        q = mm(grad, m[b], NT) * scale_in
        q_hi = q.astype(bf16)
        q_lo = q - q_hi.astype(f32)
        q2 = jnp.concatenate([q_hi.astype(f32), q_lo, jnp.zeros((32, BLOCK), f32)], axis=0)
        qqt[b] = q2[0:96].astype(bf16)
        qq[b * BLOCK : (b + 1) * BLOCK, :] = q2.T.astype(bf16)

    vec = row_scr[0:1, :]
    pos = lax.broadcasted_iota(jnp.int32, vec.shape, 1)
    vec = jnp.where(pos == 48, loss, jnp.where(pos == 49, count, vec))
    part_a = vec.astype(bf16).astype(f32)
    part_b = (vec - part_a).astype(bf16).astype(f32)
    part_c = (vec - part_a - part_b).astype(bf16).astype(f32)
    r16 = lax.broadcasted_iota(jnp.int32, (16, vec.shape[1]), 0) - jnp.where(first, 5, 8)
    scal = (
        jnp.where(r16 == 0, part_a, 0.0)
        + jnp.where(r16 == 1, part_b, 0.0)
        + jnp.where(r16 == 2, part_c, 0.0)
    )

    def backward(n, _):
        at = pl.ds(pl.multiple_of(n * sub, sub), sub)
        d1 = jnp.zeros((TOP, sub), f32)
        d2 = jnp.zeros((96, sub), f32)
        for b in range(nblk):
            to = slice(b * BLOCK, (b + 1) * BLOCK)
            gp = (mm(qq[to, :], ww[:, at]) * der[to, at].astype(f32)).astype(bf16)
            d1 = d1 + mm(pt_refs[b][...], gp)
            d2 = d2 + mm(qqt[b], hid[to, at])
        d2 = d2[0:48] + d2[48:96]
        extra = jnp.where(n == 0, scal, 0.0)
        upper = d1[0:HALF]
        lower = jnp.concatenate([d1[HALF:96], d1[96:TOP] + extra, d2], axis=0)
        keep_ref[:, at] = jnp.where(first, upper, lower)
        send_ref[:, at] = jnp.where(first, lower, upper)
        return 0

    lax.fori_loop(0, hidden // sub, backward, 0)


def add_core_kernel(keep_ref, got_ref, g0_ref, s1_ref, s2_ref, s3_ref):
    n = g0_ref.shape[1]
    g0_ref[...] = keep_ref[:, 0:n] + got_ref[:, 0:n]
    for k, out in enumerate((s1_ref, s2_ref, s3_ref)):
        at = slice((k + 1) * n, (k + 2) * n)
        out[...] = (keep_ref[:, at] + got_ref[:, at]).astype(bf16)


def add_plane_kernel(g0_ref, r1_ref, r2_ref, r3_ref, out_ref):
    out_ref[...] = (
        g0_ref[...] + r1_ref[...].astype(f32) + r2_ref[...].astype(f32) + r3_ref[...].astype(f32)
    ).astype(bf16)


def add_line_kernel(h_ref, z1_ref, z2_ref, z3_ref, out_ref):
    for s in range(4):
        here, one, two, three = (
            ref[:, (s ^ k) * LANES : ((s ^ k) + 1) * LANES].astype(f32)
            for k, ref in enumerate((h_ref, z1_ref, z2_ref, z3_ref))
        )
        out_ref[:, s * LANES : (s + 1) * LANES] = ((here + one) + (two + three)).astype(bf16)


def step_kernel(fan_in, classes, *refs):
    own = refs[0:4]
    other = refs[4:8]
    (
        w1t, w2t, b1, b2, l1, r1t, l2, r2, l1_root, r1t_root, l2_root, r2_root, m1, v1, m2, v2,
    ) = refs[8:24]
    (
        loss_o, count_o, norm_o, grad1_o, grad2_o, w1_o, w2_o, l1_o, r1_o, l2_o, r2_o,
        m1_o, v1_o, b1_o, m2_o, v2_o, b2_o,
    ) = refs[24:41]
    g = refs[41]
    chip = lax.axis_index("dp")
    core = lax.axis_index("shard")
    first = core == 0
    half = LANES // 2
    scal = jnp.zeros((16, LANES), f32)
    for k in range(4):
        for s in range(4):
            at = slice(s * LANES, (s + 1) * LANES)
            mine = own[k][:, at].astype(f32)
            theirs = other[k][:, at].astype(f32)
            upper = jnp.where(first, mine, theirs)
            lower = jnp.where(first, theirs, mine)
            scal += lower[16:32]
            to = pl.ds(pl.multiple_of((chip ^ (s * 4 + k)) * LANES, LANES), LANES)
            g[0:HALF, to] = upper.astype(bf16)
            g[HALF:96, to] = lower[0:16].astype(bf16)
            keep = lax.broadcasted_iota(jnp.int32, (16, LANES), 0) <= fan_in - 96
            g[96:TOP, to] = jnp.where(keep, lower[16:32], 0.0).astype(bf16)
            g[TOP:ROWS, to] = lower[32:80].astype(bf16)
    row16 = lax.broadcasted_iota(jnp.int32, (16, LANES), 0)
    scal = jnp.where((row16 >= 5) & (row16 <= 10), scal, 0.0)
    vec = jnp.sum(scal, axis=0, keepdims=True)
    pos = lax.broadcasted_iota(jnp.int32, (1, LANES), 1)
    loss = jnp.sum(jnp.where(pos == 48, vec, 0.0), axis=1, keepdims=True)
    count = jnp.sum(jnp.where(pos == 49, vec, 0.0), axis=1, keepdims=True)
    inv = 1.0 / jnp.maximum(count, 1.0)
    gb2 = jnp.where(pos < classes, vec, 0.0) * inv
    whole = g[...]
    gram = mm(whole, whole, NT)
    gi = lax.broadcasted_iota(jnp.int32, gram.shape, 0)
    gj = lax.broadcasted_iota(jnp.int32, gram.shape, 1)
    squares = jnp.sum(jnp.where(gi == gj, gram, 0.0), axis=0, keepdims=True)
    squares = jnp.sum(squares, axis=1, keepdims=True) * inv * inv
    squares = squares + jnp.sum(gb2 * gb2, axis=1, keepdims=True)
    norm = jnp.sqrt(squares)
    factor = jnp.minimum(1.0, clip_limit / (norm + 1e-06))
    s = factor * inv
    ss = (1.0 - beta_stat) * s * s
    loss_o[...] = loss
    count_o[...] = count
    norm_o[...] = norm
    l1_o[...] = beta_stat * l1[...] + ss * gram[0:fan_in, 0:fan_in]
    g2t = g[TOP:ROWS, :]
    r2_o[...] = beta_stat * r2[...] + ss * mm(g2t, g2t, NT)[0:classes, 0:classes]

    mine = g[:, pl.ds(pl.multiple_of(chip * LANES, LANES), LANES)].astype(f32)
    mine = jnp.where(first, mine, pltpu.roll(mine, half, 1))[:, 0:half]
    mine_b = mine.astype(bf16)
    eye = (
        lax.broadcasted_iota(jnp.int32, (half, half), 0)
        == lax.broadcasted_iota(jnp.int32, (half, half), 1)
    ).astype(bf16)
    mine_t = mm(eye, mine_b, NT)
    own1_t = mine_t[:, 0:TOP].astype(bf16)
    grad1_o[...] = s * mine_t[:, 0:fan_in]
    grad2_o[...] = s * mine[TOP : TOP + classes, :]
    own2 = mm(eye, mine_b[TOP:ROWS], NT).astype(bf16)
    g1 = g[0:TOP, :]
    zero_bias = lax.broadcasted_iota(jnp.int32, own1_t.shape, 1) < fan_in
    own1_t = jnp.where(zero_bias, own1_t.astype(f32), 0.0).astype(bf16)
    r1_o[...] = beta_stat * r1t[...] + ss * mm(own1_t, g1)
    l2_o[...] = beta_stat * l2[...] + ss * mm(own2, g2t)
    t1 = mm(r1t_root[...].astype(bf16), g1, NT)[:, 0:fan_in]
    t1 = lax.dot_general(t1, l1_root[...], NT, precision=highest, preferred_element_type=f32)
    w1_o[...] = w1t[...] - (rate_first * s) * t1
    t2 = mm(l2_root[...].astype(bf16), g2t, NT)[:, 0:classes]
    t2 = lax.dot_general(
        r2_root[...], t2, (((0,), (1,)), ((), ())), precision=highest, preferred_element_type=f32
    )
    w2_o[...] = w2t[...] - (rate_second * s) * t2
    m1_o[...], v1_o[...], b1_o[...] = adam_step(
        b1[...], s * mine[fan_in : fan_in + 1, :], m1[...], v1[...]
    )
    m2_o[...], v2_o[...], b2_o[...] = adam_step(
        b2[...], factor * gb2[:, 0:classes], m2[...], v2[...]
    )


def swap(array, bits):
    count = lax.axis_size(AXES)
    return lax.ppermute(array, AXES, [(i, i ^ bits) for i in range(count)])


def fast_device(
    features, neighbors, label_mask, labels, w_first, w_second, b_first, b_second, l_first, r_first,
    l_second, r_second, l_first_root, r_first_root, l_second_root, r_second_root, m_first, v_first,
    m_second, v_second,
):
    fan_in, width = w_first.shape
    classes = w_second.shape[1]
    degree = neighbors.shape[1]
    nblk = features.shape[0] // BLOCK
    hidden = width * lax.axis_size(AXES)
    group = hidden // 4
    shape = jax.ShapeDtypeStruct
    w1t, w2t, b1 = w_first.T, w_second.T, b_first.reshape(1, width)

    piece = pl.pallas_call(
        pack_kernel,
        out_shape=shape((HALF, LANES), bf16),
        scratch_shapes=[pltpu.VMEM((HALF, width), f32)],
        compiler_params=params(8),
        cost_estimate=cost(1),
        name="pack",
    )(w1t, w2t, b1)
    line = jnp.concatenate([piece] + [swap(piece, 8 * k) for k in (1, 2, 3)], axis=1)
    plane = [line] + [swap(line, 2 * k) for k in (1, 2, 3)]
    partner = [swap(part, 1) for part in plane]

    graphs = []
    nbr_t, feat_t = neighbors.T, features.T
    for b in range(nblk):
        graphs.append(
            pl.pallas_call(
                functools.partial(graph_kernel, fan_in),
                grid=(1,),
                in_specs=[
                    pl.BlockSpec((degree, BLOCK), lambda i, b=b: (0, b)),
                    pl.BlockSpec((fan_in, BLOCK), lambda i, b=b: (0, b)),
                ],
                out_specs=[
                    pl.BlockSpec((BLOCK, BLOCK), lambda i: (0, 0)),
                    pl.BlockSpec((BLOCK, LANES), lambda i: (0, 0)),
                    pl.BlockSpec((TOP, BLOCK), lambda i: (0, 0)),
                ],
                out_shape=[
                    shape((BLOCK, BLOCK), bf16),
                    shape((BLOCK, LANES), bf16),
                    shape((TOP, BLOCK), bf16),
                ],
                compiler_params=params(24),
                cost_estimate=cost(3),
                name="graph",
            )(nbr_t, feat_t)
        )
    ms = [graph[0] for graph in graphs]
    ps = [graph[1] for graph in graphs]
    pts = [graph[2] for graph in graphs]

    vmem = pl.BlockSpec(memory_space=pltpu.VMEM)
    keep, send = pl.pallas_call(
        functools.partial(main_kernel, nblk, classes, degree),
        in_specs=[vmem] * 8 + [pl.BlockSpec(memory_space=pl.ANY)] * nblk + [vmem] * (2 * nblk + 3),
        out_specs=[vmem, vmem],
        out_shape=[shape((HALF, hidden), f32)] * 2,
        scratch_shapes=[
            pltpu.VMEM((ROWS, hidden), bf16),
            pltpu.VMEM((LANES, hidden), bf16),
            pltpu.VMEM((nblk * BLOCK, hidden), bf16),
            pltpu.VMEM((nblk * BLOCK, hidden), bf16),
            pltpu.VMEM((nblk, BLOCK, BLOCK), bf16),
            pltpu.VMEM((nblk * BLOCK, LANES), f32),
            pltpu.VMEM((nblk * BLOCK, LANES), bf16),
            pltpu.VMEM((nblk, 96, BLOCK), bf16),
            pltpu.VMEM((8, 256), f32),
            pltpu.SemaphoreType.DMA((nblk,)),
        ],
        compiler_params=params(),
        cost_estimate=cost(15),
        name="main",
    )(
        *plane,
        *partner,
        *ms,
        *ps,
        *pts,
        label_mask.reshape(nblk, BLOCK),
        labels.reshape(nblk, BLOCK),
        jnp.pad(b_second, (0, 48 - classes)).reshape(48, 1),
    )

    got = swap(send, 1)
    g0, s1, s2, s3 = pl.pallas_call(
        add_core_kernel,
        out_shape=[shape((HALF, group), f32)] + [shape((HALF, group), bf16)] * 3,
        compiler_params=params(16),
        cost_estimate=cost(1),
        name="add_core",
    )(keep, got)
    mine = pl.pallas_call(
        add_plane_kernel,
        out_shape=shape((HALF, group), bf16),
        compiler_params=params(8),
        cost_estimate=cost(1),
        name="add_plane",
    )(g0, swap(s1, 2), swap(s2, 4), swap(s3, 6))
    mine = pl.pallas_call(
        add_line_kernel,
        out_shape=shape((HALF, group), bf16),
        compiler_params=params(8),
        cost_estimate=cost(1),
        name="add_line",
    )(mine, swap(mine, 8), swap(mine, 16), swap(mine, 24))
    plane = [mine] + [swap(mine, 2 * k) for k in (1, 2, 3)]
    partner = [swap(part, 1) for part in plane]

    one = shape((1, 1), f32)
    row1, row2 = shape((1, width), f32), shape((1, classes), f32)
    outs = pl.pallas_call(
        functools.partial(step_kernel, fan_in, classes),
        out_shape=[
            one, one, one, shape(w1t.shape, f32), shape(w2t.shape, f32), shape(w1t.shape, f32),
            shape(w2t.shape, f32), shape(l_first.shape, f32), shape((width, hidden), f32),
            shape((width, hidden), f32), shape(r_second.shape, f32),
            row1, row1, row1, row2, row2, row2,
        ],
        scratch_shapes=[pltpu.VMEM((ROWS, hidden), bf16)],
        compiler_params=params(32),
        cost_estimate=cost(5),
        name="update",
    )(
        *plane,
        *partner,
        w1t, w2t, b1, b_second.reshape(1, classes), l_first, r_first.T, l_second, r_second,
        l_first_root, r_first_root.T, l_second_root, r_second_root,
        m_first.reshape(1, width), v_first.reshape(1, width),
        m_second.reshape(1, classes), v_second.reshape(1, classes),
    )
    loss, count, norm, grad1, grad2, w1, w2, l1, r1, l2, r2, m1, v1, nb1, m2, v2, nb2 = outs
    return (
        loss.reshape(()), count.reshape(()), norm.reshape(()), grad1.T, grad2.T, w1.T, w2.T,
        l1, r1.T, l2, r2, m1.reshape(width), v1.reshape(width), nb1.reshape(width),
        m2.reshape(classes), v2.reshape(classes), nb2.reshape(classes),
    )


def general_device(
    features, neighbors, label_mask, labels, w_first, w_second, b_first, b_second, l_first, r_first,
    l_second, r_second, l_first_root, r_first_root, l_second_root, r_second_root, m_first, v_first,
    m_second, v_second,
):
    fan_in, width = w_first.shape
    classes = w_second.shape[1]
    scale_in = 1.0 / (neighbors.shape[1] + 1)
    packed = jnp.concatenate([w_first, b_first[None, :], w_second.T], axis=0).astype(bf16)
    packed = lax.all_gather(packed, AXES, axis=1, tiled=True)
    first_full, bias_full, second_full = packed[:fan_in], packed[fan_in], packed[fan_in + 1 :]
    loss = jnp.zeros((), f32)
    grads = jnp.zeros(packed.shape, f32)
    gb2 = jnp.zeros_like(b_second)
    for b in range(features.shape[0] // BLOCK):
        at = slice(b * BLOCK, (b + 1) * BLOCK)
        columns = jnp.arange(BLOCK, dtype=jnp.int32)
        counts = jnp.sum(
            (neighbors[at][:, :, None] == columns[None, None, :]).astype(f32), axis=1
        )
        eye = jnp.eye(BLOCK, dtype=f32)
        matrix = (counts + eye * (2.0 + jnp.sum(counts * eye, axis=1))[:, None]).astype(bf16)
        pooled = (mm(matrix, features[at]) * scale_in).astype(bf16)
        pre = mm(pooled, first_full) + bias_full.astype(f32)
        hidden = jax.nn.gelu(pre).astype(bf16)
        logits = (
            jnp.dot(matrix.astype(f32), mm(hidden, second_full, NT), precision=highest) * scale_in
            + b_second
        )
        log_prob = jax.nn.log_softmax(logits, axis=-1)
        onehot = (labels[at][:, None] == jnp.arange(classes, dtype=jnp.int32)[None, :]).astype(f32)
        weight = label_mask[at].astype(f32)
        loss = loss - jnp.sum(jnp.sum(log_prob * onehot, axis=-1) * weight)
        grad = ((jnp.exp(log_prob) - onehot) * weight[:, None]).astype(bf16)
        gb2 = gb2 + jnp.sum(grad.astype(f32), axis=0)
        back = (mm(matrix, grad, TN) * scale_in).astype(bf16)
        grad_pre = jax.vjp(jax.nn.gelu, pre)[1](mm(back, second_full))[0].astype(bf16)
        grads = grads + jnp.concatenate(
            [
                mm(pooled, grad_pre, TN),
                jnp.sum(grad_pre.astype(f32), axis=0, keepdims=True),
                mm(back, hidden, TN),
            ],
            axis=0,
        )
    count = jnp.sum(label_mask).astype(f32)
    grads, gb2, loss, count = lax.psum((grads, gb2, loss, count), AXES)
    inv = 1.0 / jnp.maximum(count, 1.0)
    grads, gb2 = grads * inv, gb2 * inv
    norm = jnp.sqrt(jnp.sum(grads * grads) + jnp.sum(gb2 * gb2))
    factor = jnp.minimum(1.0, clip_limit / (norm + 1e-06))
    grads, gb2 = grads * factor, gb2 * factor
    at = lax.axis_index(AXES) * width
    own = lax.dynamic_slice_in_dim(grads, at, width, axis=1)
    full_one, full_two = grads[:fan_in], grads[fan_in + 1 :].T
    own_one, own_bias, own_two = own[:fan_in], own[fan_in], own[fan_in + 1 :].T
    dot = functools.partial(jnp.dot, precision=highest)
    keep, add = beta_stat, 1.0 - beta_stat
    m1, v1, b1 = adam_step(b_first, own_bias, m_first, v_first)
    m2, v2, b2 = adam_step(b_second, gb2, m_second, v_second)
    return (
        loss, count, norm, own_one, own_two,
        w_first - rate_first * dot(l_first_root, dot(full_one, r_first_root)),
        w_second - rate_second * dot(dot(l_second_root, full_two), r_second_root),
        keep * l_first + add * dot(full_one, full_one.T),
        keep * r_first + add * dot(full_one.T, own_one),
        keep * l_second + add * dot(own_two, full_two.T),
        keep * r_second + add * dot(full_two.T, full_two),
        m1, v1, b1, m2, v2, b2,
    )


def solution(mesh):
    split0 = P(AXES)
    rows = P(AXES, None)
    columns = P(None, AXES)
    whole = P()
    fast = mesh.shape["dp"] == 16 and mesh.shape["shard"] == 2

    def per_device(*args):
        width = args[4].shape[1]
        return (fast_device if fast and 2 * width == LANES else general_device)(*args)

    return jax.shard_map(
        per_device,
        mesh=mesh,
        in_specs=(
            rows, rows, split0, split0, columns, rows, split0, whole, whole, columns, rows, whole,
            whole, columns, rows, whole, split0, split0, whole, whole,
        ),
        out_specs=(
            whole, whole, whole, columns, rows, columns, rows, whole, columns, rows, whole,
            split0, split0, split0, whole, whole, whole,
        ),
        check_vma=False,
    )
```

time: 647 us -> 86.3 us (0.13)
  blocking collectives: 318 us -> 0 us
  waiting for transfers between devices: 180 us -> 16.4 us
  matrix products: 76.2 us -> 0 us
  Pallas kernels: 0 us -> 34.6 us
  other arithmetic: 32.5 us -> 0.01 us
  starting transfers between devices: 0.08 us -> 22.5 us
  between operations: 22 us -> 1.2 us
    all_gather x4 -> x0, blocking collectives: 165 us -> none  [the longest x1 43 us: per_device(): lax.all_gather(own_one, ('dp', 'shard'), axis=1, tiled=True)]
    reduce_scatter x1 -> x0, waiting for transfers between devices: 132 us -> none  [per_device(): lax.psum_scatter(acc_first, ('dp', 'shard'), scatter_dimension=1, tiled=T...]
    psum x2 -> x0, blocking collectives: 78.9 us -> none  [the longest x1 42 us: per_device(): lax.psum(jnp.sum(label_mask).astype(jnp.float32), ('dp', 'shard'))]
    dot_general x22 -> x0, matrix products: 76.2 us -> none  [the longest x2 33.3 us: backward(): jnp.einsum('nm,nh->mh', matrix, grad_pooled, preferred_element_type=jnp.f...]
    unnamed x2 -> x0, blocking collectives: 74.1 us -> none
    unnamed x3 -> x0, waiting for transfers between devices: 48.9 us -> none
    pallas_call x0 -> x8, Pallas kernels: none -> 34.6 us  [the longest x1 26.5 us: fast_device(): pl.pallas_call(functools.partial(main_kernel, nblk, classes, degree), in_...]
    reduce_sum x13 -> x0, other arithmetic: 27.8 us -> none  [the longest x2 21.1 us: adjacency(): jnp.sum((neighbors[:, :, None] == columns[None, None, :]).astype(jnp.floa...]
  transfers between devices with their start and end apart: 2 -> 24, of which waited for: 2 -> 14; matrix products, arithmetic and copies ran while one was open for 7% -> 2% of each run, Pallas kernels for 0% -> 6%
where the time goes in v1:
time: 86.3 us; the launch traced here: 86.1 us
  Pallas kernels  34.6 us (40%)
  starting transfers between devices  22.5 us (26%)
  waiting for transfers between devices  16.4 us (19%)
  local copies, waits for them, and re-layouts  11.4 us (13%)
  between operations  1.2 us (1%)
    pallas_call x1, Pallas kernels, fast_device(): pl.pallas_call(functools.partial(main_kernel, nblk, classes, degree), in_...  26.5 us
    ppermute x24, starting transfers between devices, swap(): return lax.ppermute(array, AXES, [(i, i ^ bits) for i in range(count)])  22.5 us
    ppermute x24, waiting for transfers between devices, swap(): return lax.ppermute(array, AXES, [(i, i ^ bits) for i in range(count)])  16.4 us
    unnamed x76, local copies, waits for them, and re-layouts  9.51 us
    pallas_call x2, Pallas kernels, fast_device(): pl.pallas_call(functools.partial(graph_kernel, fan_in), grid=(1,), in_spe...  5.17 us
    pallas_call x1, Pallas kernels, fast_device(): pl.pallas_call(functools.partial(step_kernel, fan_in, classes), out_shape...  2.56 us
  transfers between devices with their start and end apart: 24, of which 14 were waited for; matrix products, arithmetic and copies ran while one was open for 2% of the time, Pallas kernels for 6%

profile of v1, /device:TPU:0, one launch (start us, length us, event | category | flops | bytes accessed | tf_op | source)
XLA Modules:
  0.0 86.1 jit_solution(1236442879272397878)
XLA Ops:
  0.7 0.8 copy-done.8
  1.5 0.7 copy-done.10
  2.2 0.7 copy-done.14
  3.1 5.1 %collective-permute-start.2 = (bf16[80,128]{1,0:T(8,128)(2,1)S(1)}, bf16[80,128]{1,0:T(8,128)(2,1)S(1)}, u32[]{:S(2)}, u32[]{:S(2)}) collective-permute-start(bf16[80,128]{1,0:T(8,128)(2,1)S(1)} %pack.1), channel_id=1, source_target_pairs={{0,24},{1,25},{2,26},{3,27},{4,28},{5,29},{6,30},{7,31},{8,16},{9,... | collective-permute-start | bytes 61448 | tf_op jit(solution)/shard_map/ppermute | solution.py:351
  8.2 0.6 collective-permute-start
  8.8 2.6 %graph.3 = (bf16[1024,1024]{1,0:T(8,128)(2,1)S(1)}, bf16[1024,128]{1,0:T(8,128)(2,1)S(1)}, bf16[112,1024]{1,0:T(8,128)(2,1)S(1)}) custom-call(s32[8,2048]{1,0:T(8,128)S(1)} %bitcast.32, bf16[100,2048]{1,0:T(8,128)(2,1)S(1)} %bitcast.30), custom_call_target="tpu_custom_call" | custom-call | flops 3000000000 | bytes 6000000 | tf_op jit(solution)/shard_map/graph/pallas_call | solution.py:384
  11.4 1.3 %copy-done.22 = bf16[1024,1024]{1,0:T(8,128)(2,1)} copy-done((bf16[1024,1024]{1,0:T(8,128)(2,1)}, bf16[1024,1024]{1,0:T(8,128)(2,1)S(1)}, u32[]{:S(2)}) %copy-start.22) | copy-done | bytes 2097176
  12.8 0.7 copy-done.24
  13.5 0.7 copy-done.26
  14.2 2.7 %collective-permute-start.5 = (bf16[80,512]{1,0:T(8,128)(2,1)S(1)}, bf16[80,512]{1,0:T(8,128)(2,1)S(1)}, u32[]{:S(2)}, u32[]{:S(2)}) collective-permute-start(bf16[80,512]{1,0:T(8,128)(2,1)S(1)} %pad_maximum_fusion.refs_0_), channel_id=1, source_target_pairs={{0,6},{1,7},{2,4},{3,5},{4,2},{5,3},{6,0},{7,1},{8,14},{9,15},{10,... | collective-permute-start | bytes 245768 | tf_op jit(solution)/shard_map/ppermute | solution.py:351
  17.8 2.6 %graph.2 = (bf16[1024,1024]{1,0:T(8,128)(2,1)S(1)}, bf16[1024,128]{1,0:T(8,128)(2,1)S(1)}, bf16[112,1024]{1,0:T(8,128)(2,1)S(1)}) custom-call(s32[8,2048]{1,0:T(8,128)S(1)} %bitcast.33, bf16[100,2048]{1,0:T(8,128)(2,1)S(1)} %bitcast.31), custom_call_target="tpu_custom_call" | custom-call | flops 3000000000 | bytes 6000000 | tf_op jit(solution)/shard_map/graph/pallas_call | solution.py:384
  20.4 1.3 %copy-done.23 = bf16[1024,1024]{1,0:T(8,128)(2,1)} copy-done((bf16[1024,1024]{1,0:T(8,128)(2,1)}, bf16[1024,1024]{1,0:T(8,128)(2,1)S(1)}, u32[]{:S(2)}) %copy-start.23) | copy-done | bytes 2097176
  21.7 0.7 copy-done.25
  22.4 0.7 copy-done.27
  25.4 0.7 copy.37.refs_16_
  26.9 26.5 %main.1 = (f32[80,2048]{1,0:T(8,128)}, f32[80,2048]{1,0:T(8,128)}) custom-call(bf16[80,512]{1,0:T(8,128)(2,1)} %copy-done.28, bf16[80,512]{1,0:T(8,128)(2,1)} %copy-done.33, bf16[80,512]{1,0:T(8,128)(2,1)} %copy-done.32, bf16[80,512]{1,0:T(8,128)(2,1)} %copy-done.31, bf16[80,512]{1,0:T(8,128)(2,1)} %copy-done.34, bf16[80,512]{1,0:T(8,128)(2,1)} %copy-done.37, ...), custom_call_target="tpu_custom_call" | custom-call | flops 15000000512 | bytes 30000000 | tf_op jit(solution)/shard_map/main/pallas_call | solution.py:411
  53.8 2.0 %collective-permute-done.10.got_ref = f32[80,2048]{1,0:T(8,128)S(1)} collective-permute-done((f32[80,2048]{1,0:T(8,128)}, f32[80,2048]{1,0:T(8,128)S(1)}, u32[]{:S(2)}, u32[]{:S(2)}) %collective-permute-start.10) | collective-permute-done | bytes 655392 | tf_op jit(solution)/shard_map/ppermute | solution.py:351
  55.8 1.1 %copy-done.21 = f32[80,2048]{1,0:T(8,128)S(1)} copy-done((f32[80,2048]{1,0:T(8,128)S(1)}, f32[80,2048]{1,0:T(8,128)}, u32[]{:S(2)}) %copy-start.21) | copy-done | bytes 655384
  56.9 1.7 %collective-permute-start.11 = (bf16[80,512]{1,0:T(8,128)(2,1)S(1)}, bf16[80,512]{1,0:T(8,128)(2,1)S(1)}, u32[]{:S(2)}, u32[]{:S(2)}) collective-permute-start(bf16[80,512]{1,0:T(8,128)(2,1)S(1)} %get-tuple-element.55), channel_id=1, source_target_pairs={{0,2},{1,3},{2,0},{3,1},{4,6},{5,7},{6,4},{7,5},{8,10},{9,11},{10,... | collective-permute-start | bytes 245768 | tf_op jit(solution)/shard_map/ppermute | solution.py:351
  58.6 1.5 %collective-permute-start.12 = (bf16[80,512]{1,0:T(8,128)(2,1)S(1)}, bf16[80,512]{1,0:T(8,128)(2,1)S(1)}, u32[]{:S(2)}, u32[]{:S(2)}) collective-permute-start(bf16[80,512]{1,0:T(8,128)(2,1)S(1)} %get-tuple-element.56), channel_id=1, source_target_pairs={{0,4},{1,5},{2,6},{3,7},{4,0},{5,1},{6,2},{7,3},{8,12},{9,13},{10,... | collective-permute-start | bytes 245768 | tf_op jit(solution)/shard_map/ppermute | solution.py:351
  60.5 1.2 %collective-permute-done.11.r1_ref = bf16[80,512]{1,0:T(8,128)(2,1)S(1)} collective-permute-done((bf16[80,512]{1,0:T(8,128)(2,1)S(1)}, bf16[80,512]{1,0:T(8,128)(2,1)S(1)}, u32[]{:S(2)}, u32[]{:S(2)}) %collective-permute-start.11) | collective-permute-done | bytes 81952 | tf_op jit(solution)/shard_map/ppermute | solution.py:351
  61.7 2.2 %collective-permute-done.12.r2_ref = bf16[80,512]{1,0:T(8,128)(2,1)S(1)} collective-permute-done((bf16[80,512]{1,0:T(8,128)(2,1)S(1)}, bf16[80,512]{1,0:T(8,128)(2,1)S(1)}, u32[]{:S(2)}, u32[]{:S(2)}) %collective-permute-start.12) | collective-permute-done | bytes 81952 | tf_op jit(solution)/shard_map/ppermute | solution.py:351
  63.9 1.6 %collective-permute-done.13.r3_ref = bf16[80,512]{1,0:T(8,128)(2,1)S(1)} collective-permute-done((bf16[80,512]{1,0:T(8,128)(2,1)S(1)}, bf16[80,512]{1,0:T(8,128)(2,1)S(1)}, u32[]{:S(2)}, u32[]{:S(2)}) %collective-permute-start.13) | collective-permute-done | bytes 81952 | tf_op jit(solution)/shard_map/ppermute | solution.py:351
  65.7 3.7 %collective-permute-start.16 = (bf16[80,512]{1,0:T(8,128)(2,1)S(1)}, bf16[80,512]{1,0:T(8,128)(2,1)S(1)}, u32[]{:S(2)}, u32[]{:S(2)}) collective-permute-start(bf16[80,512]{1,0:T(8,128)(2,1)S(1)} %add_plane.1.h_ref), channel_id=1, source_target_pairs={{0,24},{1,25},{2,26},{3,27},{4,28},{5,29},{6,30},{7,31},{8,16},{9,... | collective-permute-start | bytes 245768 | tf_op jit(solution)/shard_map/ppermute | solution.py:351
  69.4 0.8 collective-permute-start.14
  70.2 1.9 %collective-permute-done.16.z3_ref = bf16[80,512]{1,0:T(8,128)(2,1)S(1)} collective-permute-done((bf16[80,512]{1,0:T(8,128)(2,1)S(1)}, bf16[80,512]{1,0:T(8,128)(2,1)S(1)}, u32[]{:S(2)}, u32[]{:S(2)}) %collective-permute-start.16) | collective-permute-done | bytes 81952 | tf_op jit(solution)/shard_map/ppermute | solution.py:351
  72.1 3.0 %collective-permute-done.15.z2_ref = bf16[80,512]{1,0:T(8,128)(2,1)S(1)} collective-permute-done((bf16[80,512]{1,0:T(8,128)(2,1)S(1)}, bf16[80,512]{1,0:T(8,128)(2,1)S(1)}, u32[]{:S(2)}, u32[]{:S(2)}) %collective-permute-start.15) | collective-permute-done | bytes 81952 | tf_op jit(solution)/shard_map/ppermute | solution.py:351
  75.3 1.0 %collective-permute-start.19 = (bf16[80,512]{1,0:T(8,128)(2,1)S(1)}, bf16[80,512]{1,0:T(8,128)(2,1)S(1)}, u32[]{:S(2)}, u32[]{:S(2)}) collective-permute-start(bf16[80,512]{1,0:T(8,128)(2,1)S(1)} %add_line.1.refs_0_), channel_id=1, source_target_pairs={{0,6},{1,7},{2,4},{3,5},{4,2},{5,3},{6,0},{7,1},{8,14},{9,15},{10,... | collective-permute-start | bytes 245768 | tf_op jit(solution)/shard_map/ppermute | solution.py:351
  76.3 1.2 %collective-permute-start.18 = (bf16[80,512]{1,0:T(8,128)(2,1)S(1)}, bf16[80,512]{1,0:T(8,128)(2,1)S(1)}, u32[]{:S(2)}, u32[]{:S(2)}) collective-permute-start(bf16[80,512]{1,0:T(8,128)(2,1)S(1)} %add_line.1.refs_0_), channel_id=1, source_target_pairs={{0,4},{1,5},{2,6},{3,7},{4,0},{5,1},{6,2},{7,3},{8,12},{9,13},{10,... | collective-permute-start | bytes 245768 | tf_op jit(solution)/shard_map/ppermute | solution.py:351
  77.5 1.4 %collective-permute-start.17 = (bf16[80,512]{1,0:T(8,128)(2,1)S(1)}, bf16[80,512]{1,0:T(8,128)(2,1)S(1)}, u32[]{:S(2)}, u32[]{:S(2)}) collective-permute-start(bf16[80,512]{1,0:T(8,128)(2,1)S(1)} %add_line.1.refs_0_), channel_id=1, source_target_pairs={{0,2},{1,3},{2,0},{3,1},{4,6},{5,7},{6,4},{7,5},{8,10},{9,11},{10,... | collective-permute-start | bytes 245768 | tf_op jit(solution)/shard_map/ppermute | solution.py:351
  78.9 2.1 %collective-permute-done.19.refs_3_ = bf16[80,512]{1,0:T(8,128)(2,1)S(1)} collective-permute-done((bf16[80,512]{1,0:T(8,128)(2,1)S(1)}, bf16[80,512]{1,0:T(8,128)(2,1)S(1)}, u32[]{:S(2)}, u32[]{:S(2)}) %collective-permute-start.19) | collective-permute-done | bytes 81952 | tf_op jit(solution)/shard_map/ppermute | solution.py:351
  83.4 2.6 %update.1 = (f32[1,1]{1,0:T(1,128)}, f32[1,1]{1,0:T(1,128)}, f32[1,1]{1,0:T(1,128)}, f32[64,100]{1,0:T(8,128)}, f32[47,64]{1,0:T(8,128)}, /*index=5*/f32[64,100]...) custom-call(bf16[80,512]{1,0:T(8,128)(2,1)S(1)} %add_line.1.refs_0_,, ...), custom_call_target="tpu_custom_call" | custom-call | flops 5000000000 | bytes 10000000 | tf_op jit(solution)/shard_map/update/pallas_call | solution.py:469
  (105 shorter events, 7.6 us)
Async XLA Ops:
  3.1 11.1 %collective-permute-start.2 = (bf16[80,128]{1,0:T(8,128)(2,1)S(1)}, bf16[80,128]{1,0:T(8,128)(2,1)S(1)}, u32[]{:S(2)}, u32[]{:S(2)}) collective-permute-start(bf16[80,128]{1,0:T(8,128)(2,1)S(1)} %pack.1), channel_id=1, source_target_pairs={{0,24},{1,25},{2,26},{3,27},{4,28},{5,29},{6,30},{7,31},{8,16},{9,... | collective-permute-start | bytes 61448 | tf_op jit(solution)/shard_map/ppermute | solution.py:351
  8.2 6.0 %collective-permute-start.1 = (bf16[80,128]{1,0:T(8,128)(2,1)S(1)}, bf16[80,128]{1,0:T(8,128)(2,1)S(1)}, u32[]{:S(2)}, u32[]{:S(2)}) collective-permute-start(bf16[80,128]{1,0:T(8,128)(2,1)S(1)} %pack.1), channel_id=1, source_target_pairs={{0,16},{1,17},{2,18},{3,19},{4,20},{5,21},{6,22},{7,23},{8,24},{9,... | collective-permute-start | bytes 61448 | tf_op jit(solution)/shard_map/ppermute | solution.py:351
  8.2 6.0 %collective-permute-start = (bf16[80,128]{1,0:T(8,128)(2,1)S(1)}, bf16[80,128]{1,0:T(8,128)(2,1)S(1)}, u32[]{:S(2)}, u32[]{:S(2)}) collective-permute-start(bf16[80,128]{1,0:T(8,128)(2,1)S(1)} %pack.1), channel_id=1, source_target_pairs={{0,8},{1,9},{2,10},{3,11},{4,12},{5,13},{6,14},{7,15},{8,0},{9,1},... | collective-permute-start | bytes 61448 | tf_op jit(solution)/shard_map/ppermute | solution.py:351
  14.2 10.1 %collective-permute-start.5 = (bf16[80,512]{1,0:T(8,128)(2,1)S(1)}, bf16[80,512]{1,0:T(8,128)(2,1)S(1)}, u32[]{:S(2)}, u32[]{:S(2)}) collective-permute-start(bf16[80,512]{1,0:T(8,128)(2,1)S(1)} %pad_maximum_fusion.refs_0_), channel_id=1, source_target_pairs={{0,6},{1,7},{2,4},{3,5},{4,2},{5,3},{6,0},{7,1},{8,14},{9,15},{10,... | collective-permute-start | bytes 245768 | tf_op jit(solution)/shard_map/ppermute | solution.py:351
  16.9 8.0 %collective-permute-start.4 = (bf16[80,512]{1,0:T(8,128)(2,1)S(1)}, bf16[80,512]{1,0:T(8,128)(2,1)S(1)}, u32[]{:S(2)}, u32[]{:S(2)}) collective-permute-start(bf16[80,512]{1,0:T(8,128)(2,1)S(1)} %pad_maximum_fusion.refs_0_), channel_id=1, source_target_pairs={{0,4},{1,5},{2,6},{3,7},{4,0},{5,1},{6,2},{7,3},{8,12},{9,13},{10,... | collective-permute-start | bytes 245768 | tf_op jit(solution)/shard_map/ppermute | solution.py:351
  17.4 7.6 %collective-permute-start.3 = (bf16[80,512]{1,0:T(8,128)(2,1)S(1)}, bf16[80,512]{1,0:T(8,128)(2,1)S(1)}, u32[]{:S(2)}, u32[]{:S(2)}) collective-permute-start(bf16[80,512]{1,0:T(8,128)(2,1)S(1)} %pad_maximum_fusion.refs_0_), channel_id=1, source_target_pairs={{0,2},{1,3},{2,0},{3,1},{4,6},{5,7},{6,4},{7,5},{8,10},{9,11},{10,... | collective-permute-start | bytes 245768 | tf_op jit(solution)/shard_map/ppermute | solution.py:351
  24.3 1.8 %collective-permute-start.6 = (bf16[80,512]{1,0:T(8,128)(2,1)S(1)}, bf16[80,512]{1,0:T(8,128)(2,1)S(1)}, u32[]{:S(2)}, u32[]{:S(2)}) collective-permute-start(bf16[80,512]{1,0:T(8,128)(2,1)S(1)} %pad_maximum_fusion.refs_0_), channel_id=1, source_target_pairs={{0,1},{1,0},{2,3},{3,2},{4,5},{5,4},{6,7},{7,6},{8,9},{9,8},{10,11... | collective-permute-start | bytes 245768 | tf_op jit(solution)/shard_map/ppermute | solution.py:351
  24.4 1.7 %collective-permute-start.9 = (bf16[80,512]{1,0:T(8,128)(2,1)S(1)}, bf16[80,512]{1,0:T(8,128)(2,1)S(1)}, u32[]{:S(2)}, u32[]{:S(2)}) collective-permute-start(bf16[80,512]{1,0:T(8,128)(2,1)S(1)} %collective-permute-done.5.refs_3_), channel_id=1, source_target_pairs={{0,1},{1,0},{2,3},{3,2},{4,5},{5,4},{6,7},{7,6},{8,9},{9,8},{10,11... | collective-permute-start | bytes 245768 | tf_op jit(solution)/shard_map/ppermute | solution.py:351
  24.9 1.3 %collective-permute-start.8 = (bf16[80,512]{1,0:T(8,128)(2,1)S(1)}, bf16[80,512]{1,0:T(8,128)(2,1)S(1)}, u32[]{:S(2)}, u32[]{:S(2)}) collective-permute-start(bf16[80,512]{1,0:T(8,128)(2,1)S(1)} %collective-permute-done.4.refs_2_), channel_id=1, source_target_pairs={{0,1},{1,0},{2,3},{3,2},{4,5},{5,4},{6,7},{7,6},{8,9},{9,8},{10,11... | collective-permute-start | bytes 245768 | tf_op jit(solution)/shard_map/ppermute | solution.py:351
  25.0 1.3 %collective-permute-start.7 = (bf16[80,512]{1,0:T(8,128)(2,1)S(1)}, bf16[80,512]{1,0:T(8,128)(2,1)S(1)}, u32[]{:S(2)}, u32[]{:S(2)}) collective-permute-start(bf16[80,512]{1,0:T(8,128)(2,1)S(1)} %collective-permute-done.3.refs_1_), channel_id=1, source_target_pairs={{0,1},{1,0},{2,3},{3,2},{4,5},{5,4},{6,7},{7,6},{8,9},{9,8},{10,11... | collective-permute-start | bytes 245768 | tf_op jit(solution)/shard_map/ppermute | solution.py:351
  53.4 2.4 %collective-permute-start.10 = (f32[80,2048]{1,0:T(8,128)}, f32[80,2048]{1,0:T(8,128)S(1)}, u32[]{:S(2)}, u32[]{:S(2)}) collective-permute-start(f32[80,2048]{1,0:T(8,128)} %get-tuple-element.53), channel_id=1, source_target_pairs={{0,1},{1,0},{2,3},{3,2},{4,5},{5,4},{6,7},{7,6},{8,9},{9,8},{10,11... | collective-permute-start | bytes 1966088 | tf_op jit(solution)/shard_map/ppermute | solution.py:351
  56.9 4.8 %collective-permute-start.11 = (bf16[80,512]{1,0:T(8,128)(2,1)S(1)}, bf16[80,512]{1,0:T(8,128)(2,1)S(1)}, u32[]{:S(2)}, u32[]{:S(2)}) collective-permute-start(bf16[80,512]{1,0:T(8,128)(2,1)S(1)} %get-tuple-element.55), channel_id=1, source_target_pairs={{0,2},{1,3},{2,0},{3,1},{4,6},{5,7},{6,4},{7,5},{8,10},{9,11},{10,... | collective-permute-start | bytes 245768 | tf_op jit(solution)/shard_map/ppermute | solution.py:351
  58.6 5.3 %collective-permute-start.12 = (bf16[80,512]{1,0:T(8,128)(2,1)S(1)}, bf16[80,512]{1,0:T(8,128)(2,1)S(1)}, u32[]{:S(2)}, u32[]{:S(2)}) collective-permute-start(bf16[80,512]{1,0:T(8,128)(2,1)S(1)} %get-tuple-element.56), channel_id=1, source_target_pairs={{0,4},{1,5},{2,6},{3,7},{4,0},{5,1},{6,2},{7,3},{8,12},{9,13},{10,... | collective-permute-start | bytes 245768 | tf_op jit(solution)/shard_map/ppermute | solution.py:351
  60.2 5.3 %collective-permute-start.13 = (bf16[80,512]{1,0:T(8,128)(2,1)S(1)}, bf16[80,512]{1,0:T(8,128)(2,1)S(1)}, u32[]{:S(2)}, u32[]{:S(2)}) collective-permute-start(bf16[80,512]{1,0:T(8,128)(2,1)S(1)} %get-tuple-element.57), channel_id=1, source_target_pairs={{0,6},{1,7},{2,4},{3,5},{4,2},{5,3},{6,0},{7,1},{8,14},{9,15},{10,... | collective-permute-start | bytes 245768 | tf_op jit(solution)/shard_map/ppermute | solution.py:351
  65.5 17.7 %copy-start = (f32[2048,64]{0,1:T(8,128)S(1)}, f32[2048,64]{0,1:T(8,128)}, u32[]{:S(2)}) copy-start(f32[2048,64]{0,1:T(8,128)} %param.29) | copy-start | bytes 1572868
  65.6 17.7 %copy-start.1 = (f32[64,2048]{1,0:T(8,128)S(1)}, f32[64,2048]{1,0:T(8,128)}, u32[]{:S(2)}) copy-start(f32[64,2048]{1,0:T(8,128)} %refs_14_.1) | copy-start | bytes 1572868
  65.6 17.7 %copy-start.2 = (f32[2048,64]{0,1:T(8,128)S(1)}, f32[2048,64]{0,1:T(8,128)}, u32[]{:S(2)}) copy-start(f32[2048,64]{0,1:T(8,128)} %param.33) | copy-start | bytes 1572868
  65.6 17.7 %copy-start.3 = (f32[64,2048]{1,0:T(8,128)S(1)}, f32[64,2048]{1,0:T(8,128)}, u32[]{:S(2)}) copy-start(f32[64,2048]{1,0:T(8,128)} %refs_18_.1) | copy-start | bytes 1572868
  65.6 17.7 %copy-start.6 = (f32[100,100]{1,0:T(8,128)S(1)}, f32[100,100]{1,0:T(8,128)}, u32[]{:S(2)}) copy-start(f32[100,100]{1,0:T(8,128)} %refs_12_.1) | copy-start | bytes 120004
  65.6 17.7 %copy-start.7 = (f32[100,100]{1,0:T(8,128)S(1)}, f32[100,100]{1,0:T(8,128)}, u32[]{:S(2)}) copy-start(f32[100,100]{1,0:T(8,128)} %refs_16_.1) | copy-start | bytes 120004
  65.6 17.7 %copy-start.9 = (f32[100,64]{0,1:T(8,128)S(1)}, f32[100,64]{0,1:T(8,128)}, u32[]{:S(2)}) copy-start(f32[100,64]{0,1:T(8,128)} %param.24) | copy-start | bytes 76804
  65.6 17.7 %copy-start.11 = (f32[64,47]{0,1:T(8,128)S(1)}, f32[64,47]{0,1:T(8,128)}, u32[]{:S(2)}) copy-start(f32[64,47]{0,1:T(8,128)} %param.25) | copy-start | bytes 36100
  65.7 6.4 %collective-permute-start.16 = (bf16[80,512]{1,0:T(8,128)(2,1)S(1)}, bf16[80,512]{1,0:T(8,128)(2,1)S(1)}, u32[]{:S(2)}, u32[]{:S(2)}) collective-permute-start(bf16[80,512]{1,0:T(8,128)(2,1)S(1)} %add_plane.1.h_ref), channel_id=1, source_target_pairs={{0,24},{1,25},{2,26},{3,27},{4,28},{5,29},{6,30},{7,31},{8,16},{9,... | collective-permute-start | bytes 245768 | tf_op jit(solution)/shard_map/ppermute | solution.py:351
  69.4 5.7 %collective-permute-start.15 = (bf16[80,512]{1,0:T(8,128)(2,1)S(1)}, bf16[80,512]{1,0:T(8,128)(2,1)S(1)}, u32[]{:S(2)}, u32[]{:S(2)}) collective-permute-start(bf16[80,512]{1,0:T(8,128)(2,1)S(1)} %add_plane.1.h_ref), channel_id=1, source_target_pairs={{0,16},{1,17},{2,18},{3,19},{4,20},{5,21},{6,22},{7,23},{8,24},{9,... | collective-permute-start | bytes 245768 | tf_op jit(solution)/shard_map/ppermute | solution.py:351
  69.4 5.9 %collective-permute-start.14 = (bf16[80,512]{1,0:T(8,128)(2,1)S(1)}, bf16[80,512]{1,0:T(8,128)(2,1)S(1)}, u32[]{:S(2)}, u32[]{:S(2)}) collective-permute-start(bf16[80,512]{1,0:T(8,128)(2,1)S(1)} %add_plane.1.h_ref), channel_id=1, source_target_pairs={{0,8},{1,9},{2,10},{3,11},{4,12},{5,13},{6,14},{7,15},{8,0},{9,1},... | collective-permute-start | bytes 245768 | tf_op jit(solution)/shard_map/ppermute | solution.py:351
  75.3 5.7 %collective-permute-start.19 = (bf16[80,512]{1,0:T(8,128)(2,1)S(1)}, bf16[80,512]{1,0:T(8,128)(2,1)S(1)}, u32[]{:S(2)}, u32[]{:S(2)}) collective-permute-start(bf16[80,512]{1,0:T(8,128)(2,1)S(1)} %add_line.1.refs_0_), channel_id=1, source_target_pairs={{0,6},{1,7},{2,4},{3,5},{4,2},{5,3},{6,0},{7,1},{8,14},{9,15},{10,... | collective-permute-start | bytes 245768 | tf_op jit(solution)/shard_map/ppermute | solution.py:351
  76.3 5.3 %collective-permute-start.18 = (bf16[80,512]{1,0:T(8,128)(2,1)S(1)}, bf16[80,512]{1,0:T(8,128)(2,1)S(1)}, u32[]{:S(2)}, u32[]{:S(2)}) collective-permute-start(bf16[80,512]{1,0:T(8,128)(2,1)S(1)} %add_line.1.refs_0_), channel_id=1, source_target_pairs={{0,4},{1,5},{2,6},{3,7},{4,0},{5,1},{6,2},{7,3},{8,12},{9,13},{10,... | collective-permute-start | bytes 245768 | tf_op jit(solution)/shard_map/ppermute | solution.py:351
  77.5 4.4 %collective-permute-start.17 = (bf16[80,512]{1,0:T(8,128)(2,1)S(1)}, bf16[80,512]{1,0:T(8,128)(2,1)S(1)}, u32[]{:S(2)}, u32[]{:S(2)}) collective-permute-start(bf16[80,512]{1,0:T(8,128)(2,1)S(1)} %add_line.1.refs_0_), channel_id=1, source_target_pairs={{0,2},{1,3},{2,0},{3,1},{4,6},{5,7},{6,4},{7,5},{8,10},{9,11},{10,... | collective-permute-start | bytes 245768 | tf_op jit(solution)/shard_map/ppermute | solution.py:351
  78.9 3.3 %collective-permute-start.20 = (bf16[80,512]{1,0:T(8,128)(2,1)S(1)}, bf16[80,512]{1,0:T(8,128)(2,1)S(1)}, u32[]{:S(2)}, u32[]{:S(2)}) collective-permute-start(bf16[80,512]{1,0:T(8,128)(2,1)S(1)} %add_line.1.refs_0_), channel_id=1, source_target_pairs={{0,1},{1,0},{2,3},{3,2},{4,5},{5,4},{6,7},{7,6},{8,9},{9,8},{10,11... | collective-permute-start | bytes 245768 | tf_op jit(solution)/shard_map/ppermute | solution.py:351
  81.0 1.3 %collective-permute-start.23 = (bf16[80,512]{1,0:T(8,128)(2,1)S(1)}, bf16[80,512]{1,0:T(8,128)(2,1)S(1)}, u32[]{:S(2)}, u32[]{:S(2)}) collective-permute-start(bf16[80,512]{1,0:T(8,128)(2,1)S(1)} %collective-permute-done.19.refs_3_), channel_id=1, source_target_pairs={{0,1},{1,0},{2,3},{3,2},{4,5},{5,4},{6,7},{7,6},{8,9},{9,8},{10,11... | collective-permute-start | bytes 245768 | tf_op jit(solution)/shard_map/ppermute | solution.py:351
  81.6 1.3 %collective-permute-start.22 = (bf16[80,512]{1,0:T(8,128)(2,1)S(1)}, bf16[80,512]{1,0:T(8,128)(2,1)S(1)}, u32[]{:S(2)}, u32[]{:S(2)}) collective-permute-start(bf16[80,512]{1,0:T(8,128)(2,1)S(1)} %collective-permute-done.18.refs_2_), channel_id=1, source_target_pairs={{0,1},{1,0},{2,3},{3,2},{4,5},{5,4},{6,7},{7,6},{8,9},{9,8},{10,11... | collective-permute-start | bytes 245768 | tf_op jit(solution)/shard_map/ppermute | solution.py:351
  81.9 1.3 %collective-permute-start.21 = (bf16[80,512]{1,0:T(8,128)(2,1)S(1)}, bf16[80,512]{1,0:T(8,128)(2,1)S(1)}, u32[]{:S(2)}, u32[]{:S(2)}) collective-permute-start(bf16[80,512]{1,0:T(8,128)(2,1)S(1)} %collective-permute-done.17.refs_1_), channel_id=1, source_target_pairs={{0,1},{1,0},{2,3},{3,2},{4,5},{5,4},{6,7},{7,6},{8,9},{9,8},{10,11... | collective-permute-start | bytes 245768 | tf_op jit(solution)/shard_map/ppermute | solution.py:351
  (30 other events, 195.7 us)

commit v2 on v1

--- a/solution.py
+++ b/solution.py
@@ -38,12 +38,25 @@
     return lax.dot_general(a, b, dims, preferred_element_type=f32)
 
 
-def params(limit=56):
-    return pltpu.CompilerParams(vmem_limit_bytes=limit * 2**20)
-
-
-def cost(us):
-    return pl.CostEstimate(flops=int(us * 1e9), bytes_accessed=int(us * 2e6), transcendentals=0)
+def call(kernel, name, us, limit, out_shape, *args, after=(), scratch=(), **kw):
+    n = len(args)
+
+    def body(*refs):
+        kernel(*refs[:n], *refs[n + len(after) :])
+
+    kw.setdefault("in_specs", [pl.BlockSpec(memory_space=pltpu.VMEM)] * n)
+    kw["in_specs"] = list(kw["in_specs"]) + [pl.BlockSpec(memory_space=pl.ANY)] * len(after)
+    return pl.pallas_call(
+        body,
+        out_shape=out_shape,
+        scratch_shapes=scratch,
+        compiler_params=pltpu.CompilerParams(vmem_limit_bytes=limit * 2**20),
+        cost_estimate=pl.CostEstimate(
+            flops=int(us * 1e9), bytes_accessed=int(us * 2e6), transcendentals=0
+        ),
+        name=name,
+        **kw,
+    )(*args, *after)
 
 
 def adam_step(param, grad, first, second):
@@ -57,7 +70,17 @@
     return (first_new, second_new, param - rate_bias * update)
 
 
-def pack_kernel(w1t_ref, w2t_ref, b_ref, out_ref, bottom):
+def pack_kernel(w1t_hbm, w2t_hbm, b_hbm, out_ref, w1t_ref, w2t_ref, b_ref, bottom, sem):
+    copies = [
+        pltpu.make_async_copy(source, target, sem.at[k])
+        for k, (source, target) in enumerate(
+            ((w1t_hbm, w1t_ref), (w2t_hbm, w2t_ref), (b_hbm, b_ref))
+        )
+    ]
+    for copy in copies:
+        copy.start()
+    for copy in copies:
+        copy.wait()
     fan_in = w1t_ref.shape[1]
     width = w1t_ref.shape[0]
     classes = w2t_ref.shape[0]
@@ -74,7 +97,7 @@
     out_ref[:, width : 2 * width] = bottom[...].astype(bf16)
 
 
-def graph_kernel(fan_in, nbr_ref, feat_ref, m_ref, p_ref, pt_ref):
+def graph_kernel(fan_in, block, nbr_ref, feat_ref, m_ref, p_ref, pt_ref):
     classes = nbr_ref.shape[0]
     scale_in = 1.0 / (classes + 1)
     base = lax.broadcasted_iota(jnp.int32, (16, LANES), 0).astype(jnp.int16)
@@ -82,10 +105,11 @@
     zero = jnp.zeros((16, LANES), bf16)
     row = lax.broadcasted_iota(jnp.int32, (LANES, LANES), 0)
     col = lax.broadcasted_iota(jnp.int32, (LANES, LANES), 1)
+    base_at = block * BLOCK
     for t in range(BLOCK // LANES):
         at = slice(t * LANES, (t + 1) * LANES)
         slots = [
-            jnp.broadcast_to(nbr_ref[k : k + 1, at], (16, LANES)).astype(jnp.int16)
+            jnp.broadcast_to(nbr_ref[k : k + 1, base_at + t * LANES : base_at + (t + 1) * LANES], (16, LANES)).astype(jnp.int16)
             for k in range(classes)
         ]
         for u in range(BLOCK // 16):
@@ -96,7 +120,7 @@
             m_ref[u * 16 : (u + 1) * 16, at] = terms[0]
         square = m_ref[at, at].astype(f32)
         m_ref[at, at] = jnp.where(row == col, 2.0 * square + 2.0, square).astype(bf16)
-    pooled = mm(feat_ref[...], m_ref[...]) * scale_in
+    pooled = mm(feat_ref[:, base_at : base_at + BLOCK], m_ref[...]) * scale_in
     rest = LANES - fan_in - 1
     pooled = jnp.concatenate(
         [pooled, jnp.ones((1, BLOCK), f32), jnp.zeros((rest, BLOCK), f32)], axis=0
@@ -105,101 +129,87 @@
     p_ref[...] = pooled.T.astype(bf16)
 
 
-def main_kernel(nblk, classes, degree, *refs):
-    own = refs[0:4]
-    other = refs[4:8]
-    m_hbm = refs[8 : 8 + nblk]
-    p_refs = refs[8 + nblk : 8 + 2 * nblk]
-    pt_refs = refs[8 + 2 * nblk : 8 + 3 * nblk]
-    mask_ref, label_ref, b2_ref = refs[8 + 3 * nblk : 11 + 3 * nblk]
-    keep_ref, send_ref = refs[11 + 3 * nblk : 13 + 3 * nblk]
-    w, ww, hid, der, m, z, qq, qqt, row_scr, sem = refs[13 + 3 * nblk :]
-    hidden = w.shape[1]
-    core = lax.axis_index("shard")
-    first = core == 0
-    scale_in = 1.0 / (degree + 1)
-    copies = [
-        pltpu.make_async_copy(m_hbm[b], m.at[b], sem.at[b]) for b in range(nblk)
-    ]
-    for c in copies:
-        c.start()
-
-    lane = lax.broadcasted_iota(jnp.int32, (HALF, LANES), 1)
-    left = lane < LANES // 2
-    for g in range(4):
-        for s in range(4):
-            at = slice(s * LANES, (s + 1) * LANES)
-            to = slice((g * 4 + s) * LANES, (g * 4 + s + 1) * LANES)
-            mine = own[g][:, at].astype(f32)
-            theirs = other[g][:, at].astype(f32)
-            lo = jnp.where(first, mine, theirs)
-            hi = jnp.where(first, theirs, mine)
-            w[0:HALF, to] = jnp.where(left, lo, pltpu.roll(hi, LANES // 2, 1)).astype(bf16)
-            w[HALF:ROWS, to] = jnp.where(left, pltpu.roll(lo, LANES // 2, 1), hi).astype(bf16)
+def forward_kernel(nblk, *refs):
+    own_ref, other_ref = refs[0:2]
+    p_refs = refs[2 : 2 + nblk]
+    ww, hid, der, zt, w = refs[2 + nblk :]
+    group = w.shape[1]
+    first = lax.axis_index("shard") == 0
+
+    left = lax.broadcasted_iota(jnp.int32, (HALF, LANES), 1) < LANES // 2
+    row = lax.broadcasted_iota(jnp.int32, (HALF, LANES), 0)
+    for s in range(group // LANES):
+        at = slice(s * LANES, (s + 1) * LANES)
+        mine = own_ref[:, at].astype(f32)
+        theirs = other_ref[:, at].astype(f32)
+        lo = jnp.where(first, mine, theirs)
+        hi = jnp.where(first, theirs, mine)
+        upper = jnp.where(left, lo, pltpu.roll(hi, LANES // 2, 1))
+        lower = jnp.where(left, pltpu.roll(lo, LANES // 2, 1), hi)
+        w[0:HALF, at] = (0.5 * upper).astype(bf16)
+        w[HALF:ROWS, at] = jnp.where(row < TOP - HALF, 0.5 * lower, lower).astype(bf16)
     ww[0:48, :] = w[TOP:ROWS, :]
     ww[48:96, :] = w[TOP:ROWS, :]
-    ww[96:128, :] = jnp.zeros((32, hidden), bf16)
+    ww[96:128, :] = jnp.zeros((32, group), bf16)
 
     c0 = 0.7978845608028654
     c1 = c0 * 0.044715
-    chunk = 512
-    sub = 256
-    rows = 256
-
-    def forward(n, _):
-        n0 = pl.multiple_of(n * chunk, chunk)
+    narrow = 256
+    for n in range(group // narrow):
+        at = slice(n * narrow, (n + 1) * narrow)
         for b in range(nblk):
-            for r in range(BLOCK // rows):
-                total = None
-                for k in range(chunk // sub):
-                    at = pl.ds(n0 + k * sub, sub)
-                    to = slice(b * BLOCK + r * rows, b * BLOCK + (r + 1) * rows)
-                    x = mm(p_refs[b][r * rows : (r + 1) * rows, :], w[0:LANES, at])
-                    x2 = x * x
-                    t = jnp.tanh(x * (c0 + c1 * x2))
-                    p = 0.5 * t + 0.5
-                    h = x * p
-                    d = p + h * (1.0 - p) * (2.0 * c0 + 6.0 * c1 * x2)
-                    hb = h.astype(bf16)
-                    hid[to, at] = hb
-                    der[to, at] = d.astype(bf16)
-                    part = mm(hb, w[TOP:ROWS, at], NT)
-                    total = part if total is None else total + part
-                z[to, 0:48] += total
-        return 0
-
-    z[...] = jnp.zeros_like(z)
-    lax.fori_loop(0, hidden // chunk, forward, 0)
-
+            to = slice(b * BLOCK, (b + 1) * BLOCK)
+            x = mm(p_refs[b][...], w[0:LANES, at])
+            xb = x.astype(bf16)
+            k = bf16(8.0 * c1) * (xb * xb)
+            s = bf16(1.0) + jnp.tanh(xb * (k + bf16(2.0 * c0)))
+            hb = xb * s
+            d = s + ((bf16(2.0) - s) * hb) * (bf16(3.0) * k + bf16(2.0 * c0))
+            hid[to, at] = hb
+            der[to, at] = d.astype(bf16)
+            part = mm(w[TOP:ROWS, at], hb, NT)
+            zt[b] = part if n == 0 else zt[b] + part
+
+
+def middle_kernel(nblk, classes, degree, *refs):
+    z_refs = refs[0:4]
+    m_refs = refs[4 : 4 + nblk]
+    mask_ref, label_ref, b2_ref = refs[4 + nblk : 7 + nblk]
+    qq, qqt, scal_ref, row_scr = refs[7 + nblk :]
+    first = lax.axis_index("shard") == 0
+    scale_in = 1.0 / (degree + 1)
+    pick = lax.broadcasted_iota(jnp.int32, (48, classes), 0) == lax.broadcasted_iota(
+        jnp.int32, (48, classes), 1
+    )
+    bias = jnp.sum(jnp.where(pick, b2_ref[...], 0.0), axis=1, keepdims=True)
     row_scr[...] = jnp.zeros_like(row_scr)
     loss = jnp.zeros((1, 1), f32)
     count = jnp.zeros((1, 1), f32)
     for b in range(nblk):
-        copies[b].wait()
-        zb = z[b * BLOCK : (b + 1) * BLOCK, :].T
-        zb = zb[0:48]
+        zb = (z_refs[0][b] + z_refs[1][b]) + (z_refs[2][b] + z_refs[3][b])
         z_hi = zb.astype(bf16)
         z_lo = (zb - z_hi.astype(f32)).astype(bf16)
-        both = mm(jnp.concatenate([z_hi, z_lo], axis=0), m[b])
-        logits = (both[0:48] + both[48:96]) * scale_in + b2_ref[...]
+        both = mm(jnp.concatenate([z_hi, z_lo], axis=0), m_refs[b][...])
+        logits = (both[0:48] + both[48:96]) * scale_in + bias
         cls = lax.broadcasted_iota(jnp.int32, (48, BLOCK), 0)
         logits = jnp.where(cls < classes, logits, -1e30)
         top = jnp.max(logits, axis=0, keepdims=True)
         e = jnp.exp(logits - top)
         total = jnp.sum(e, axis=0, keepdims=True)
-        hit = cls == label_ref[b : b + 1, :]
-        weight = mask_ref[b : b + 1, :].astype(f32)
+        mine = slice(b * BLOCK, (b + 1) * BLOCK)
+        hit = cls == label_ref[mine].reshape(1, BLOCK)
+        weight = mask_ref[mine].reshape(1, BLOCK).astype(f32)
         picked = jnp.sum(jnp.where(hit, logits, 0.0), axis=0, keepdims=True)
         loss += jnp.sum((jnp.log(total) + top - picked) * weight, axis=1, keepdims=True)
         count += jnp.sum(weight, axis=1, keepdims=True)
         grad = ((e / total - hit.astype(f32)) * weight).astype(bf16)
         row_scr[:, 0:48] += mm(jnp.ones((8, BLOCK), bf16), grad, NT)
-        q = mm(grad, m[b], NT) * scale_in
+        q = mm(grad, m_refs[b][...], NT) * scale_in
         q_hi = q.astype(bf16)
         q_lo = q - q_hi.astype(f32)
         q2 = jnp.concatenate([q_hi.astype(f32), q_lo, jnp.zeros((32, BLOCK), f32)], axis=0)
         qqt[b] = q2[0:96].astype(bf16)
-        qq[b * BLOCK : (b + 1) * BLOCK, :] = q2.T.astype(bf16)
+        qq[b * BLOCK : (b + 1) * BLOCK, :] = (0.5 * q2).T.astype(bf16)
 
     vec = row_scr[0:1, :]
     pos = lax.broadcasted_iota(jnp.int32, vec.shape, 1)
@@ -207,44 +217,57 @@
     part_a = vec.astype(bf16).astype(f32)
     part_b = (vec - part_a).astype(bf16).astype(f32)
     part_c = (vec - part_a - part_b).astype(bf16).astype(f32)
-    r16 = lax.broadcasted_iota(jnp.int32, (16, vec.shape[1]), 0) - jnp.where(first, 5, 8)
-    scal = (
+    r16 = lax.broadcasted_iota(jnp.int32, (16, LANES), 0) - jnp.where(first, 5, 8)
+    scal_ref[...] = (
         jnp.where(r16 == 0, part_a, 0.0)
         + jnp.where(r16 == 1, part_b, 0.0)
         + jnp.where(r16 == 2, part_c, 0.0)
     )
 
-    def backward(n, _):
-        at = pl.ds(pl.multiple_of(n * sub, sub), sub)
-        d1 = jnp.zeros((TOP, sub), f32)
-        d2 = jnp.zeros((96, sub), f32)
-        for b in range(nblk):
-            to = slice(b * BLOCK, (b + 1) * BLOCK)
-            gp = (mm(qq[to, :], ww[:, at]) * der[to, at].astype(f32)).astype(bf16)
-            d1 = d1 + mm(pt_refs[b][...], gp)
-            d2 = d2 + mm(qqt[b], hid[to, at])
-        d2 = d2[0:48] + d2[48:96]
-        extra = jnp.where(n == 0, scal, 0.0)
-        upper = d1[0:HALF]
-        lower = jnp.concatenate([d1[HALF:96], d1[96:TOP] + extra, d2], axis=0)
-        keep_ref[:, at] = jnp.where(first, upper, lower)
-        send_ref[:, at] = jnp.where(first, lower, upper)
-        return 0
-
-    lax.fori_loop(0, hidden // sub, backward, 0)
-
-
-def add_core_kernel(keep_ref, got_ref, g0_ref, s1_ref, s2_ref, s3_ref):
-    n = g0_ref.shape[1]
-    g0_ref[...] = keep_ref[:, 0:n] + got_ref[:, 0:n]
-    for k, out in enumerate((s1_ref, s2_ref, s3_ref)):
-        at = slice((k + 1) * n, (k + 2) * n)
-        out[...] = (keep_ref[:, at] + got_ref[:, at]).astype(bf16)
-
-
-def add_plane_kernel(g0_ref, r1_ref, r2_ref, r3_ref, out_ref):
+
+def backward_kernel(nblk, has_scalars, *refs):
+    qq, qqt = refs[0:2]
+    pt_refs = refs[2 : 2 + nblk]
+    ww, hid, der, scal_ref = refs[2 + nblk : 6 + nblk]
+    keep_ref, send_ref = refs[6 + nblk :]
+    first = lax.axis_index("shard") == 0
+    group = ww.shape[1]
+    d1 = jnp.zeros((TOP, group), f32)
+    d2 = jnp.zeros((96, group), f32)
+    for b in range(nblk):
+        to = slice(b * BLOCK, (b + 1) * BLOCK)
+        gp = (mm(qq[to, :], ww[...]) * der[to, :].astype(f32)).astype(bf16)
+        d1 = d1 + mm(pt_refs[b][...], gp)
+        d2 = d2 + mm(qqt[b], hid[to, :])
+    d2 = d2[0:48] + d2[48:96]
+    upper = d1[0:HALF]
+    middle = d1[96:TOP]
+    if has_scalars:
+        middle += jnp.concatenate([scal_ref[...], jnp.zeros((16, group - LANES), f32)], axis=1)
+    lower = jnp.concatenate([d1[HALF:96], middle, d2], axis=0)
+    keep_ref[...] = jnp.where(first, upper, lower)
+    send_ref[...] = jnp.where(first, lower, upper)
+
+
+def add_core_kernel(*refs):
+    keeps, gots, outs = refs[0:4], refs[4:8], refs[8:12]
+    first = lax.axis_index("shard") == 0
+    total = [
+        [
+            keep[:, u * LANES : (u + 1) * LANES] + got[:, u * LANES : (u + 1) * LANES]
+            for u in range(4)
+        ]
+        for keep, got in zip(keeps, gots, strict=True)
+    ]
+    for k, out in enumerate(outs):
+        for u in range(4):
+            picked = jnp.where(first, total[k][u], total[u][k])
+            out[:, u * LANES : (u + 1) * LANES] = picked.astype(out.dtype)
+
+
+def add_piece_kernel(own_ref, r1_ref, r2_ref, r3_ref, out_ref):
     out_ref[...] = (
-        g0_ref[...] + r1_ref[...].astype(f32) + r2_ref[...].astype(f32) + r3_ref[...].astype(f32)
+        own_ref[...] + r1_ref[...].astype(f32) + r2_ref[...].astype(f32) + r3_ref[...].astype(f32)
     ).astype(bf16)
 
 
@@ -272,21 +295,17 @@
     core = lax.axis_index("shard")
     first = core == 0
     half = LANES // 2
-    scal = jnp.zeros((16, LANES), f32)
-    for k in range(4):
-        for s in range(4):
-            at = slice(s * LANES, (s + 1) * LANES)
-            mine = own[k][:, at].astype(f32)
-            theirs = other[k][:, at].astype(f32)
-            upper = jnp.where(first, mine, theirs)
-            lower = jnp.where(first, theirs, mine)
-            scal += lower[16:32]
-            to = pl.ds(pl.multiple_of((chip ^ (s * 4 + k)) * LANES, LANES), LANES)
-            g[0:HALF, to] = upper.astype(bf16)
-            g[HALF:96, to] = lower[0:16].astype(bf16)
-            keep = lax.broadcasted_iota(jnp.int32, (16, LANES), 0) <= fan_in - 96
-            g[96:TOP, to] = jnp.where(keep, lower[16:32], 0.0).astype(bf16)
-            g[TOP:ROWS, to] = lower[32:80].astype(bf16)
+    for refs_of, owner in ((own, core), (other, 1 - core)):
+        rows = pl.ds(pl.multiple_of(owner * HALF, 16), HALF)
+        for k in range(4):
+            for u in range(4):
+                slot = jnp.where(owner == 0, u * 4 + k, k * 4 + u)
+                to = pl.ds(pl.multiple_of((chip ^ slot) * LANES, LANES), LANES)
+                g[rows, to] = refs_of[k][:, u * LANES : (u + 1) * LANES]
+    mixed = g[96:TOP, :].astype(f32)
+    scal = sum(mixed[:, u * LANES : (u + 1) * LANES] for u in range(mixed.shape[1] // LANES))
+    keep = lax.broadcasted_iota(jnp.int32, mixed.shape, 0) <= fan_in - 96
+    g[96:TOP, :] = jnp.where(keep, mixed, 0.0).astype(bf16)
     row16 = lax.broadcasted_iota(jnp.int32, (16, LANES), 0)
     scal = jnp.where((row16 >= 5) & (row16 <= 10), scal, 0.0)
     vec = jnp.sum(scal, axis=0, keepdims=True)
@@ -346,9 +365,10 @@
     )
 
 
-def swap(array, bits):
+def swap(array, bits, bits_one=None):
     count = lax.axis_size(AXES)
-    return lax.ppermute(array, AXES, [(i, i ^ bits) for i in range(count)])
+    both = (bits, bits if bits_one is None else bits_one)
+    return lax.ppermute(array, AXES, [(i, i ^ both[i % 2]) for i in range(count)])
 
 
 def fast_device(
@@ -365,126 +385,95 @@
     shape = jax.ShapeDtypeStruct
     w1t, w2t, b1 = w_first.T, w_second.T, b_first.reshape(1, width)
 
-    piece = pl.pallas_call(
-        pack_kernel,
-        out_shape=shape((HALF, LANES), bf16),
-        scratch_shapes=[pltpu.VMEM((HALF, width), f32)],
-        compiler_params=params(8),
-        cost_estimate=cost(1),
-        name="pack",
-    )(w1t, w2t, b1)
+    piece = call(
+        pack_kernel, "pack", 1, 60, shape((HALF, LANES), bf16), w1t, w2t, b1,
+        in_specs=[pl.BlockSpec(memory_space=pl.ANY)] * 3,
+        scratch=[
+            pltpu.VMEM(w1t.shape, f32),
+            pltpu.VMEM(w2t.shape, f32),
+            pltpu.VMEM(b1.shape, f32),
+            pltpu.VMEM((HALF, width), f32),
+            pltpu.SemaphoreType.DMA((3,)),
+        ],
+    )
     line = jnp.concatenate([piece] + [swap(piece, 8 * k) for k in (1, 2, 3)], axis=1)
     plane = [line] + [swap(line, 2 * k) for k in (1, 2, 3)]
-    partner = [swap(part, 1) for part in plane]
-
-    graphs = []
+    partner = [swap(line, 1)]
+
     nbr_t, feat_t = neighbors.T, features.T
-    for b in range(nblk):
-        graphs.append(
-            pl.pallas_call(
-                functools.partial(graph_kernel, fan_in),
-                grid=(1,),
-                in_specs=[
-                    pl.BlockSpec((degree, BLOCK), lambda i, b=b: (0, b)),
-                    pl.BlockSpec((fan_in, BLOCK), lambda i, b=b: (0, b)),
+    graphs = [
+        call(
+            functools.partial(graph_kernel, fan_in, b), "graph", 2.6, 4,
+            [shape((BLOCK, BLOCK), bf16), shape((BLOCK, LANES), bf16), shape((TOP, BLOCK), bf16)],
+            nbr_t, feat_t, after=[line] * (b > 0),
+        )
+        for b in range(nblk)
+    ]
+    ms, ps, pts = ([graph[k] for graph in graphs] for k in range(3))
+
+    nodes = nblk * BLOCK
+    fwd = []
+    for g in range(4):
+        if g:
+            plane[g], _ = lax.optimization_barrier((plane[g], fwd[0][3]))
+            partner.append(swap(plane[g], 1))
+        fwd.append(
+            call(
+                functools.partial(forward_kernel, nblk), "forward", 2, 4,
+                [
+                    shape((LANES, group), bf16), shape((nodes, group), bf16),
+                    shape((nodes, group), bf16), shape((nblk, 48, BLOCK), f32),
                 ],
-                out_specs=[
-                    pl.BlockSpec((BLOCK, BLOCK), lambda i: (0, 0)),
-                    pl.BlockSpec((BLOCK, LANES), lambda i: (0, 0)),
-                    pl.BlockSpec((TOP, BLOCK), lambda i: (0, 0)),
-                ],
-                out_shape=[
-                    shape((BLOCK, BLOCK), bf16),
-                    shape((BLOCK, LANES), bf16),
-                    shape((TOP, BLOCK), bf16),
-                ],
-                compiler_params=params(24),
-                cost_estimate=cost(3),
-                name="graph",
-            )(nbr_t, feat_t)
-        )
-    ms = [graph[0] for graph in graphs]
-    ps = [graph[1] for graph in graphs]
-    pts = [graph[2] for graph in graphs]
-
-    vmem = pl.BlockSpec(memory_space=pltpu.VMEM)
-    keep, send = pl.pallas_call(
-        functools.partial(main_kernel, nblk, classes, degree),
-        in_specs=[vmem] * 8 + [pl.BlockSpec(memory_space=pl.ANY)] * nblk + [vmem] * (2 * nblk + 3),
-        out_specs=[vmem, vmem],
-        out_shape=[shape((HALF, hidden), f32)] * 2,
-        scratch_shapes=[
-            pltpu.VMEM((ROWS, hidden), bf16),
-            pltpu.VMEM((LANES, hidden), bf16),
-            pltpu.VMEM((nblk * BLOCK, hidden), bf16),
-            pltpu.VMEM((nblk * BLOCK, hidden), bf16),
-            pltpu.VMEM((nblk, BLOCK, BLOCK), bf16),
-            pltpu.VMEM((nblk * BLOCK, LANES), f32),
-            pltpu.VMEM((nblk * BLOCK, LANES), bf16),
-            pltpu.VMEM((nblk, 96, BLOCK), bf16),
-            pltpu.VMEM((8, 256), f32),
-            pltpu.SemaphoreType.DMA((nblk,)),
-        ],
-        compiler_params=params(),
-        cost_estimate=cost(15),
-        name="main",
-    )(
-        *plane,
-        *partner,
-        *ms,
-        *ps,
-        *pts,
-        label_mask.reshape(nblk, BLOCK),
-        labels.reshape(nblk, BLOCK),
-        jnp.pad(b_second, (0, 48 - classes)).reshape(48, 1),
-    )
-
-    got = swap(send, 1)
-    g0, s1, s2, s3 = pl.pallas_call(
-        add_core_kernel,
-        out_shape=[shape((HALF, group), f32)] + [shape((HALF, group), bf16)] * 3,
-        compiler_params=params(16),
-        cost_estimate=cost(1),
-        name="add_core",
-    )(keep, got)
-    mine = pl.pallas_call(
-        add_plane_kernel,
-        out_shape=shape((HALF, group), bf16),
-        compiler_params=params(8),
-        cost_estimate=cost(1),
-        name="add_plane",
-    )(g0, swap(s1, 2), swap(s2, 4), swap(s3, 6))
-    mine = pl.pallas_call(
-        add_line_kernel,
-        out_shape=shape((HALF, group), bf16),
-        compiler_params=params(8),
-        cost_estimate=cost(1),
-        name="add_line",
-    )(mine, swap(mine, 8), swap(mine, 16), swap(mine, 24))
-    plane = [mine] + [swap(mine, 2 * k) for k in (1, 2, 3)]
+                plane[g], partner[g], *ps,
+                scratch=[pltpu.VMEM((ROWS, group), bf16)],
+            )
+        )
+    qq, qqt, scal = call(
+        functools.partial(middle_kernel, nblk, classes, degree), "middle", 2.6, 4,
+        [shape((nodes, LANES), bf16), shape((nblk, 96, BLOCK), bf16), shape((16, LANES), f32)],
+        *[f[3] for f in fwd], *ms, label_mask, labels, b_second.reshape(1, classes),
+        scratch=[pltpu.VMEM((8, LANES), f32)],
+    )
+    keeps, gots = [], []
+    for g in range(4):
+        keep, send = call(
+            functools.partial(backward_kernel, nblk, g == 0), "backward", 1.4, 4,
+            [shape((HALF, group), f32)] * 2,
+            qq, qqt, *pts, *fwd[g][0:3], scal,
+        )
+        keeps.append(keep)
+        gots.append(swap(send, 1))
+    mine, *rest = call(
+        add_core_kernel, "add_core", 0.3, 4,
+        [shape((HALF, group), f32)] + [shape((HALF, group), bf16)] * 3, *keeps, *gots,
+    )
+    mine = call(
+        add_piece_kernel, "add_piece", 0.3, 2, shape((HALF, group), bf16),
+        mine, *[swap(rest[k - 1], 2 * k, 8 * k) for k in (1, 2, 3)],
+    )
+    mine = call(
+        add_line_kernel, "add_line", 0.3, 2, shape((HALF, group), bf16),
+        mine, *[swap(mine, 8 * k, 2 * k) for k in (1, 2, 3)],
+    )
+    plane = [mine] + [swap(mine, 2 * k, 8 * k) for k in (1, 2, 3)]
     partner = [swap(part, 1) for part in plane]
 
     one = shape((1, 1), f32)
     row1, row2 = shape((1, width), f32), shape((1, classes), f32)
-    outs = pl.pallas_call(
-        functools.partial(step_kernel, fan_in, classes),
-        out_shape=[
+    outs = call(
+        functools.partial(step_kernel, fan_in, classes), "update", 2.5, 8,
+        [
             one, one, one, shape(w1t.shape, f32), shape(w2t.shape, f32), shape(w1t.shape, f32),
             shape(w2t.shape, f32), shape(l_first.shape, f32), shape((width, hidden), f32),
             shape((width, hidden), f32), shape(r_second.shape, f32),
             row1, row1, row1, row2, row2, row2,
         ],
-        scratch_shapes=[pltpu.VMEM((ROWS, hidden), bf16)],
-        compiler_params=params(32),
-        cost_estimate=cost(5),
-        name="update",
-    )(
-        *plane,
-        *partner,
+        *plane, *partner,
         w1t, w2t, b1, b_second.reshape(1, classes), l_first, r_first.T, l_second, r_second,
         l_first_root, r_first_root.T, l_second_root, r_second_root,
         m_first.reshape(1, width), v_first.reshape(1, width),
         m_second.reshape(1, classes), v_second.reshape(1, classes),
+        scratch=[pltpu.VMEM((ROWS, hidden), bf16)],
     )
     loss, count, norm, grad1, grad2, w1, w2, l1, r1, l2, r2, m1, v1, nb1, m2, v2, nb2 = outs
     return (

time: 86.3 us -> 64.9 us (0.75)
  local copies, waits for them, and re-layouts: 11.4 us -> 0.13 us
  Pallas kernels: 34.6 us -> 23.9 us
  starting transfers between devices: 22.5 us -> 23.7 us
    pallas_call x8 -> x16, Pallas kernels: 34.6 us -> 23.9 us  [call(): pl.pallas_call(body, out_shape=out_shape, scratch_shapes=scratch, compile...]
    unnamed x76 -> x42, local copies, waits for them, and re-layouts: 9.51 us -> 0.13 us
    reshape x4 -> x0, local copies, waits for them, and re-layouts: 1.92 us -> none  [the longest x2 0.7 us: fast_device(): jnp.pad(b_second, (0, 48 - classes)).reshape(48, 1)]
    ppermute x24 -> x27, starting transfers between devices: 22.5 us -> 23.7 us  [swap(): lax.ppermute(array, AXES, [(i, i ^ both[i % 2]) for i in range(count)])]
    ppermute x24 -> x27, waiting for transfers between devices: 16.4 us -> 15.7 us  [swap(): lax.ppermute(array, AXES, [(i, i ^ both[i % 2]) for i in range(count)])]
  transfers between devices with their start and end apart: 24 -> 27, of which waited for: 14 -> 13; matrix products, arithmetic and copies ran while one was open for 2% -> 0% of each run, Pallas kernels for 6% -> 21%
where the time goes in v2:
time: 64.9 us; the launch traced here: 64.8 us
  Pallas kernels  23.9 us (37%)
  starting transfers between devices  23.7 us (37%)
  waiting for transfers between devices  15.7 us (24%)
  between operations  1.23 us (2%)
    pallas_call x16, Pallas kernels, call(): pl.pallas_call(body, out_shape=out_shape, scratch_shapes=scratch, compile...  23.9 us
    ppermute x27, starting transfers between devices, swap(): lax.ppermute(array, AXES, [(i, i ^ both[i % 2]) for i in range(count)])  23.7 us
    ppermute x27, waiting for transfers between devices, swap(): lax.ppermute(array, AXES, [(i, i ^ both[i % 2]) for i in range(count)])  15.7 us
  transfers between devices with their start and end apart: 27, of which 13 were waited for; matrix products, arithmetic and copies ran while one was open for 0% of the time, Pallas kernels for 21%

profile of v2, /device:TPU:0, one launch (start us, length us, event | category | flops | bytes accessed | tf_op | source)
XLA Modules:
  0.0 64.8 jit_solution(310754583555740241)
XLA Ops:
  0.7 1.7 %pack.1 = bf16[80,128]{1,0:T(8,128)(2,1)} custom-call(f32[64,100]{1,0:T(8,128)} %bitcast.32, f32[47,64]{1,0:T(8,128)} %bitcast.34, f32[1,64]{1,0:T(1,128)} %bitcast.36), custom_call_target="tpu_custom_call" | custom-call | flops 1000000000 | bytes 2000000 | tf_op jit(solution)/shard_map/pack/pallas_call | solution.py:49
  2.4 5.1 %collective-permute-start.2 = (bf16[80,128]{1,0:T(8,128)(2,1)}, bf16[80,128]{1,0:T(8,128)(2,1)S(1)}, u32[]{:S(2)}, u32[]{:S(2)}) collective-permute-start(bf16[80,128]{1,0:T(8,128)(2,1)} %pack.1), channel_id=1, source_target_pairs={{0,24},{1,25},{2,26},{3,27},{4,28},{5,29},{6,30},{7,31},{8,16},{9,... | collective-permute-start | bytes 61448 | tf_op jit(solution)/shard_map/ppermute | solution.py:371
  7.5 0.6 collective-permute-start
  8.1 2.6 %graph.2 = (bf16[1024,1024]{1,0:T(8,128)(2,1)S(1)}, bf16[1024,128]{1,0:T(8,128)(2,1)S(1)}, bf16[112,1024]{1,0:T(8,128)(2,1)S(1)}) custom-call(s32[8,2048]{1,0:T(8,128)S(1)} %bitcast.30, bf16[100,2048]{1,0:T(8,128)(2,1)S(1)} %bitcast.28), custom_call_target="tpu_custom_call" | custom-call | flops 2600000000 | bytes 5200000 | tf_op jit(solution)/shard_map/graph/pallas_call | solution.py:49
  10.7 1.6 %collective-permute-done.1 = bf16[80,128]{1,0:T(8,128)(2,1)S(1)} collective-permute-done((bf16[80,128]{1,0:T(8,128)(2,1)}, bf16[80,128]{1,0:T(8,128)(2,1)S(1)}, u32[]{:S(2)}, u32[]{:S(2)}) %collective-permute-start.1) | collective-permute-done | bytes 20512 | tf_op jit(solution)/shard_map/ppermute | solution.py:371
  12.4 2.5 %collective-permute-start.8 = (bf16[80,512]{1,0:T(8,128)(2,1)S(1)}, bf16[80,512]{1,0:T(8,128)(2,1)S(1)}, u32[]{:S(2)}, u32[]{:S(2)}) collective-permute-start(bf16[80,512]{1,0:T(8,128)(2,1)S(1)} %pad_maximum_fusion.refs_2_.refs_0_), channel_id=1, source_target_pairs={{0,6},{1,7},{2,4},{3,5},{4,2},{5,3},{6,0},{7,1},{8,14},{9,15},{10,... | collective-permute-start | bytes 245768 | tf_op jit(solution)/shard_map/ppermute | solution.py:371
  15.9 2.6 %graph.3 = (bf16[1024,1024]{1,0:T(8,128)(2,1)S(1)}, bf16[1024,128]{1,0:T(8,128)(2,1)S(1)}, bf16[112,1024]{1,0:T(8,128)(2,1)S(1)}) custom-call(s32[8,2048]{1,0:T(8,128)S(1)} %bitcast.31, bf16[100,2048]{1,0:T(8,128)(2,1)S(1)} %bitcast.29, bf16[80,512]{1,0:T(8,128)(2,1)S(1)} %pad_maximum_fusion.refs_2_.refs_0_), custom_call_target="tpu_custom_call" | custom-call | flops 2600000000 | bytes 5200000 | tf_op jit(solution)/shard_map/graph/pallas_call | solution.py:49
  18.5 1.5 %forward.4 = (bf16[128,512]{1,0:T(8,128)(2,1)S(1)}, bf16[2048,512]{1,0:T(8,128)(2,1)S(1)}, bf16[2048,512]{1,0:T(8,128)(2,1)S(1)}, f32[2,48,1024]{2,1,0:T(8,128)S(1)}) custom-call(bf16[80,512]{1,0:T(8,128)(2,1)S(1)} %pad_maximum_fusion.refs_2_.refs_0_, bf16[80,512]{1,0:T(8,128)(2,1)S(1)} %collective-permute-done.3.refs_1_, ...), custom_call_target="tpu_custom_call" | custom-call | flops 2000000000 | bytes 4000000 | tf_op jit(solution)/shard_map/forward/pallas_call | solution.py:49
  20.1 0.6 collective-permute-start.9
  21.6 1.5 %forward.7 = (bf16[128,512]{1,0:T(8,128)(2,1)S(1)}, bf16[2048,512]{1,0:T(8,128)(2,1)S(1)}, bf16[2048,512]{1,0:T(8,128)(2,1)S(1)}, f32[2,48,1024]{2,1,0:T(8,128)S(1)}) custom-call(bf16[80,512]{1,0:T(8,128)(2,1)S(1)} %collective-permute-done.8.refs_0_, bf16[80,512]{1,0:T(8,128)(2,1)S(1)} %collective-permute-done.9.refs_1_, ...), custom_call_target="tpu_custom_call" | custom-call | flops 2000000000 | bytes 4000000 | tf_op jit(solution)/shard_map/forward/pallas_call | solution.py:49
  23.1 1.5 %forward.6 = (bf16[128,512]{1,0:T(8,128)(2,1)S(1)}, bf16[2048,512]{1,0:T(8,128)(2,1)S(1)}, bf16[2048,512]{1,0:T(8,128)(2,1)S(1)}, f32[2,48,1024]{2,1,0:T(8,128)S(1)}) custom-call(bf16[80,512]{1,0:T(8,128)(2,1)S(1)} %collective-permute-done.6.refs_0_, bf16[80,512]{1,0:T(8,128)(2,1)S(1)} %collective-permute-done.7.refs_1_, ...), custom_call_target="tpu_custom_call" | custom-call | flops 2000000000 | bytes 4000000 | tf_op jit(solution)/shard_map/forward/pallas_call | solution.py:49
  24.7 1.5 %forward.5 = (bf16[128,512]{1,0:T(8,128)(2,1)S(1)}, bf16[2048,512]{1,0:T(8,128)(2,1)S(1)}, bf16[2048,512]{1,0:T(8,128)(2,1)S(1)}, f32[2,48,1024]{2,1,0:T(8,128)S(1)}) custom-call(bf16[80,512]{1,0:T(8,128)(2,1)S(1)} %collective-permute-done.4.refs_0_, bf16[80,512]{1,0:T(8,128)(2,1)S(1)} %collective-permute-done.5.refs_1_, ...), custom_call_target="tpu_custom_call" | custom-call | flops 2000000000 | bytes 4000000 | tf_op jit(solution)/shard_map/forward/pallas_call | solution.py:49
  26.3 2.8 %middle.1 = (bf16[2048,128]{1,0:T(8,128)(2,1)S(1)}, bf16[2,96,1024]{2,1,0:T(8,128)(2,1)S(1)}, f32[16,128]{1,0:T(8,128)S(1)}) custom-call(f32[2,48,1024]{2,1,0:T(8,128)S(1)} %get-tuple-element.76.refs_0_, f32[2,48,1024]{2,1,0:T(8,128)S(1)} %get-tuple-element.78.refs_1_, f32[2,48,1024]{2,1,0:T(8,128)S(1)} %get-tuple-element.80.refs_2_, ...), custom_call_target="tpu_custom_call" | custom-call | flops 2600000000 | bytes 5200000 | tf_op jit(solution)/shard_map/middle/pallas_call | solution.py:49
  29.1 1.4 %backward.7 = (f32[80,512]{1,0:T(8,128)S(1)}, f32[80,512]{1,0:T(8,128)S(1)}) custom-call(bf16[2048,128]{1,0:T(8,128)(2,1)S(1)} %get-tuple-element.85.refs_0_, bf16[2,96,1024]{2,1,0:T(8,128)(2,1)S(1)} %get-tuple-element.86.refs_1_, bf16[112,1024]{1,0:T(8,128)(2,1)S(1)} %get-tuple-element.87.refs_2_, bf16[112,1024]{1,0:T(8,128)(2,1)S(1)} %get-tuple-element.88.refs_3_, ...), custom_call_target="tpu_custom_call" | custom-call | flops 1400000000 | bytes 2800000 | tf_op jit(solution)/shard_map/backward/pallas_call | solution.py:49
  30.8 1.4 %backward.6 = (f32[80,512]{1,0:T(8,128)S(1)}, f32[80,512]{1,0:T(8,128)S(1)}) custom-call(bf16[2048,128]{1,0:T(8,128)(2,1)S(1)} %get-tuple-element.85.refs_0_, bf16[2,96,1024]{2,1,0:T(8,128)(2,1)S(1)} %get-tuple-element.86.refs_1_, bf16[112,1024]{1,0:T(8,128)(2,1)S(1)} %get-tuple-element.87.refs_2_, bf16[112,1024]{1,0:T(8,128)(2,1)S(1)} %get-tuple-element.88.refs_3_, ...), custom_call_target="tpu_custom_call" | custom-call | flops 1400000000 | bytes 2800000 | tf_op jit(solution)/shard_map/backward/pallas_call | solution.py:49
  32.4 1.4 %backward.5 = (f32[80,512]{1,0:T(8,128)S(1)}, f32[80,512]{1,0:T(8,128)S(1)}) custom-call(bf16[2048,128]{1,0:T(8,128)(2,1)S(1)} %get-tuple-element.85.refs_0_, bf16[2,96,1024]{2,1,0:T(8,128)(2,1)S(1)} %get-tuple-element.86.refs_1_, bf16[112,1024]{1,0:T(8,128)(2,1)S(1)} %get-tuple-element.87.refs_2_, bf16[112,1024]{1,0:T(8,128)(2,1)S(1)} %get-tuple-element.88.refs_3_, ...), custom_call_target="tpu_custom_call" | custom-call | flops 1400000000 | bytes 2800000 | tf_op jit(solution)/shard_map/backward/pallas_call | solution.py:49
  34.2 1.4 %backward.4 = (f32[80,512]{1,0:T(8,128)S(1)}, f32[80,512]{1,0:T(8,128)S(1)}) custom-call(bf16[2048,128]{1,0:T(8,128)(2,1)S(1)} %get-tuple-element.85.refs_0_, bf16[2,96,1024]{2,1,0:T(8,128)(2,1)S(1)} %get-tuple-element.86.refs_1_, bf16[112,1024]{1,0:T(8,128)(2,1)S(1)} %get-tuple-element.87.refs_2_, bf16[112,1024]{1,0:T(8,128)(2,1)S(1)} %get-tuple-element.88.refs_3_, ...), custom_call_target="tpu_custom_call" | custom-call | flops 1400000000 | bytes 2800000 | tf_op jit(solution)/shard_map/backward/pallas_call | solution.py:49
  36.0 1.2 %collective-permute-done.10.refs_4_ = f32[80,512]{1,0:T(8,128)S(1)} collective-permute-done((f32[80,512]{1,0:T(8,128)S(1)}, f32[80,512]{1,0:T(8,128)S(1)}, u32[]{:S(2)}, u32[]{:S(2)}) %collective-permute-start.10) | collective-permute-done | bytes 163872 | tf_op jit(solution)/shard_map/ppermute | solution.py:371
  37.3 1.6 %collective-permute-start.14 = (bf16[80,512]{1,0:T(8,128)(2,1)S(1)}, bf16[80,512]{1,0:T(8,128)(2,1)S(1)}, u32[]{:S(2)}, u32[]{:S(2)}) collective-permute-start(bf16[80,512]{1,0:T(8,128)(2,1)S(1)} %get-tuple-element.111), channel_id=1, source_target_pairs={{0,2},{1,9},{2,0},{3,11},{4,6},{5,13},{6,4},{7,15},{8,10},{9,1},{1... | collective-permute-start | bytes 245768 | tf_op jit(solution)/shard_map/ppermute | solution.py:371
  38.9 1.5 %collective-permute-start.15 = (bf16[80,512]{1,0:T(8,128)(2,1)S(1)}, bf16[80,512]{1,0:T(8,128)(2,1)S(1)}, u32[]{:S(2)}, u32[]{:S(2)}) collective-permute-start(bf16[80,512]{1,0:T(8,128)(2,1)S(1)} %get-tuple-element.112), channel_id=1, source_target_pairs={{0,4},{1,17},{2,6},{3,19},{4,0},{5,21},{6,2},{7,23},{8,12},{9,25},... | collective-permute-start | bytes 245768 | tf_op jit(solution)/shard_map/ppermute | solution.py:371
  40.9 1.0 %collective-permute-done.14.refs_1_ = bf16[80,512]{1,0:T(8,128)(2,1)S(1)} collective-permute-done((bf16[80,512]{1,0:T(8,128)(2,1)S(1)}, bf16[80,512]{1,0:T(8,128)(2,1)S(1)}, u32[]{:S(2)}, u32[]{:S(2)}) %collective-permute-start.14) | collective-permute-done | bytes 81952 | tf_op jit(solution)/shard_map/ppermute | solution.py:371
  41.8 1.5 %collective-permute-done.15.refs_2_ = bf16[80,512]{1,0:T(8,128)(2,1)S(1)} collective-permute-done((bf16[80,512]{1,0:T(8,128)(2,1)S(1)}, bf16[80,512]{1,0:T(8,128)(2,1)S(1)}, u32[]{:S(2)}, u32[]{:S(2)}) %collective-permute-start.15) | collective-permute-done | bytes 81952 | tf_op jit(solution)/shard_map/ppermute | solution.py:371
  43.3 2.4 %collective-permute-done.16.refs_3_ = bf16[80,512]{1,0:T(8,128)(2,1)S(1)} collective-permute-done((bf16[80,512]{1,0:T(8,128)(2,1)S(1)}, bf16[80,512]{1,0:T(8,128)(2,1)S(1)}, u32[]{:S(2)}, u32[]{:S(2)}) %collective-permute-start.16) | collective-permute-done | bytes 81952 | tf_op jit(solution)/shard_map/ppermute | solution.py:371
  45.8 2.2 %collective-permute-start.19 = (bf16[80,512]{1,0:T(8,128)(2,1)S(1)}, bf16[80,512]{1,0:T(8,128)(2,1)S(1)}, u32[]{:S(2)}, u32[]{:S(2)}) collective-permute-start(bf16[80,512]{1,0:T(8,128)(2,1)S(1)} %add_piece.1.refs_0_), channel_id=1, source_target_pairs={{0,24},{1,7},{2,26},{3,5},{4,28},{5,3},{6,30},{7,1},{8,16},{9,15},... | collective-permute-start | bytes 245768 | tf_op jit(solution)/shard_map/ppermute | solution.py:371
  48.0 2.3 %collective-permute-start.17 = (bf16[80,512]{1,0:T(8,128)(2,1)S(1)}, bf16[80,512]{1,0:T(8,128)(2,1)S(1)}, u32[]{:S(2)}, u32[]{:S(2)}) collective-permute-start(bf16[80,512]{1,0:T(8,128)(2,1)S(1)} %add_piece.1.refs_0_), channel_id=1, source_target_pairs={{0,8},{1,3},{2,10},{3,1},{4,12},{5,7},{6,14},{7,5},{8,0},{9,11},{1... | collective-permute-start | bytes 245768 | tf_op jit(solution)/shard_map/ppermute | solution.py:371
  50.3 1.9 %collective-permute-done.19.refs_3_ = bf16[80,512]{1,0:T(8,128)(2,1)S(1)} collective-permute-done((bf16[80,512]{1,0:T(8,128)(2,1)S(1)}, bf16[80,512]{1,0:T(8,128)(2,1)S(1)}, u32[]{:S(2)}, u32[]{:S(2)}) %collective-permute-start.19) | collective-permute-done | bytes 81952 | tf_op jit(solution)/shard_map/ppermute | solution.py:371
  52.1 2.3 %collective-permute-done.18.refs_2_ = bf16[80,512]{1,0:T(8,128)(2,1)S(1)} collective-permute-done((bf16[80,512]{1,0:T(8,128)(2,1)S(1)}, bf16[80,512]{1,0:T(8,128)(2,1)S(1)}, u32[]{:S(2)}, u32[]{:S(2)}) %collective-permute-start.18) | collective-permute-done | bytes 81952 | tf_op jit(solution)/shard_map/ppermute | solution.py:371
  54.7 1.5 %collective-permute-start.21 = (bf16[80,512]{1,0:T(8,128)(2,1)S(1)}, bf16[80,512]{1,0:T(8,128)(2,1)S(1)}, u32[]{:S(2)}, u32[]{:S(2)}) collective-permute-start(bf16[80,512]{1,0:T(8,128)(2,1)S(1)} %add_line.1.refs_0_), channel_id=1, source_target_pairs={{0,4},{1,17},{2,6},{3,19},{4,0},{5,21},{6,2},{7,23},{8,12},{9,25},... | collective-permute-start | bytes 245768 | tf_op jit(solution)/shard_map/ppermute | solution.py:371
  56.2 1.9 %collective-permute-start.20 = (bf16[80,512]{1,0:T(8,128)(2,1)S(1)}, bf16[80,512]{1,0:T(8,128)(2,1)S(1)}, u32[]{:S(2)}, u32[]{:S(2)}) collective-permute-start(bf16[80,512]{1,0:T(8,128)(2,1)S(1)} %add_line.1.refs_0_), channel_id=1, source_target_pairs={{0,2},{1,9},{2,0},{3,11},{4,6},{5,13},{6,4},{7,15},{8,10},{9,1},{1... | collective-permute-start | bytes 245768 | tf_op jit(solution)/shard_map/ppermute | solution.py:371
  58.1 1.9 %collective-permute-done.22.refs_3_ = bf16[80,512]{1,0:T(8,128)(2,1)S(1)} collective-permute-done((bf16[80,512]{1,0:T(8,128)(2,1)S(1)}, bf16[80,512]{1,0:T(8,128)(2,1)S(1)}, u32[]{:S(2)}, u32[]{:S(2)}) %collective-permute-start.22) | collective-permute-done | bytes 81952 | tf_op jit(solution)/shard_map/ppermute | solution.py:371
  60.7 0.6 collective-permute-done.26.refs_7_
  62.1 2.5 %update.1 = (f32[1,1]{1,0:T(1,128)}, f32[1,1]{1,0:T(1,128)}, f32[1,1]{1,0:T(1,128)}, f32[64,100]{1,0:T(8,128)}, f32[47,64]{1,0:T(8,128)}, /*index=5*/f32[64,100]...) custom-call(bf16[80,512]{1,0:T(8,128)(2,1)S(1)} %add_line.1.refs_0_,, ...), custom_call_target="tpu_custom_call" | custom-call | flops 2500000000 | bytes 5000000 | tf_op jit(solution)/shard_map/update/pallas_call | solution.py:49
  (81 shorter events, 5.6 us)
Async XLA Ops:
  2.4 8.4 %collective-permute-start.2 = (bf16[80,128]{1,0:T(8,128)(2,1)}, bf16[80,128]{1,0:T(8,128)(2,1)S(1)}, u32[]{:S(2)}, u32[]{:S(2)}) collective-permute-start(bf16[80,128]{1,0:T(8,128)(2,1)} %pack.1), channel_id=1, source_target_pairs={{0,24},{1,25},{2,26},{3,27},{4,28},{5,29},{6,30},{7,31},{8,16},{9,... | collective-permute-start | bytes 61448 | tf_op jit(solution)/shard_map/ppermute | solution.py:371
  7.5 4.9 %collective-permute-start.1 = (bf16[80,128]{1,0:T(8,128)(2,1)}, bf16[80,128]{1,0:T(8,128)(2,1)S(1)}, u32[]{:S(2)}, u32[]{:S(2)}) collective-permute-start(bf16[80,128]{1,0:T(8,128)(2,1)} %pack.1), channel_id=1, source_target_pairs={{0,16},{1,17},{2,18},{3,19},{4,20},{5,21},{6,22},{7,23},{8,24},{9,... | collective-permute-start | bytes 61448 | tf_op jit(solution)/shard_map/ppermute | solution.py:371
  7.5 4.9 %collective-permute-start = (bf16[80,128]{1,0:T(8,128)(2,1)}, bf16[80,128]{1,0:T(8,128)(2,1)S(1)}, u32[]{:S(2)}, u32[]{:S(2)}) collective-permute-start(bf16[80,128]{1,0:T(8,128)(2,1)} %pack.1), channel_id=1, source_target_pairs={{0,8},{1,9},{2,10},{3,11},{4,12},{5,13},{6,14},{7,15},{8,0},{9,1},... | collective-permute-start | bytes 61448 | tf_op jit(solution)/shard_map/ppermute | solution.py:371
  12.4 7.7 %collective-permute-start.8 = (bf16[80,512]{1,0:T(8,128)(2,1)S(1)}, bf16[80,512]{1,0:T(8,128)(2,1)S(1)}, u32[]{:S(2)}, u32[]{:S(2)}) collective-permute-start(bf16[80,512]{1,0:T(8,128)(2,1)S(1)} %pad_maximum_fusion.refs_2_.refs_0_), channel_id=1, source_target_pairs={{0,6},{1,7},{2,4},{3,5},{4,2},{5,3},{6,0},{7,1},{8,14},{9,15},{10,... | collective-permute-start | bytes 245768 | tf_op jit(solution)/shard_map/ppermute | solution.py:371
  14.9 5.8 %collective-permute-start.6 = (bf16[80,512]{1,0:T(8,128)(2,1)S(1)}, bf16[80,512]{1,0:T(8,128)(2,1)S(1)}, u32[]{:S(2)}, u32[]{:S(2)}) collective-permute-start(bf16[80,512]{1,0:T(8,128)(2,1)S(1)} %pad_maximum_fusion.refs_2_.refs_0_), channel_id=1, source_target_pairs={{0,4},{1,5},{2,6},{3,7},{4,0},{5,1},{6,2},{7,3},{8,12},{9,13},{10,... | collective-permute-start | bytes 245768 | tf_op jit(solution)/shard_map/ppermute | solution.py:371
  15.4 5.3 %collective-permute-start.4 = (bf16[80,512]{1,0:T(8,128)(2,1)S(1)}, bf16[80,512]{1,0:T(8,128)(2,1)S(1)}, u32[]{:S(2)}, u32[]{:S(2)}) collective-permute-start(bf16[80,512]{1,0:T(8,128)(2,1)S(1)} %pad_maximum_fusion.refs_2_.refs_0_), channel_id=1, source_target_pairs={{0,2},{1,3},{2,0},{3,1},{4,6},{5,7},{6,4},{7,5},{8,10},{9,11},{10,... | collective-permute-start | bytes 245768 | tf_op jit(solution)/shard_map/ppermute | solution.py:371
  15.9 2.6 %collective-permute-start.3 = (bf16[80,512]{1,0:T(8,128)(2,1)S(1)}, bf16[80,512]{1,0:T(8,128)(2,1)S(1)}, u32[]{:S(2)}, u32[]{:S(2)}) collective-permute-start(bf16[80,512]{1,0:T(8,128)(2,1)S(1)} %pad_maximum_fusion.refs_2_.refs_0_), channel_id=1, source_target_pairs={{0,1},{1,0},{2,3},{3,2},{4,5},{5,4},{6,7},{7,6},{8,9},{9,8},{10,11... | collective-permute-start | bytes 245768 | tf_op jit(solution)/shard_map/ppermute | solution.py:371
  20.1 1.5 %collective-permute-start.9 = (bf16[80,512]{1,0:T(8,128)(2,1)S(1)}, bf16[80,512]{1,0:T(8,128)(2,1)S(1)}, u32[]{:S(2)}, u32[]{:S(2)}) collective-permute-start(bf16[80,512]{1,0:T(8,128)(2,1)S(1)} %collective-permute-done.8.refs_0_), channel_id=1, source_target_pairs={{0,1},{1,0},{2,3},{3,2},{4,5},{5,4},{6,7},{7,6},{8,9},{9,8},{10,11... | collective-permute-start | bytes 245768 | tf_op jit(solution)/shard_map/ppermute | solution.py:371
  20.7 4.0 %collective-permute-start.5 = (bf16[80,512]{1,0:T(8,128)(2,1)S(1)}, bf16[80,512]{1,0:T(8,128)(2,1)S(1)}, u32[]{:S(2)}, u32[]{:S(2)}) collective-permute-start(bf16[80,512]{1,0:T(8,128)(2,1)S(1)} %collective-permute-done.4.refs_0_), channel_id=1, source_target_pairs={{0,1},{1,0},{2,3},{3,2},{4,5},{5,4},{6,7},{7,6},{8,9},{9,8},{10,11... | collective-permute-start | bytes 245768 | tf_op jit(solution)/shard_map/ppermute | solution.py:371
  20.8 2.4 %collective-permute-start.7 = (bf16[80,512]{1,0:T(8,128)(2,1)S(1)}, bf16[80,512]{1,0:T(8,128)(2,1)S(1)}, u32[]{:S(2)}, u32[]{:S(2)}) collective-permute-start(bf16[80,512]{1,0:T(8,128)(2,1)S(1)} %collective-permute-done.6.refs_0_), channel_id=1, source_target_pairs={{0,1},{1,0},{2,3},{3,2},{4,5},{5,4},{6,7},{7,6},{8,9},{9,8},{10,11... | collective-permute-start | bytes 245768 | tf_op jit(solution)/shard_map/ppermute | solution.py:371
  30.4 5.6 %collective-permute-start.13 = (f32[80,512]{1,0:T(8,128)S(1)}, f32[80,512]{1,0:T(8,128)S(1)}, u32[]{:S(2)}, u32[]{:S(2)}) collective-permute-start(f32[80,512]{1,0:T(8,128)S(1)} %get-tuple-element.109), channel_id=1, source_target_pairs={{0,1},{1,0},{2,3},{3,2},{4,5},{5,4},{6,7},{7,6},{8,9},{9,8},{10,11... | collective-permute-start | bytes 491528 | tf_op jit(solution)/shard_map/ppermute | solution.py:371
  32.2 3.8 %collective-permute-start.12 = (f32[80,512]{1,0:T(8,128)S(1)}, f32[80,512]{1,0:T(8,128)S(1)}, u32[]{:S(2)}, u32[]{:S(2)}) collective-permute-start(f32[80,512]{1,0:T(8,128)S(1)} %get-tuple-element.108), channel_id=1, source_target_pairs={{0,1},{1,0},{2,3},{3,2},{4,5},{5,4},{6,7},{7,6},{8,9},{9,8},{10,11... | collective-permute-start | bytes 491528 | tf_op jit(solution)/shard_map/ppermute | solution.py:371
  33.8 2.2 %collective-permute-start.11 = (f32[80,512]{1,0:T(8,128)S(1)}, f32[80,512]{1,0:T(8,128)S(1)}, u32[]{:S(2)}, u32[]{:S(2)}) collective-permute-start(f32[80,512]{1,0:T(8,128)S(1)} %get-tuple-element.107), channel_id=1, source_target_pairs={{0,1},{1,0},{2,3},{3,2},{4,5},{5,4},{6,7},{7,6},{8,9},{9,8},{10,11... | collective-permute-start | bytes 491528 | tf_op jit(solution)/shard_map/ppermute | solution.py:371
  35.6 26.4 %copy-start = (f32[2048,64]{0,1:T(8,128)S(1)}, f32[2048,64]{0,1:T(8,128)}, u32[]{:S(2)}) copy-start(f32[2048,64]{0,1:T(8,128)} %param.29) | copy-start | bytes 1572868
  35.6 26.4 %copy-start.1 = (f32[64,2048]{1,0:T(8,128)S(1)}, f32[64,2048]{1,0:T(8,128)}, u32[]{:S(2)}) copy-start(f32[64,2048]{1,0:T(8,128)} %refs_14_.1) | copy-start | bytes 1572868
  35.6 26.3 %copy-start.2 = (f32[2048,64]{0,1:T(8,128)S(1)}, f32[2048,64]{0,1:T(8,128)}, u32[]{:S(2)}) copy-start(f32[2048,64]{0,1:T(8,128)} %param.33) | copy-start | bytes 1572868
  35.6 26.3 %copy-start.3 = (f32[64,2048]{1,0:T(8,128)S(1)}, f32[64,2048]{1,0:T(8,128)}, u32[]{:S(2)}) copy-start(f32[64,2048]{1,0:T(8,128)} %refs_18_.1) | copy-start | bytes 1572868
  35.6 26.3 %copy-start.6 = (f32[100,100]{1,0:T(8,128)S(1)}, f32[100,100]{1,0:T(8,128)}, u32[]{:S(2)}) copy-start(f32[100,100]{1,0:T(8,128)} %refs_12_.1) | copy-start | bytes 120004
  35.8 1.5 %collective-permute-start.10 = (f32[80,512]{1,0:T(8,128)S(1)}, f32[80,512]{1,0:T(8,128)S(1)}, u32[]{:S(2)}, u32[]{:S(2)}) collective-permute-start(f32[80,512]{1,0:T(8,128)S(1)} %get-tuple-element.106), channel_id=1, source_target_pairs={{0,1},{1,0},{2,3},{3,2},{4,5},{5,4},{6,7},{7,6},{8,9},{9,8},{10,11... | collective-permute-start | bytes 491528 | tf_op jit(solution)/shard_map/ppermute | solution.py:371
  37.3 4.5 %collective-permute-start.14 = (bf16[80,512]{1,0:T(8,128)(2,1)S(1)}, bf16[80,512]{1,0:T(8,128)(2,1)S(1)}, u32[]{:S(2)}, u32[]{:S(2)}) collective-permute-start(bf16[80,512]{1,0:T(8,128)(2,1)S(1)} %get-tuple-element.111), channel_id=1, source_target_pairs={{0,2},{1,9},{2,0},{3,11},{4,6},{5,13},{6,4},{7,15},{8,10},{9,1},{1... | collective-permute-start | bytes 245768 | tf_op jit(solution)/shard_map/ppermute | solution.py:371
  38.9 4.4 %collective-permute-start.15 = (bf16[80,512]{1,0:T(8,128)(2,1)S(1)}, bf16[80,512]{1,0:T(8,128)(2,1)S(1)}, u32[]{:S(2)}, u32[]{:S(2)}) collective-permute-start(bf16[80,512]{1,0:T(8,128)(2,1)S(1)} %get-tuple-element.112), channel_id=1, source_target_pairs={{0,4},{1,17},{2,6},{3,19},{4,0},{5,21},{6,2},{7,23},{8,12},{9,25},... | collective-permute-start | bytes 245768 | tf_op jit(solution)/shard_map/ppermute | solution.py:371
  40.4 5.3 %collective-permute-start.16 = (bf16[80,512]{1,0:T(8,128)(2,1)S(1)}, bf16[80,512]{1,0:T(8,128)(2,1)S(1)}, u32[]{:S(2)}, u32[]{:S(2)}) collective-permute-start(bf16[80,512]{1,0:T(8,128)(2,1)S(1)} %get-tuple-element.113), channel_id=1, source_target_pairs={{0,6},{1,25},{2,4},{3,27},{4,2},{5,29},{6,0},{7,31},{8,14},{9,17},... | collective-permute-start | bytes 245768 | tf_op jit(solution)/shard_map/ppermute | solution.py:371
  45.8 6.3 %collective-permute-start.19 = (bf16[80,512]{1,0:T(8,128)(2,1)S(1)}, bf16[80,512]{1,0:T(8,128)(2,1)S(1)}, u32[]{:S(2)}, u32[]{:S(2)}) collective-permute-start(bf16[80,512]{1,0:T(8,128)(2,1)S(1)} %add_piece.1.refs_0_), channel_id=1, source_target_pairs={{0,24},{1,7},{2,26},{3,5},{4,28},{5,3},{6,30},{7,1},{8,16},{9,15},... | collective-permute-start | bytes 245768 | tf_op jit(solution)/shard_map/ppermute | solution.py:371
  48.0 6.5 %collective-permute-start.18 = (bf16[80,512]{1,0:T(8,128)(2,1)S(1)}, bf16[80,512]{1,0:T(8,128)(2,1)S(1)}, u32[]{:S(2)}, u32[]{:S(2)}) collective-permute-start(bf16[80,512]{1,0:T(8,128)(2,1)S(1)} %add_piece.1.refs_0_), channel_id=1, source_target_pairs={{0,16},{1,5},{2,18},{3,7},{4,20},{5,1},{6,22},{7,3},{8,24},{9,13},... | collective-permute-start | bytes 245768 | tf_op jit(solution)/shard_map/ppermute | solution.py:371
  48.0 6.5 %collective-permute-start.17 = (bf16[80,512]{1,0:T(8,128)(2,1)S(1)}, bf16[80,512]{1,0:T(8,128)(2,1)S(1)}, u32[]{:S(2)}, u32[]{:S(2)}) collective-permute-start(bf16[80,512]{1,0:T(8,128)(2,1)S(1)} %add_piece.1.refs_0_), channel_id=1, source_target_pairs={{0,8},{1,3},{2,10},{3,1},{4,12},{5,7},{6,14},{7,5},{8,0},{9,11},{1... | collective-permute-start | bytes 245768 | tf_op jit(solution)/shard_map/ppermute | solution.py:371
  54.5 5.5 %collective-permute-start.22 = (bf16[80,512]{1,0:T(8,128)(2,1)S(1)}, bf16[80,512]{1,0:T(8,128)(2,1)S(1)}, u32[]{:S(2)}, u32[]{:S(2)}) collective-permute-start(bf16[80,512]{1,0:T(8,128)(2,1)S(1)} %add_line.1.refs_0_), channel_id=1, source_target_pairs={{0,6},{1,25},{2,4},{3,27},{4,2},{5,29},{6,0},{7,31},{8,14},{9,17},... | collective-permute-start | bytes 245768 | tf_op jit(solution)/shard_map/ppermute | solution.py:371
  54.7 5.3 %collective-permute-start.21 = (bf16[80,512]{1,0:T(8,128)(2,1)S(1)}, bf16[80,512]{1,0:T(8,128)(2,1)S(1)}, u32[]{:S(2)}, u32[]{:S(2)}) collective-permute-start(bf16[80,512]{1,0:T(8,128)(2,1)S(1)} %add_line.1.refs_0_), channel_id=1, source_target_pairs={{0,4},{1,17},{2,6},{3,19},{4,0},{5,21},{6,2},{7,23},{8,12},{9,25},... | collective-permute-start | bytes 245768 | tf_op jit(solution)/shard_map/ppermute | solution.py:371
  56.2 4.4 %collective-permute-start.20 = (bf16[80,512]{1,0:T(8,128)(2,1)S(1)}, bf16[80,512]{1,0:T(8,128)(2,1)S(1)}, u32[]{:S(2)}, u32[]{:S(2)}) collective-permute-start(bf16[80,512]{1,0:T(8,128)(2,1)S(1)} %add_line.1.refs_0_), channel_id=1, source_target_pairs={{0,2},{1,9},{2,0},{3,11},{4,6},{5,13},{6,4},{7,15},{8,10},{9,1},{1... | collective-permute-start | bytes 245768 | tf_op jit(solution)/shard_map/ppermute | solution.py:371
  58.1 2.6 %collective-permute-start.23 = (bf16[80,512]{1,0:T(8,128)(2,1)S(1)}, bf16[80,512]{1,0:T(8,128)(2,1)S(1)}, u32[]{:S(2)}, u32[]{:S(2)}) collective-permute-start(bf16[80,512]{1,0:T(8,128)(2,1)S(1)} %add_line.1.refs_0_), channel_id=1, source_target_pairs={{0,1},{1,0},{2,3},{3,2},{4,5},{5,4},{6,7},{7,6},{8,9},{9,8},{10,11... | collective-permute-start | bytes 245768 | tf_op jit(solution)/shard_map/ppermute | solution.py:371
  60.0 1.3 %collective-permute-start.26 = (bf16[80,512]{1,0:T(8,128)(2,1)S(1)}, bf16[80,512]{1,0:T(8,128)(2,1)S(1)}, u32[]{:S(2)}, u32[]{:S(2)}) collective-permute-start(bf16[80,512]{1,0:T(8,128)(2,1)S(1)} %collective-permute-done.22.refs_3_), channel_id=1, source_target_pairs={{0,1},{1,0},{2,3},{3,2},{4,5},{5,4},{6,7},{7,6},{8,9},{9,8},{10,11... | collective-permute-start | bytes 245768 | tf_op jit(solution)/shard_map/ppermute | solution.py:371
  60.0 1.4 %collective-permute-start.25 = (bf16[80,512]{1,0:T(8,128)(2,1)S(1)}, bf16[80,512]{1,0:T(8,128)(2,1)S(1)}, u32[]{:S(2)}, u32[]{:S(2)}) collective-permute-start(bf16[80,512]{1,0:T(8,128)(2,1)S(1)} %collective-permute-done.21.refs_2_), channel_id=1, source_target_pairs={{0,1},{1,0},{2,3},{3,2},{4,5},{5,4},{6,7},{7,6},{8,9},{9,8},{10,11... | collective-permute-start | bytes 245768 | tf_op jit(solution)/shard_map/ppermute | solution.py:371
  60.7 1.3 %collective-permute-start.24 = (bf16[80,512]{1,0:T(8,128)(2,1)S(1)}, bf16[80,512]{1,0:T(8,128)(2,1)S(1)}, u32[]{:S(2)}, u32[]{:S(2)}) collective-permute-start(bf16[80,512]{1,0:T(8,128)(2,1)S(1)} %collective-permute-done.20.refs_1_), channel_id=1, source_target_pairs={{0,1},{1,0},{2,3},{3,2},{4,5},{5,4},{6,7},{7,6},{8,9},{9,8},{10,11... | collective-permute-start | bytes 245768 | tf_op jit(solution)/shard_map/ppermute | solution.py:371
  (16 other events, 287.2 us)

commit v3 on v2

--- a/solution.py
+++ b/solution.py
@@ -129,19 +129,21 @@
     p_ref[...] = pooled.T.astype(bf16)
 
 
-def forward_kernel(nblk, *refs):
-    own_ref, other_ref = refs[0:2]
-    p_refs = refs[2 : 2 + nblk]
-    ww, hid, der, zt, w = refs[2 + nblk :]
+def forward_kernel(nblk, count, *refs):
+    own_refs, other_refs = refs[0:count], refs[count : 2 * count]
+    p_refs = refs[2 * count : 2 * count + nblk]
+    ww, hid, der, zt, w = refs[2 * count + nblk :]
     group = w.shape[1]
+    each = group // LANES // count
     first = lax.axis_index("shard") == 0
 
     left = lax.broadcasted_iota(jnp.int32, (HALF, LANES), 1) < LANES // 2
     row = lax.broadcasted_iota(jnp.int32, (HALF, LANES), 0)
     for s in range(group // LANES):
         at = slice(s * LANES, (s + 1) * LANES)
-        mine = own_ref[:, at].astype(f32)
-        theirs = other_ref[:, at].astype(f32)
+        part = slice(s % each * LANES, (s % each + 1) * LANES)
+        mine = own_refs[s // each][:, part].astype(f32)
+        theirs = other_refs[s // each][:, part].astype(f32)
         lo = jnp.where(first, mine, theirs)
         hi = jnp.where(first, theirs, mine)
         upper = jnp.where(left, lo, pltpu.roll(hi, LANES // 2, 1))
@@ -171,22 +173,22 @@
             zt[b] = part if n == 0 else zt[b] + part
 
 
-def middle_kernel(nblk, classes, degree, *refs):
-    z_refs = refs[0:4]
-    m_refs = refs[4 : 4 + nblk]
-    mask_ref, label_ref, b2_ref = refs[4 + nblk : 7 + nblk]
-    qq, qqt, scal_ref, row_scr = refs[7 + nblk :]
+def middle_kernel(nblk, shares, classes, degree, *refs):
+    z_refs, refs = refs[0:shares], refs[shares:]
+    m_refs, refs = refs[0:nblk], refs[nblk:]
+    mask_ref, label_ref, b2_ref, qq, qqt, scal_ref, row_scr = refs
     first = lax.axis_index("shard") == 0
     scale_in = 1.0 / (degree + 1)
     pick = lax.broadcasted_iota(jnp.int32, (48, classes), 0) == lax.broadcasted_iota(
         jnp.int32, (48, classes), 1
     )
     bias = jnp.sum(jnp.where(pick, b2_ref[...], 0.0), axis=1, keepdims=True)
+    lane = lax.broadcasted_iota(jnp.int32, (BLOCK, LANES), 1)
     row_scr[...] = jnp.zeros_like(row_scr)
     loss = jnp.zeros((1, 1), f32)
     count = jnp.zeros((1, 1), f32)
     for b in range(nblk):
-        zb = (z_refs[0][b] + z_refs[1][b]) + (z_refs[2][b] + z_refs[3][b])
+        zb = sum([z[b] for z in z_refs[1:]], z_refs[0][b])
         z_hi = zb.astype(bf16)
         z_lo = (zb - z_hi.astype(f32)).astype(bf16)
         both = mm(jnp.concatenate([z_hi, z_lo], axis=0), m_refs[b][...])
@@ -204,12 +206,12 @@
         count += jnp.sum(weight, axis=1, keepdims=True)
         grad = ((e / total - hit.astype(f32)) * weight).astype(bf16)
         row_scr[:, 0:48] += mm(jnp.ones((8, BLOCK), bf16), grad, NT)
-        q = mm(grad, m_refs[b][...], NT) * scale_in
-        q_hi = q.astype(bf16)
-        q_lo = q - q_hi.astype(f32)
-        q2 = jnp.concatenate([q_hi.astype(f32), q_lo, jnp.zeros((32, BLOCK), f32)], axis=0)
-        qqt[b] = q2[0:96].astype(bf16)
-        qq[b * BLOCK : (b + 1) * BLOCK, :] = (0.5 * q2).T.astype(bf16)
+        grad_t = jnp.concatenate([grad.astype(f32), jnp.zeros((80, BLOCK), f32)], axis=0).T
+        q = mm(m_refs[b][...], grad_t.astype(bf16)) * scale_in
+        q_hi = q.astype(bf16).astype(f32)
+        q2 = jnp.where(lane < 48, q_hi, pltpu.roll(q - q_hi, 48, 1))
+        qq[b * BLOCK : (b + 1) * BLOCK, :] = (0.5 * q2).astype(bf16)
+        qqt[b] = q2.T[0:96].astype(bf16)
 
     vec = row_scr[0:1, :]
     pos = lax.broadcasted_iota(jnp.int32, vec.shape, 1)
@@ -225,43 +227,80 @@
     )
 
 
-def backward_kernel(nblk, has_scalars, *refs):
+ORDER = (3, 1, 2)
+PASSES = tuple(
+    tuple((k, u) for k in range(4) for u in range(4) if (k in ORDER[:2] or u in ORDER[:2]) == early)
+    for early in (True, False)
+)
+PIECES = (ORDER[:2], (0, ORDER[2]))
+
+
+def lanes_of(first_ref, rest_ref, slots, rows=slice(None)):
+    parts = []
+    for k, u in slots:
+        ref, n = (first_ref, u) if k == 0 else (rest_ref, (k - 1) * 4 + u)
+        parts.append(ref[rows, n * LANES : (n + 1) * LANES])
+    return jnp.concatenate(parts, axis=1)
+
+
+def backward_kernel(nblk, slots, *refs):
     qq, qqt = refs[0:2]
     pt_refs = refs[2 : 2 + nblk]
-    ww, hid, der, scal_ref = refs[2 + nblk : 6 + nblk]
-    keep_ref, send_ref = refs[6 + nblk :]
+    ww0, hid0, der0, ww1, hid1, der1, scal_ref = refs[2 + nblk : 9 + nblk]
+    keep_ref, send_ref = refs[9 + nblk :]
     first = lax.axis_index("shard") == 0
-    group = ww.shape[1]
-    d1 = jnp.zeros((TOP, group), f32)
-    d2 = jnp.zeros((96, group), f32)
-    for b in range(nblk):
-        to = slice(b * BLOCK, (b + 1) * BLOCK)
-        gp = (mm(qq[to, :], ww[...]) * der[to, :].astype(f32)).astype(bf16)
-        d1 = d1 + mm(pt_refs[b][...], gp)
-        d2 = d2 + mm(qqt[b], hid[to, :])
-    d2 = d2[0:48] + d2[48:96]
-    upper = d1[0:HALF]
-    middle = d1[96:TOP]
-    if has_scalars:
-        middle += jnp.concatenate([scal_ref[...], jnp.zeros((16, group - LANES), f32)], axis=1)
-    lower = jnp.concatenate([d1[HALF:96], middle, d2], axis=0)
-    keep_ref[...] = jnp.where(first, upper, lower)
-    send_ref[...] = jnp.where(first, lower, upper)
-
-
-def add_core_kernel(*refs):
-    keeps, gots, outs = refs[0:4], refs[4:8], refs[8:12]
+    for n in range(0, len(slots), 4):
+        some = slots[n : n + 4]
+        wide = len(some) * LANES
+        d1 = jnp.zeros((TOP, wide), f32)
+        d2 = jnp.zeros((96, wide), f32)
+        weights = lanes_of(ww0, ww1, some)
+        for b in range(nblk):
+            to = slice(b * BLOCK, (b + 1) * BLOCK)
+            slope = lanes_of(der0, der1, some, to).astype(f32)
+            gp = (mm(qq[to, :], weights) * slope).astype(bf16)
+            d1 = d1 + mm(pt_refs[b][...], gp)
+            d2 = d2 + mm(qqt[b], lanes_of(hid0, hid1, some, to))
+        d2 = d2[0:48] + d2[48:96]
+        upper = d1[0:HALF]
+        middle = d1[96:TOP]
+        if some[0] == (0, 0):
+            middle += jnp.concatenate([scal_ref[...], jnp.zeros((16, wide - LANES), f32)], axis=1)
+        lower = jnp.concatenate([d1[HALF:96], middle, d2], axis=0)
+        at = slice(n * LANES, n * LANES + wide)
+        keep_ref[:, at] = jnp.where(first, upper, lower)
+        send_ref[:, at] = jnp.where(first, lower, upper)
+
+
+def turn_kernel(nblk, count, shares, classes, degree, slots, *refs):
+    ins, refs = refs[: 2 * count], refs[2 * count :]
+    p_refs, refs = refs[:nblk], refs[nblk:]
+    pt_refs, refs = refs[:nblk], refs[nblk:]
+    early, refs = refs[:4], refs[4:]
+    labels, refs = refs[: nblk + 3], refs[nblk + 3 :]
+    ww, hid, der, qq, qqt, scal, keep, send, w, zt, row_scr = refs
+    forward_kernel(nblk, count, *ins, *p_refs, ww, hid, der, zt, w)
+    middle_kernel(nblk, 2, classes, degree, early[3], zt, *labels, qq, qqt, scal, row_scr)
+    backward_kernel(
+        nblk, slots, qq, qqt, *pt_refs, *early[0:3], ww, hid, der, scal, keep, send
+    )
+
+
+def add_core_kernel(pieces, passes, *refs):
+    keeps, gots, outs = refs[0:passes], refs[passes : 2 * passes], refs[2 * passes :]
     first = lax.axis_index("shard") == 0
-    total = [
-        [
-            keep[:, u * LANES : (u + 1) * LANES] + got[:, u * LANES : (u + 1) * LANES]
-            for u in range(4)
-        ]
-        for keep, got in zip(keeps, gots, strict=True)
-    ]
-    for k, out in enumerate(outs):
+
+    def total(slot):
+        for p in range(passes):
+            if slot in PASSES[p]:
+                n = PASSES[p].index(slot)
+                at = slice(n * LANES, (n + 1) * LANES)
+                return keeps[p][:, at] + gots[p][:, at]
+        raise KeyError(slot)
+
+    for k, out in zip(pieces, outs, strict=True):
         for u in range(4):
-            picked = jnp.where(first, total[k][u], total[u][k])
+            picked = jnp.where(first, total((k, u)), total((u, k)))
             out[:, u * LANES : (u + 1) * LANES] = picked.astype(out.dtype)
 
 
@@ -315,7 +354,11 @@
     inv = 1.0 / jnp.maximum(count, 1.0)
     gb2 = jnp.where(pos < classes, vec, 0.0) * inv
     whole = g[...]
-    gram = mm(whole, whole, NT)
+    stacked = jnp.concatenate(
+        [whole, r1t_root[...].astype(bf16), l2_root[...].astype(bf16)], axis=0
+    )
+    products = mm(stacked, whole, NT)
+    gram = products[0:ROWS]
     gi = lax.broadcasted_iota(jnp.int32, gram.shape, 0)
     gj = lax.broadcasted_iota(jnp.int32, gram.shape, 1)
     squares = jnp.sum(jnp.where(gi == gj, gram, 0.0), axis=0, keepdims=True)
@@ -329,8 +372,8 @@
     count_o[...] = count
     norm_o[...] = norm
     l1_o[...] = beta_stat * l1[...] + ss * gram[0:fan_in, 0:fan_in]
-    g2t = g[TOP:ROWS, :]
-    r2_o[...] = beta_stat * r2[...] + ss * mm(g2t, g2t, NT)[0:classes, 0:classes]
+    gram2 = gram[TOP : TOP + classes, TOP : TOP + classes]
+    r2_o[...] = beta_stat * r2[...] + ss * gram2
 
     mine = g[:, pl.ds(pl.multiple_of(chip * LANES, LANES), LANES)].astype(f32)
     mine = jnp.where(first, mine, pltpu.roll(mine, half, 1))[:, 0:half]
@@ -340,19 +383,19 @@
         == lax.broadcasted_iota(jnp.int32, (half, half), 1)
     ).astype(bf16)
     mine_t = mm(eye, mine_b, NT)
-    own1_t = mine_t[:, 0:TOP].astype(bf16)
     grad1_o[...] = s * mine_t[:, 0:fan_in]
     grad2_o[...] = s * mine[TOP : TOP + classes, :]
-    own2 = mm(eye, mine_b[TOP:ROWS], NT).astype(bf16)
-    g1 = g[0:TOP, :]
-    zero_bias = lax.broadcasted_iota(jnp.int32, own1_t.shape, 1) < fan_in
-    own1_t = jnp.where(zero_bias, own1_t.astype(f32), 0.0).astype(bf16)
-    r1_o[...] = beta_stat * r1t[...] + ss * mm(own1_t, g1)
-    l2_o[...] = beta_stat * l2[...] + ss * mm(own2, g2t)
-    t1 = mm(r1t_root[...].astype(bf16), g1, NT)[:, 0:fan_in]
+    at = lax.broadcasted_iota(jnp.int32, mine_t.shape, 1)
+    owns = jnp.concatenate(
+        [jnp.where(at < fan_in, mine_t, 0.0), jnp.where(at >= TOP, mine_t, 0.0)], axis=0
+    )
+    stats = mm(owns.astype(bf16), whole)
+    r1_o[...] = beta_stat * r1t[...] + ss * stats[0:half]
+    l2_o[...] = beta_stat * l2[...] + ss * stats[half:LANES]
+    t1 = products[ROWS : ROWS + half, 0:fan_in]
     t1 = lax.dot_general(t1, l1_root[...], NT, precision=highest, preferred_element_type=f32)
     w1_o[...] = w1t[...] - (rate_first * s) * t1
-    t2 = mm(l2_root[...].astype(bf16), g2t, NT)[:, 0:classes]
+    t2 = products[ROWS + half : ROWS + LANES, TOP : TOP + classes]
     t2 = lax.dot_general(
         r2_root[...], t2, (((0,), (1,)), ((), ())), precision=highest, preferred_element_type=f32
     )
@@ -363,6 +406,10 @@
     m2_o[...], v2_o[...], b2_o[...] = adam_step(
         b2[...], factor * gb2[:, 0:classes], m2[...], v2[...]
     )
+
+
+def later(array, after):
+    return lax.optimization_barrier((array, after))[0]
 
 
 def swap(array, bits, bits_one=None):
@@ -396,60 +443,71 @@
             pltpu.SemaphoreType.DMA((3,)),
         ],
     )
-    line = jnp.concatenate([piece] + [swap(piece, 8 * k) for k in (1, 2, 3)], axis=1)
-    plane = [line] + [swap(line, 2 * k) for k in (1, 2, 3)]
-    partner = [swap(line, 1)]
-
     nbr_t, feat_t = neighbors.T, features.T
-    graphs = [
-        call(
+
+    def graph(b, after=()):
+        return call(
             functools.partial(graph_kernel, fan_in, b), "graph", 2.6, 4,
             [shape((BLOCK, BLOCK), bf16), shape((BLOCK, LANES), bf16), shape((TOP, BLOCK), bf16)],
-            nbr_t, feat_t, after=[line] * (b > 0),
+            nbr_t, feat_t, after=after,
         )
-        for b in range(nblk)
-    ]
+
+    graphs = [graph(0)]
+    line = [later(swap(piece, 8 * k), graphs[0][2]) for k in (1, 2, 3)]
+    line = jnp.concatenate([piece] + line, axis=1)
+    plane = [line] + [swap(line, 2 * k) for k in (1, 2, 3)]
+    graphs += [graph(b, [line]) for b in range(1, nblk)]
     ms, ps, pts = ([graph[k] for graph in graphs] for k in range(3))
+    partner = [swap(later(line, pts[-1]), 1)]
 
     nodes = nblk * BLOCK
-    fwd = []
-    for g in range(4):
-        if g:
-            plane[g], _ = lax.optimization_barrier((plane[g], fwd[0][3]))
-            partner.append(swap(plane[g], 1))
-        fwd.append(
-            call(
-                functools.partial(forward_kernel, nblk), "forward", 2, 4,
-                [
-                    shape((LANES, group), bf16), shape((nodes, group), bf16),
-                    shape((nodes, group), bf16), shape((nblk, 48, BLOCK), f32),
-                ],
-                plane[g], partner[g], *ps,
-                scratch=[pltpu.VMEM((ROWS, group), bf16)],
+    def forward_shapes(count):
+        wide = count * group
+        return [
+            shape((LANES, wide), bf16), shape((nodes, wide), bf16), shape((nodes, wide), bf16),
+        ]
+
+    logit_share = shape((nblk, 48, BLOCK), f32)
+    early = call(
+        functools.partial(forward_kernel, nblk, 1), "forward", 1.5, 4,
+        forward_shapes(1) + [logit_share], line, partner[0], *ps,
+        scratch=[pltpu.VMEM((ROWS, group), bf16)],
+    )
+    partner += [swap(part, 1) for part in plane[1:]]
+    half_pass = [shape((HALF, len(PASSES[0]) * LANES), f32)] * 2
+    *late, qq, qqt, scal, keep, send = call(
+        functools.partial(turn_kernel, nblk, 3, 2, classes, degree, PASSES[0]), "turn", 9, 8,
+        forward_shapes(3)
+        + [shape((nodes, LANES), bf16), shape((nblk, 96, BLOCK), bf16), shape((16, LANES), f32)]
+        + half_pass,
+        *plane[1:], *partner[1:], *ps, *pts, *early, *ms, label_mask, labels,
+        b_second.reshape(1, classes),
+        scratch=[
+            pltpu.VMEM((ROWS, 3 * group), bf16),
+            pltpu.VMEM((nblk, 48, BLOCK), f32),
+            pltpu.VMEM((8, LANES), f32),
+        ],
+    )
+    keeps, gots, received = [], [], []
+    for n, (slots, pieces) in enumerate(zip(PASSES, PIECES, strict=True)):
+        if n:
+            keep, send = call(
+                functools.partial(backward_kernel, nblk, slots), "backward", 0.35 * len(slots), 6,
+                [shape((HALF, len(slots) * LANES), f32)] * 2,
+                qq, qqt, *pts, *early[0:3], *late, scal,
             )
-        )
-    qq, qqt, scal = call(
-        functools.partial(middle_kernel, nblk, classes, degree), "middle", 2.6, 4,
-        [shape((nodes, LANES), bf16), shape((nblk, 96, BLOCK), bf16), shape((16, LANES), f32)],
-        *[f[3] for f in fwd], *ms, label_mask, labels, b_second.reshape(1, classes),
-        scratch=[pltpu.VMEM((8, LANES), f32)],
-    )
-    keeps, gots = [], []
-    for g in range(4):
-        keep, send = call(
-            functools.partial(backward_kernel, nblk, g == 0), "backward", 1.4, 4,
-            [shape((HALF, group), f32)] * 2,
-            qq, qqt, *pts, *fwd[g][0:3], scal,
-        )
         keeps.append(keep)
         gots.append(swap(send, 1))
-    mine, *rest = call(
-        add_core_kernel, "add_core", 0.3, 4,
-        [shape((HALF, group), f32)] + [shape((HALF, group), bf16)] * 3, *keeps, *gots,
-    )
+        sums = call(
+            functools.partial(add_core_kernel, pieces, n + 1), "add_core", 0.3, 4,
+            [shape((HALF, group), f32 if k in (0, ORDER[0]) else bf16) for k in pieces],
+            *keeps, *gots,
+        )
+        for k, part in zip(pieces, sums, strict=True):
+            received.append(swap(part, 2 * k, 8 * k) if k else part)
+    received = [received[n] for n in (2, 0, 1, 3)]
     mine = call(
-        add_piece_kernel, "add_piece", 0.3, 2, shape((HALF, group), bf16),
-        mine, *[swap(rest[k - 1], 2 * k, 8 * k) for k in (1, 2, 3)],
+        add_piece_kernel, "add_piece", 0.3, 2, shape((HALF, group), bf16), *received
     )
     mine = call(
         add_line_kernel, "add_line", 0.3, 2, shape((HALF, group), bf16),

time: 64.9 us -> 61.2 us (0.943)
  starting transfers between devices: 23.7 us -> 22.4 us
  Pallas kernels: 23.9 us -> 22.6 us
  waiting for transfers between devices: 15.7 us -> 14.7 us
    ppermute x27 -> x25, starting transfers between devices: 23.7 us -> 22.4 us  [swap(): lax.ppermute(array, AXES, [(i, i ^ both[i % 2]) for i in range(count)])]
    pallas_call x16 -> x11, Pallas kernels: 23.9 us -> 22.6 us  [call(): pl.pallas_call(body, out_shape=out_shape, scratch_shapes=scratch, compile...]
    ppermute x27 -> x25, waiting for transfers between devices: 15.7 us -> 14.7 us  [swap(): lax.ppermute(array, AXES, [(i, i ^ both[i % 2]) for i in range(count)])]
  transfers between devices with their start and end apart: 27 -> 25, of which waited for: 13 -> 12; matrix products, arithmetic and copies ran while one was open for 0% -> 0% of each run, Pallas kernels for 21% -> 13%
where the time goes in v3:
time: 61.2 us; the launch traced here: 61.1 us
  Pallas kernels  22.6 us (37%)
  starting transfers between devices  22.4 us (37%)
  waiting for transfers between devices  14.7 us (24%)
  between operations  1.19 us (2%)
    pallas_call x11, Pallas kernels, call(): pl.pallas_call(body, out_shape=out_shape, scratch_shapes=scratch, compile...  22.6 us
    ppermute x25, starting transfers between devices, swap(): lax.ppermute(array, AXES, [(i, i ^ both[i % 2]) for i in range(count)])  22.4 us
    ppermute x25, waiting for transfers between devices, swap(): lax.ppermute(array, AXES, [(i, i ^ both[i % 2]) for i in range(count)])  14.7 us
  transfers between devices with their start and end apart: 25, of which 12 were waited for; matrix products, arithmetic and copies ran while one was open for 0% of the time, Pallas kernels for 13%

profile of v3, /device:TPU:0, one launch (start us, length us, event | category | flops | bytes accessed | tf_op | source)
XLA Modules:
  0.0 61.1 jit_solution(11678514009228685127)
XLA Ops:
  0.7 1.7 %pack.1 = bf16[80,128]{1,0:T(8,128)(2,1)} custom-call(f32[64,100]{1,0:T(8,128)} %bitcast.32, f32[47,64]{1,0:T(8,128)} %bitcast.34, f32[1,64]{1,0:T(1,128)} %bitcast.36), custom_call_target="tpu_custom_call" | custom-call | flops 1000000000 | bytes 2000000 | tf_op jit(solution)/shard_map/pack/pallas_call | solution.py:49
  2.4 5.1 %collective-permute-start.2 = (bf16[80,128]{1,0:T(8,128)(2,1)}, bf16[80,128]{1,0:T(8,128)(2,1)S(1)}, u32[]{:S(2)}, u32[]{:S(2)}) collective-permute-start(bf16[80,128]{1,0:T(8,128)(2,1)} %pack.1), channel_id=1, source_target_pairs={{0,24},{1,25},{2,26},{3,27},{4,28},{5,29},{6,30},{7,31},{8,16},{9,... | collective-permute-start | bytes 61448 | tf_op jit(solution)/shard_map/ppermute | solution.py:418
  7.5 0.6 %collective-permute-start = (bf16[80,128]{1,0:T(8,128)(2,1)}, bf16[80,128]{1,0:T(8,128)(2,1)S(1)}, u32[]{:S(2)}, u32[]{:S(2)}) collective-permute-start(bf16[80,128]{1,0:T(8,128)(2,1)} %pack.1), channel_id=1, source_target_pairs={{0,8},{1,9},{2,10},{3,11},{4,12},{5,13},{6,14},{7,15},{8,0},{9,1},... | collective-permute-start | bytes 61448 | tf_op jit(solution)/shard_map/ppermute | solution.py:418
  8.1 2.6 %graph.2 = (bf16[1024,1024]{1,0:T(8,128)(2,1)S(1)}, bf16[1024,128]{1,0:T(8,128)(2,1)S(1)}, bf16[112,1024]{1,0:T(8,128)(2,1)S(1)}) custom-call(s32[8,2048]{1,0:T(8,128)S(1)} %bitcast.30, bf16[100,2048]{1,0:T(8,128)(2,1)S(1)} %bitcast.28), custom_call_target="tpu_custom_call" | custom-call | flops 2600000000 | bytes 5200000 | tf_op jit(solution)/shard_map/graph/pallas_call | solution.py:49
  10.7 1.6 %collective-permute-done.1 = bf16[80,128]{1,0:T(8,128)(2,1)S(1)} collective-permute-done((bf16[80,128]{1,0:T(8,128)(2,1)}, bf16[80,128]{1,0:T(8,128)(2,1)S(1)}, u32[]{:S(2)}, u32[]{:S(2)}) %collective-permute-start.1) | collective-permute-done | bytes 20512 | tf_op jit(solution)/shard_map/ppermute | solution.py:418
  12.4 2.5 %collective-permute-start.5 = (bf16[80,512]{1,0:T(8,128)(2,1)S(1)}, bf16[80,512]{1,0:T(8,128)(2,1)S(1)}, u32[]{:S(2)}, u32[]{:S(2)}) collective-permute-start(bf16[80,512]{1,0:T(8,128)(2,1)S(1)} %pad_maximum_fusion.refs_2_.refs_0_), channel_id=1, source_target_pairs={{0,6},{1,7},{2,4},{3,5},{4,2},{5,3},{6,0},{7,1},{8,14},{9,15},{10,... | collective-permute-start | bytes 245768 | tf_op jit(solution)/shard_map/ppermute | solution.py:418
  14.9 0.5 collective-permute-start.4
  15.4 0.5 collective-permute-start.3
  15.9 2.6 %graph.3 = (bf16[1024,1024]{1,0:T(8,128)(2,1)S(1)}, bf16[1024,128]{1,0:T(8,128)(2,1)S(1)}, bf16[112,1024]{1,0:T(8,128)(2,1)S(1)}) custom-call(s32[8,2048]{1,0:T(8,128)S(1)} %bitcast.31, bf16[100,2048]{1,0:T(8,128)(2,1)S(1)} %bitcast.29, bf16[80,512]{1,0:T(8,128)(2,1)S(1)} %pad_maximum_fusion.refs_2_.refs_0_), custom_call_target="tpu_custom_call" | custom-call | flops 2600000000 | bytes 5200000 | tf_op jit(solution)/shard_map/graph/pallas_call | solution.py:49
  18.6 0.5 collective-permute-start.8
  19.4 0.4 collective-permute-done.3.refs_0_
  20.0 1.5 %forward.1 = (bf16[128,512]{1,0:T(8,128)(2,1)S(1)}, bf16[2048,512]{1,0:T(8,128)(2,1)S(1)}, bf16[2048,512]{1,0:T(8,128)(2,1)S(1)}, f32[2,48,1024]{2,1,0:T(8,128)S(1)}) custom-call(bf16[80,512]{1,0:T(8,128)(2,1)S(1)} %pad_maximum_fusion.refs_2_.refs_0_, bf16[80,512]{1,0:T(8,128)(2,1)S(1)} %collective-permute-done.9.refs_1_, ...), custom_call_target="tpu_custom_call" | custom-call | flops 1500000000 | bytes 3000000 | tf_op jit(solution)/shard_map/forward/pallas_call | solution.py:49
  21.6 10.3 %turn.1 = (bf16[128,1536]{1,0:T(8,128)(2,1)S(1)}, bf16[2048,1536]{1,0:T(8,128)(2,1)S(1)}, bf16[2048,1536]{1,0:T(8,128)(2,1)S(1)}, bf16[2048,128]{1,0:T(8,128)(2,...) custom-call(bf16[80,512]{1,0:T(8,128)(2,1)S(1)} %collective-permute-, ...), custom_call_target="tpu_custom_call" | custom-call | flops 8999999488 | bytes 18000000 | tf_op jit(solution)/shard_map/turn/pallas_call | solution.py:49
  31.8 0.5 collective-permute-start.10
  32.3 1.3 %backward.1 = (f32[80,512]{1,0:T(8,128)S(1)}, f32[80,512]{1,0:T(8,128)S(1)}) custom-call(bf16[2048,128]{1,0:T(8,128)(2,1)S(1)} %get-tuple-element.77.refs_0_, bf16[2,96,1024]{2,1,0:T(8,128)(2,1)S(1)} %get-tuple-element.78.refs_1_, bf16[112,1024]{1,0:T(8,128)(2,1)S(1)} %get-tuple-element.62.refs_8_.refs_2_, ...), custom_call_target="tpu_custom_call" | custom-call | flops 1400000000 | bytes 2800000 | tf_op jit(solution)/shard_map/backward/pallas_call | solution.py:49
  34.1 2.4 %collective-permute-start.12 = (f32[80,512]{1,0:T(8,128)S(1)}, f32[80,512]{1,0:T(8,128)S(1)}, u32[]{:S(2)}, u32[]{:S(2)}) collective-permute-start(f32[80,512]{1,0:T(8,128)S(1)} %get-tuple-element.87), channel_id=1, source_target_pairs={{0,6},{1,25},{2,4},{3,27},{4,2},{5,29},{6,0},{7,31},{8,14},{9,17},... | collective-permute-start | bytes 491528 | tf_op jit(solution)/shard_map/ppermute | solution.py:418
  36.6 0.6 collective-permute-start.14
  37.1 0.8 %collective-permute-start.13 = (bf16[80,512]{1,0:T(8,128)(2,1)S(1)}, bf16[80,512]{1,0:T(8,128)(2,1)S(1)}, u32[]{:S(2)}, u32[]{:S(2)}) collective-permute-start(bf16[80,512]{1,0:T(8,128)(2,1)S(1)} %get-tuple-element.88), channel_id=1, source_target_pairs={{0,2},{1,9},{2,0},{3,11},{4,6},{5,13},{6,4},{7,15},{8,10},{9,1},{1... | collective-permute-start | bytes 245768 | tf_op jit(solution)/shard_map/ppermute | solution.py:418
  37.9 3.3 %collective-permute-done.14.refs_3_ = bf16[80,512]{1,0:T(8,128)(2,1)S(1)} collective-permute-done((bf16[80,512]{1,0:T(8,128)(2,1)S(1)}, bf16[80,512]{1,0:T(8,128)(2,1)S(1)}, u32[]{:S(2)}, u32[]{:S(2)}) %collective-permute-start.14) | collective-permute-done | bytes 81952 | tf_op jit(solution)/shard_map/ppermute | solution.py:418
  41.6 2.2 %collective-permute-start.17 = (bf16[80,512]{1,0:T(8,128)(2,1)S(1)}, bf16[80,512]{1,0:T(8,128)(2,1)S(1)}, u32[]{:S(2)}, u32[]{:S(2)}) collective-permute-start(bf16[80,512]{1,0:T(8,128)(2,1)S(1)} %add_piece.1.refs_0_), channel_id=1, source_target_pairs={{0,24},{1,7},{2,26},{3,5},{4,28},{5,3},{6,30},{7,1},{8,16},{9,15},... | collective-permute-start | bytes 245768 | tf_op jit(solution)/shard_map/ppermute | solution.py:418
  43.8 2.3 %collective-permute-start.15 = (bf16[80,512]{1,0:T(8,128)(2,1)S(1)}, bf16[80,512]{1,0:T(8,128)(2,1)S(1)}, u32[]{:S(2)}, u32[]{:S(2)}) collective-permute-start(bf16[80,512]{1,0:T(8,128)(2,1)S(1)} %add_piece.1.refs_0_), channel_id=1, source_target_pairs={{0,8},{1,3},{2,10},{3,1},{4,12},{5,7},{6,14},{7,5},{8,0},{9,11},{1... | collective-permute-start | bytes 245768 | tf_op jit(solution)/shard_map/ppermute | solution.py:418
  46.1 1.9 %collective-permute-done.17.refs_3_ = bf16[80,512]{1,0:T(8,128)(2,1)S(1)} collective-permute-done((bf16[80,512]{1,0:T(8,128)(2,1)S(1)}, bf16[80,512]{1,0:T(8,128)(2,1)S(1)}, u32[]{:S(2)}, u32[]{:S(2)}) %collective-permute-start.17) | collective-permute-done | bytes 81952 | tf_op jit(solution)/shard_map/ppermute | solution.py:418
  48.0 2.0 %collective-permute-done.16.refs_2_ = bf16[80,512]{1,0:T(8,128)(2,1)S(1)} collective-permute-done((bf16[80,512]{1,0:T(8,128)(2,1)S(1)}, bf16[80,512]{1,0:T(8,128)(2,1)S(1)}, u32[]{:S(2)}, u32[]{:S(2)}) %collective-permute-start.16) | collective-permute-done | bytes 81952 | tf_op jit(solution)/shard_map/ppermute | solution.py:418
  50.0 2.1 %collective-permute-start.20 = (bf16[80,512]{1,0:T(8,128)(2,1)S(1)}, bf16[80,512]{1,0:T(8,128)(2,1)S(1)}, u32[]{:S(2)}, u32[]{:S(2)}) collective-permute-start(bf16[80,512]{1,0:T(8,128)(2,1)S(1)} %add_line.1.refs_0_), channel_id=1, source_target_pairs={{0,6},{1,25},{2,4},{3,27},{4,2},{5,29},{6,0},{7,31},{8,14},{9,17},... | collective-permute-start | bytes 245768 | tf_op jit(solution)/shard_map/ppermute | solution.py:418
  52.0 0.6 %collective-permute-start.19 = (bf16[80,512]{1,0:T(8,128)(2,1)S(1)}, bf16[80,512]{1,0:T(8,128)(2,1)S(1)}, u32[]{:S(2)}, u32[]{:S(2)}) collective-permute-start(bf16[80,512]{1,0:T(8,128)(2,1)S(1)} %add_line.1.refs_0_), channel_id=1, source_target_pairs={{0,4},{1,17},{2,6},{3,19},{4,0},{5,21},{6,2},{7,23},{8,12},{9,25},... | collective-permute-start | bytes 245768 | tf_op jit(solution)/shard_map/ppermute | solution.py:418
  52.7 0.9 %collective-permute-start.18 = (bf16[80,512]{1,0:T(8,128)(2,1)S(1)}, bf16[80,512]{1,0:T(8,128)(2,1)S(1)}, u32[]{:S(2)}, u32[]{:S(2)}) collective-permute-start(bf16[80,512]{1,0:T(8,128)(2,1)S(1)} %add_line.1.refs_0_), channel_id=1, source_target_pairs={{0,2},{1,9},{2,0},{3,11},{4,6},{5,13},{6,4},{7,15},{8,10},{9,1},{1... | collective-permute-start | bytes 245768 | tf_op jit(solution)/shard_map/ppermute | solution.py:418
  53.5 1.8 %collective-permute-done.20.refs_3_ = bf16[80,512]{1,0:T(8,128)(2,1)S(1)} collective-permute-done((bf16[80,512]{1,0:T(8,128)(2,1)S(1)}, bf16[80,512]{1,0:T(8,128)(2,1)S(1)}, u32[]{:S(2)}, u32[]{:S(2)}) %collective-permute-start.20) | collective-permute-done | bytes 81952 | tf_op jit(solution)/shard_map/ppermute | solution.py:418
  55.4 1.1 %collective-permute-done.19.refs_2_ = bf16[80,512]{1,0:T(8,128)(2,1)S(1)} collective-permute-done((bf16[80,512]{1,0:T(8,128)(2,1)S(1)}, bf16[80,512]{1,0:T(8,128)(2,1)S(1)}, u32[]{:S(2)}, u32[]{:S(2)}) %collective-permute-start.19) | collective-permute-done | bytes 81952 | tf_op jit(solution)/shard_map/ppermute | solution.py:418
  56.5 0.6 %collective-permute-done.18.refs_1_ = bf16[80,512]{1,0:T(8,128)(2,1)S(1)} collective-permute-done((bf16[80,512]{1,0:T(8,128)(2,1)S(1)}, bf16[80,512]{1,0:T(8,128)(2,1)S(1)}, u32[]{:S(2)}, u32[]{:S(2)}) %collective-permute-start.18) | collective-permute-done | bytes 81952 | tf_op jit(solution)/shard_map/ppermute | solution.py:418
  57.1 0.6 %collective-permute-done.23.refs_6_ = bf16[80,512]{1,0:T(8,128)(2,1)S(1)} collective-permute-done((bf16[80,512]{1,0:T(8,128)(2,1)S(1)}, bf16[80,512]{1,0:T(8,128)(2,1)S(1)}, u32[]{:S(2)}, u32[]{:S(2)}) %collective-permute-start.23) | collective-permute-done | bytes 81952 | tf_op jit(solution)/shard_map/ppermute | solution.py:418
  57.8 0.6 %collective-permute-done.22.refs_5_ = bf16[80,512]{1,0:T(8,128)(2,1)S(1)} collective-permute-done((bf16[80,512]{1,0:T(8,128)(2,1)S(1)}, bf16[80,512]{1,0:T(8,128)(2,1)S(1)}, u32[]{:S(2)}, u32[]{:S(2)}) %collective-permute-start.22) | collective-permute-done | bytes 81952 | tf_op jit(solution)/shard_map/ppermute | solution.py:418
  58.5 2.4 %update.1 = (f32[1,1]{1,0:T(1,128)}, f32[1,1]{1,0:T(1,128)}, f32[1,1]{1,0:T(1,128)}, f32[64,100]{1,0:T(8,128)}, f32[47,64]{1,0:T(8,128)}, /*index=5*/f32[64,100]...) custom-call(bf16[80,512]{1,0:T(8,128)(2,1)S(1)} %add_line.1.refs_0_,, ...), custom_call_target="tpu_custom_call" | custom-call | flops 2500000000 | bytes 5000000 | tf_op jit(solution)/shard_map/update/pallas_call | solution.py:49
  (72 shorter events, 1.4 us)
Async XLA Ops:
  2.4 8.4 %collective-permute-start.2 = (bf16[80,128]{1,0:T(8,128)(2,1)}, bf16[80,128]{1,0:T(8,128)(2,1)S(1)}, u32[]{:S(2)}, u32[]{:S(2)}) collective-permute-start(bf16[80,128]{1,0:T(8,128)(2,1)} %pack.1), channel_id=1, source_target_pairs={{0,24},{1,25},{2,26},{3,27},{4,28},{5,29},{6,30},{7,31},{8,16},{9,... | collective-permute-start | bytes 61448 | tf_op jit(solution)/shard_map/ppermute | solution.py:418
  7.5 4.9 %collective-permute-start.1 = (bf16[80,128]{1,0:T(8,128)(2,1)}, bf16[80,128]{1,0:T(8,128)(2,1)S(1)}, u32[]{:S(2)}, u32[]{:S(2)}) collective-permute-start(bf16[80,128]{1,0:T(8,128)(2,1)} %pack.1), channel_id=1, source_target_pairs={{0,16},{1,17},{2,18},{3,19},{4,20},{5,21},{6,22},{7,23},{8,24},{9,... | collective-permute-start | bytes 61448 | tf_op jit(solution)/shard_map/ppermute | solution.py:418
  7.5 4.9 %collective-permute-start = (bf16[80,128]{1,0:T(8,128)(2,1)}, bf16[80,128]{1,0:T(8,128)(2,1)S(1)}, u32[]{:S(2)}, u32[]{:S(2)}) collective-permute-start(bf16[80,128]{1,0:T(8,128)(2,1)} %pack.1), channel_id=1, source_target_pairs={{0,8},{1,9},{2,10},{3,11},{4,12},{5,13},{6,14},{7,15},{8,0},{9,1},... | collective-permute-start | bytes 61448 | tf_op jit(solution)/shard_map/ppermute | solution.py:418
  12.4 6.2 %collective-permute-start.5 = (bf16[80,512]{1,0:T(8,128)(2,1)S(1)}, bf16[80,512]{1,0:T(8,128)(2,1)S(1)}, u32[]{:S(2)}, u32[]{:S(2)}) collective-permute-start(bf16[80,512]{1,0:T(8,128)(2,1)S(1)} %pad_maximum_fusion.refs_2_.refs_0_), channel_id=1, source_target_pairs={{0,6},{1,7},{2,4},{3,5},{4,2},{5,3},{6,0},{7,1},{8,14},{9,15},{10,... | collective-permute-start | bytes 245768 | tf_op jit(solution)/shard_map/ppermute | solution.py:418
  14.9 4.5 %collective-permute-start.4 = (bf16[80,512]{1,0:T(8,128)(2,1)S(1)}, bf16[80,512]{1,0:T(8,128)(2,1)S(1)}, u32[]{:S(2)}, u32[]{:S(2)}) collective-permute-start(bf16[80,512]{1,0:T(8,128)(2,1)S(1)} %pad_maximum_fusion.refs_2_.refs_0_), channel_id=1, source_target_pairs={{0,4},{1,5},{2,6},{3,7},{4,0},{5,1},{6,2},{7,3},{8,12},{9,13},{10,... | collective-permute-start | bytes 245768 | tf_op jit(solution)/shard_map/ppermute | solution.py:418
  15.4 4.4 %collective-permute-start.3 = (bf16[80,512]{1,0:T(8,128)(2,1)S(1)}, bf16[80,512]{1,0:T(8,128)(2,1)S(1)}, u32[]{:S(2)}, u32[]{:S(2)}) collective-permute-start(bf16[80,512]{1,0:T(8,128)(2,1)S(1)} %pad_maximum_fusion.refs_2_.refs_0_), channel_id=1, source_target_pairs={{0,2},{1,3},{2,0},{3,1},{4,6},{5,7},{6,4},{7,5},{8,10},{9,11},{10,... | collective-permute-start | bytes 245768 | tf_op jit(solution)/shard_map/ppermute | solution.py:418
  18.5 1.4 %collective-permute-start.9 = (bf16[80,512]{1,0:T(8,128)(2,1)S(1)}, bf16[80,512]{1,0:T(8,128)(2,1)S(1)}, u32[]{:S(2)}, u32[]{:S(2)}) collective-permute-start(bf16[80,512]{1,0:T(8,128)(2,1)S(1)} %pad_maximum_fusion.refs_2_.refs_0_), channel_id=1, source_target_pairs={{0,1},{1,0},{2,3},{3,2},{4,5},{5,4},{6,7},{7,6},{8,9},{9,8},{10,11... | collective-permute-start | bytes 245768 | tf_op jit(solution)/shard_map/ppermute | solution.py:418
  18.6 2.9 %collective-permute-start.8 = (bf16[80,512]{1,0:T(8,128)(2,1)S(1)}, bf16[80,512]{1,0:T(8,128)(2,1)S(1)}, u32[]{:S(2)}, u32[]{:S(2)}) collective-permute-start(bf16[80,512]{1,0:T(8,128)(2,1)S(1)} %collective-permute-done.5.refs_2_), channel_id=1, source_target_pairs={{0,1},{1,0},{2,3},{3,2},{4,5},{5,4},{6,7},{7,6},{8,9},{9,8},{10,11... | collective-permute-start | bytes 245768 | tf_op jit(solution)/shard_map/ppermute | solution.py:418
  19.4 2.1 %collective-permute-start.7 = (bf16[80,512]{1,0:T(8,128)(2,1)S(1)}, bf16[80,512]{1,0:T(8,128)(2,1)S(1)}, u32[]{:S(2)}, u32[]{:S(2)}) collective-permute-start(bf16[80,512]{1,0:T(8,128)(2,1)S(1)} %collective-permute-done.4.refs_1_), channel_id=1, source_target_pairs={{0,1},{1,0},{2,3},{3,2},{4,5},{5,4},{6,7},{7,6},{8,9},{9,8},{10,11... | collective-permute-start | bytes 245768 | tf_op jit(solution)/shard_map/ppermute | solution.py:418
  19.8 1.7 %collective-permute-start.6 = (bf16[80,512]{1,0:T(8,128)(2,1)S(1)}, bf16[80,512]{1,0:T(8,128)(2,1)S(1)}, u32[]{:S(2)}, u32[]{:S(2)}) collective-permute-start(bf16[80,512]{1,0:T(8,128)(2,1)S(1)} %collective-permute-done.3.refs_0_), channel_id=1, source_target_pairs={{0,1},{1,0},{2,3},{3,2},{4,5},{5,4},{6,7},{7,6},{8,9},{9,8},{10,11... | collective-permute-start | bytes 245768 | tf_op jit(solution)/shard_map/ppermute | solution.py:418
  31.8 2.0 %collective-permute-start.10 = (f32[80,1536]{1,0:T(8,128)S(1)}, f32[80,1536]{1,0:T(8,128)S(1)}, u32[]{:S(2)}, u32[]{:S(2)}) collective-permute-start(f32[80,1536]{1,0:T(8,128)S(1)} %get-tuple-element.84), channel_id=1, source_target_pairs={{0,1},{1,0},{2,3},{3,2},{4,5},{5,4},{6,7},{7,6},{8,9},{9,8},{10,11... | collective-permute-start | bytes 1474568 | tf_op jit(solution)/shard_map/ppermute | solution.py:418
  33.7 2.8 %collective-permute-start.11 = (f32[80,512]{1,0:T(8,128)S(1)}, f32[80,512]{1,0:T(8,128)S(1)}, u32[]{:S(2)}, u32[]{:S(2)}) collective-permute-start(f32[80,512]{1,0:T(8,128)S(1)} %get-tuple-element.85), channel_id=1, source_target_pairs={{0,1},{1,0},{2,3},{3,2},{4,5},{5,4},{6,7},{7,6},{8,9},{9,8},{10,11... | collective-permute-start | bytes 491528 | tf_op jit(solution)/shard_map/ppermute | solution.py:418
  33.8 24.6 %copy-start = (f32[2048,64]{0,1:T(8,128)S(1)}, f32[2048,64]{0,1:T(8,128)}, u32[]{:S(2)}) copy-start(f32[2048,64]{0,1:T(8,128)} %param.29) | copy-start | bytes 1572868
  33.8 24.6 %copy-start.1 = (f32[64,2048]{1,0:T(8,128)S(1)}, f32[64,2048]{1,0:T(8,128)}, u32[]{:S(2)}) copy-start(f32[64,2048]{1,0:T(8,128)} %refs_14_.1) | copy-start | bytes 1572868
  33.8 24.6 %copy-start.2 = (f32[2048,64]{0,1:T(8,128)S(1)}, f32[2048,64]{0,1:T(8,128)}, u32[]{:S(2)}) copy-start(f32[2048,64]{0,1:T(8,128)} %param.33) | copy-start | bytes 1572868
  33.9 24.6 %copy-start.3 = (f32[64,2048]{1,0:T(8,128)S(1)}, f32[64,2048]{1,0:T(8,128)}, u32[]{:S(2)}) copy-start(f32[64,2048]{1,0:T(8,128)} %refs_18_.1) | copy-start | bytes 1572868
  33.9 24.5 %copy-start.6 = (f32[100,100]{1,0:T(8,128)S(1)}, f32[100,100]{1,0:T(8,128)}, u32[]{:S(2)}) copy-start(f32[100,100]{1,0:T(8,128)} %refs_12_.1) | copy-start | bytes 120004
  33.9 24.5 %copy-start.7 = (f32[100,100]{1,0:T(8,128)S(1)}, f32[100,100]{1,0:T(8,128)}, u32[]{:S(2)}) copy-start(f32[100,100]{1,0:T(8,128)} %refs_16_.3) | copy-start | bytes 120004
  33.9 24.5 %copy-start.8 = (f32[100,64]{0,1:T(8,128)S(1)}, f32[100,64]{0,1:T(8,128)}, u32[]{:S(2)}) copy-start(f32[100,64]{0,1:T(8,128)} %param.24) | copy-start | bytes 76804
  34.1 7.5 %collective-permute-start.12 = (f32[80,512]{1,0:T(8,128)S(1)}, f32[80,512]{1,0:T(8,128)S(1)}, u32[]{:S(2)}, u32[]{:S(2)}) collective-permute-start(f32[80,512]{1,0:T(8,128)S(1)} %get-tuple-element.87), channel_id=1, source_target_pairs={{0,6},{1,25},{2,4},{3,27},{4,2},{5,29},{6,0},{7,31},{8,14},{9,17},... | collective-permute-start | bytes 491528 | tf_op jit(solution)/shard_map/ppermute | solution.py:418
  36.6 4.7 %collective-permute-start.14 = (bf16[80,512]{1,0:T(8,128)(2,1)S(1)}, bf16[80,512]{1,0:T(8,128)(2,1)S(1)}, u32[]{:S(2)}, u32[]{:S(2)}) collective-permute-start(bf16[80,512]{1,0:T(8,128)(2,1)S(1)} %get-tuple-element.89), channel_id=1, source_target_pairs={{0,4},{1,17},{2,6},{3,19},{4,0},{5,21},{6,2},{7,23},{8,12},{9,25},... | collective-permute-start | bytes 245768 | tf_op jit(solution)/shard_map/ppermute | solution.py:418
  37.1 4.4 %collective-permute-start.13 = (bf16[80,512]{1,0:T(8,128)(2,1)S(1)}, bf16[80,512]{1,0:T(8,128)(2,1)S(1)}, u32[]{:S(2)}, u32[]{:S(2)}) collective-permute-start(bf16[80,512]{1,0:T(8,128)(2,1)S(1)} %get-tuple-element.88), channel_id=1, source_target_pairs={{0,2},{1,9},{2,0},{3,11},{4,6},{5,13},{6,4},{7,15},{8,10},{9,1},{1... | collective-permute-start | bytes 245768 | tf_op jit(solution)/shard_map/ppermute | solution.py:418
  41.6 6.3 %collective-permute-start.17 = (bf16[80,512]{1,0:T(8,128)(2,1)S(1)}, bf16[80,512]{1,0:T(8,128)(2,1)S(1)}, u32[]{:S(2)}, u32[]{:S(2)}) collective-permute-start(bf16[80,512]{1,0:T(8,128)(2,1)S(1)} %add_piece.1.refs_0_), channel_id=1, source_target_pairs={{0,24},{1,7},{2,26},{3,5},{4,28},{5,3},{6,30},{7,1},{8,16},{9,15},... | collective-permute-start | bytes 245768 | tf_op jit(solution)/shard_map/ppermute | solution.py:418
  43.8 6.1 %collective-permute-start.16 = (bf16[80,512]{1,0:T(8,128)(2,1)S(1)}, bf16[80,512]{1,0:T(8,128)(2,1)S(1)}, u32[]{:S(2)}, u32[]{:S(2)}) collective-permute-start(bf16[80,512]{1,0:T(8,128)(2,1)S(1)} %add_piece.1.refs_0_), channel_id=1, source_target_pairs={{0,16},{1,5},{2,18},{3,7},{4,20},{5,1},{6,22},{7,3},{8,24},{9,13},... | collective-permute-start | bytes 245768 | tf_op jit(solution)/shard_map/ppermute | solution.py:418
  43.8 6.1 %collective-permute-start.15 = (bf16[80,512]{1,0:T(8,128)(2,1)S(1)}, bf16[80,512]{1,0:T(8,128)(2,1)S(1)}, u32[]{:S(2)}, u32[]{:S(2)}) collective-permute-start(bf16[80,512]{1,0:T(8,128)(2,1)S(1)} %add_piece.1.refs_0_), channel_id=1, source_target_pairs={{0,8},{1,3},{2,10},{3,1},{4,12},{5,7},{6,14},{7,5},{8,0},{9,11},{1... | collective-permute-start | bytes 245768 | tf_op jit(solution)/shard_map/ppermute | solution.py:418
  50.0 5.4 %collective-permute-start.20 = (bf16[80,512]{1,0:T(8,128)(2,1)S(1)}, bf16[80,512]{1,0:T(8,128)(2,1)S(1)}, u32[]{:S(2)}, u32[]{:S(2)}) collective-permute-start(bf16[80,512]{1,0:T(8,128)(2,1)S(1)} %add_line.1.refs_0_), channel_id=1, source_target_pairs={{0,6},{1,25},{2,4},{3,27},{4,2},{5,29},{6,0},{7,31},{8,14},{9,17},... | collective-permute-start | bytes 245768 | tf_op jit(solution)/shard_map/ppermute | solution.py:418
  52.0 4.4 %collective-permute-start.19 = (bf16[80,512]{1,0:T(8,128)(2,1)S(1)}, bf16[80,512]{1,0:T(8,128)(2,1)S(1)}, u32[]{:S(2)}, u32[]{:S(2)}) collective-permute-start(bf16[80,512]{1,0:T(8,128)(2,1)S(1)} %add_line.1.refs_0_), channel_id=1, source_target_pairs={{0,4},{1,17},{2,6},{3,19},{4,0},{5,21},{6,2},{7,23},{8,12},{9,25},... | collective-permute-start | bytes 245768 | tf_op jit(solution)/shard_map/ppermute | solution.py:418
  52.7 4.4 %collective-permute-start.18 = (bf16[80,512]{1,0:T(8,128)(2,1)S(1)}, bf16[80,512]{1,0:T(8,128)(2,1)S(1)}, u32[]{:S(2)}, u32[]{:S(2)}) collective-permute-start(bf16[80,512]{1,0:T(8,128)(2,1)S(1)} %add_line.1.refs_0_), channel_id=1, source_target_pairs={{0,2},{1,9},{2,0},{3,11},{4,6},{5,13},{6,4},{7,15},{8,10},{9,1},{1... | collective-permute-start | bytes 245768 | tf_op jit(solution)/shard_map/ppermute | solution.py:418
  53.5 3.6 %collective-permute-start.21 = (bf16[80,512]{1,0:T(8,128)(2,1)S(1)}, bf16[80,512]{1,0:T(8,128)(2,1)S(1)}, u32[]{:S(2)}, u32[]{:S(2)}) collective-permute-start(bf16[80,512]{1,0:T(8,128)(2,1)S(1)} %add_line.1.refs_0_), channel_id=1, source_target_pairs={{0,1},{1,0},{2,3},{3,2},{4,5},{5,4},{6,7},{7,6},{8,9},{9,8},{10,11... | collective-permute-start | bytes 245768 | tf_op jit(solution)/shard_map/ppermute | solution.py:418
  55.4 1.7 %collective-permute-start.24 = (bf16[80,512]{1,0:T(8,128)(2,1)S(1)}, bf16[80,512]{1,0:T(8,128)(2,1)S(1)}, u32[]{:S(2)}, u32[]{:S(2)}) collective-permute-start(bf16[80,512]{1,0:T(8,128)(2,1)S(1)} %collective-permute-done.20.refs_3_), channel_id=1, source_target_pairs={{0,1},{1,0},{2,3},{3,2},{4,5},{5,4},{6,7},{7,6},{8,9},{9,8},{10,11... | collective-permute-start | bytes 245768 | tf_op jit(solution)/shard_map/ppermute | solution.py:418
  56.5 1.3 %collective-permute-start.23 = (bf16[80,512]{1,0:T(8,128)(2,1)S(1)}, bf16[80,512]{1,0:T(8,128)(2,1)S(1)}, u32[]{:S(2)}, u32[]{:S(2)}) collective-permute-start(bf16[80,512]{1,0:T(8,128)(2,1)S(1)} %collective-permute-done.19.refs_2_), channel_id=1, source_target_pairs={{0,1},{1,0},{2,3},{3,2},{4,5},{5,4},{6,7},{7,6},{8,9},{9,8},{10,11... | collective-permute-start | bytes 245768 | tf_op jit(solution)/shard_map/ppermute | solution.py:418
  57.1 1.3 %collective-permute-start.22 = (bf16[80,512]{1,0:T(8,128)(2,1)S(1)}, bf16[80,512]{1,0:T(8,128)(2,1)S(1)}, u32[]{:S(2)}, u32[]{:S(2)}) collective-permute-start(bf16[80,512]{1,0:T(8,128)(2,1)S(1)} %collective-permute-done.18.refs_1_), channel_id=1, source_target_pairs={{0,1},{1,0},{2,3},{3,2},{4,5},{5,4},{6,7},{7,6},{8,9},{9,8},{10,11... | collective-permute-start | bytes 245768 | tf_op jit(solution)/shard_map/ppermute | solution.py:418
  (14 other events, 220.2 us)

commit v4 on v3

--- a/solution.py
+++ b/solution.py
@@ -304,10 +304,12 @@
             out[:, u * LANES : (u + 1) * LANES] = picked.astype(out.dtype)
 
 
-def add_piece_kernel(own_ref, r1_ref, r2_ref, r3_ref, out_ref):
-    out_ref[...] = (
-        own_ref[...] + r1_ref[...].astype(f32) + r2_ref[...].astype(f32) + r3_ref[...].astype(f32)
-    ).astype(bf16)
+def add_first_kernel(own_ref, got_ref, out_ref):
+    out_ref[...] = own_ref[...] + got_ref[...].astype(f32)
+
+
+def add_piece_kernel(own_ref, one_ref, two_ref, out_ref):
+    out_ref[...] = (own_ref[...] + one_ref[...].astype(f32) + two_ref[...].astype(f32)).astype(bf16)
 
 
 def add_line_kernel(h_ref, z1_ref, z2_ref, z3_ref, out_ref):
@@ -500,14 +502,17 @@
         gots.append(swap(send, 1))
         sums = call(
             functools.partial(add_core_kernel, pieces, n + 1), "add_core", 0.3, 4,
-            [shape((HALF, group), f32 if k in (0, ORDER[0]) else bf16) for k in pieces],
+            [shape((HALF, group), bf16 if k else f32) for k in pieces],
             *keeps, *gots,
         )
         for k, part in zip(pieces, sums, strict=True):
             received.append(swap(part, 2 * k, 8 * k) if k else part)
-    received = [received[n] for n in (2, 0, 1, 3)]
     mine = call(
-        add_piece_kernel, "add_piece", 0.3, 2, shape((HALF, group), bf16), *received
+        add_first_kernel, "add_first", 1, 2, shape((HALF, group), f32), received[2], received[0]
+    )
+    mine = call(
+        add_piece_kernel, "add_piece", 0.3, 2, shape((HALF, group), bf16),
+        mine, received[1], received[3],
     )
     mine = call(
         add_line_kernel, "add_line", 0.3, 2, shape((HALF, group), bf16),

time: 61.2 us -> 61.2 us (level)
    pallas_call x11 -> x12, Pallas kernels: 22.6 us -> 22.6 us  [call(): pl.pallas_call(body, out_shape=out_shape, scratch_shapes=scratch, compile...]
  transfers between devices with their start and end apart: 25 -> 25, of which waited for: 12 -> 13; matrix products, arithmetic and copies ran while one was open for 0% -> 0% of each run, Pallas kernels for 13% -> 13%
where the time goes in v4:
time: 61.2 us; the launch traced here: 61.1 us
  Pallas kernels  22.6 us (37%)
  starting transfers between devices  22.6 us (37%)
  waiting for transfers between devices  14.6 us (24%)
  between operations  1.19 us (2%)
    pallas_call x12, Pallas kernels, call(): pl.pallas_call(body, out_shape=out_shape, scratch_shapes=scratch, compile...  22.6 us
    ppermute x25, starting transfers between devices, swap(): lax.ppermute(array, AXES, [(i, i ^ both[i % 2]) for i in range(count)])  22.6 us
    ppermute x25, waiting for transfers between devices, swap(): lax.ppermute(array, AXES, [(i, i ^ both[i % 2]) for i in range(count)])  14.6 us
  transfers between devices with their start and end apart: 25, of which 13 were waited for; matrix products, arithmetic and copies ran while one was open for 0% of the time, Pallas kernels for 13%

profile of v4, /device:TPU:0, one launch (start us, length us, event | category | flops | bytes accessed | tf_op | source)
XLA Modules:
  0.0 61.1 jit_solution(11864219701402025618)
XLA Ops:
  0.7 1.7 %pack.1 = bf16[80,128]{1,0:T(8,128)(2,1)} custom-call(f32[64,100]{1,0:T(8,128)} %bitcast.32, f32[47,64]{1,0:T(8,128)} %bitcast.34, f32[1,64]{1,0:T(1,128)} %bitcast.36), custom_call_target="tpu_custom_call" | custom-call | flops 1000000000 | bytes 2000000 | tf_op jit(solution)/shard_map/pack/pallas_call | solution.py:49
  2.4 5.1 %collective-permute-start.2 = (bf16[80,128]{1,0:T(8,128)(2,1)}, bf16[80,128]{1,0:T(8,128)(2,1)S(1)}, u32[]{:S(2)}, u32[]{:S(2)}) collective-permute-start(bf16[80,128]{1,0:T(8,128)(2,1)} %pack.1), channel_id=1, source_target_pairs={{0,24},{1,25},{2,26},{3,27},{4,28},{5,29},{6,30},{7,31},{8,16},{9,... | collective-permute-start | bytes 61448 | tf_op jit(solution)/shard_map/ppermute | solution.py:420
  7.5 0.6 %collective-permute-start = (bf16[80,128]{1,0:T(8,128)(2,1)}, bf16[80,128]{1,0:T(8,128)(2,1)S(1)}, u32[]{:S(2)}, u32[]{:S(2)}) collective-permute-start(bf16[80,128]{1,0:T(8,128)(2,1)} %pack.1), channel_id=1, source_target_pairs={{0,8},{1,9},{2,10},{3,11},{4,12},{5,13},{6,14},{7,15},{8,0},{9,1},... | collective-permute-start | bytes 61448 | tf_op jit(solution)/shard_map/ppermute | solution.py:420
  8.1 2.6 %graph.2 = (bf16[1024,1024]{1,0:T(8,128)(2,1)S(1)}, bf16[1024,128]{1,0:T(8,128)(2,1)S(1)}, bf16[112,1024]{1,0:T(8,128)(2,1)S(1)}) custom-call(s32[8,2048]{1,0:T(8,128)S(1)} %bitcast.30, bf16[100,2048]{1,0:T(8,128)(2,1)S(1)} %bitcast.28), custom_call_target="tpu_custom_call" | custom-call | flops 2600000000 | bytes 5200000 | tf_op jit(solution)/shard_map/graph/pallas_call | solution.py:49
  10.7 1.6 %collective-permute-done.1 = bf16[80,128]{1,0:T(8,128)(2,1)S(1)} collective-permute-done((bf16[80,128]{1,0:T(8,128)(2,1)}, bf16[80,128]{1,0:T(8,128)(2,1)S(1)}, u32[]{:S(2)}, u32[]{:S(2)}) %collective-permute-start.1) | collective-permute-done | bytes 20512 | tf_op jit(solution)/shard_map/ppermute | solution.py:420
  12.4 2.5 %collective-permute-start.5 = (bf16[80,512]{1,0:T(8,128)(2,1)S(1)}, bf16[80,512]{1,0:T(8,128)(2,1)S(1)}, u32[]{:S(2)}, u32[]{:S(2)}) collective-permute-start(bf16[80,512]{1,0:T(8,128)(2,1)S(1)} %pad_maximum_fusion.refs_2_.refs_0_), channel_id=1, source_target_pairs={{0,6},{1,7},{2,4},{3,5},{4,2},{5,3},{6,0},{7,1},{8,14},{9,15},{10,... | collective-permute-start | bytes 245768 | tf_op jit(solution)/shard_map/ppermute | solution.py:420
  14.9 0.5 collective-permute-start.4
  15.4 0.5 collective-permute-start.3
  15.9 2.6 %graph.3 = (bf16[1024,1024]{1,0:T(8,128)(2,1)S(1)}, bf16[1024,128]{1,0:T(8,128)(2,1)S(1)}, bf16[112,1024]{1,0:T(8,128)(2,1)S(1)}) custom-call(s32[8,2048]{1,0:T(8,128)S(1)} %bitcast.31, bf16[100,2048]{1,0:T(8,128)(2,1)S(1)} %bitcast.29, bf16[80,512]{1,0:T(8,128)(2,1)S(1)} %pad_maximum_fusion.refs_2_.refs_0_), custom_call_target="tpu_custom_call" | custom-call | flops 2600000000 | bytes 5200000 | tf_op jit(solution)/shard_map/graph/pallas_call | solution.py:49
  18.6 0.5 collective-permute-start.8
  20.0 1.5 %forward.1 = (bf16[128,512]{1,0:T(8,128)(2,1)S(1)}, bf16[2048,512]{1,0:T(8,128)(2,1)S(1)}, bf16[2048,512]{1,0:T(8,128)(2,1)S(1)}, f32[2,48,1024]{2,1,0:T(8,128)S(1)}) custom-call(bf16[80,512]{1,0:T(8,128)(2,1)S(1)} %pad_maximum_fusion.refs_2_.refs_0_, bf16[80,512]{1,0:T(8,128)(2,1)S(1)} %collective-permute-done.9.refs_1_, ...), custom_call_target="tpu_custom_call" | custom-call | flops 1500000000 | bytes 3000000 | tf_op jit(solution)/shard_map/forward/pallas_call | solution.py:49
  21.6 10.3 %turn.1 = (bf16[128,1536]{1,0:T(8,128)(2,1)S(1)}, bf16[2048,1536]{1,0:T(8,128)(2,1)S(1)}, bf16[2048,1536]{1,0:T(8,128)(2,1)S(1)}, bf16[2048,128]{1,0:T(8,128)(2,...) custom-call(bf16[80,512]{1,0:T(8,128)(2,1)S(1)} %collective-permute-, ...), custom_call_target="tpu_custom_call" | custom-call | flops 8999999488 | bytes 18000000 | tf_op jit(solution)/shard_map/turn/pallas_call | solution.py:49
  32.3 1.3 %backward.1 = (f32[80,512]{1,0:T(8,128)S(1)}, f32[80,512]{1,0:T(8,128)S(1)}) custom-call(bf16[2048,128]{1,0:T(8,128)(2,1)S(1)} %get-tuple-element.77.refs_0_, bf16[2,96,1024]{2,1,0:T(8,128)(2,1)S(1)} %get-tuple-element.78.refs_1_, bf16[112,1024]{1,0:T(8,128)(2,1)S(1)} %get-tuple-element.62.refs_8_.refs_2_, ...), custom_call_target="tpu_custom_call" | custom-call | flops 1400000000 | bytes 2800000 | tf_op jit(solution)/shard_map/backward/pallas_call | solution.py:49
  33.9 2.4 %collective-permute-start.12 = (bf16[80,512]{1,0:T(8,128)(2,1)S(1)}, bf16[80,512]{1,0:T(8,128)(2,1)S(1)}, u32[]{:S(2)}, u32[]{:S(2)}) collective-permute-start(bf16[80,512]{1,0:T(8,128)(2,1)S(1)} %get-tuple-element.87), channel_id=1, source_target_pairs={{0,6},{1,25},{2,4},{3,27},{4,2},{5,29},{6,0},{7,31},{8,14},{9,17},... | collective-permute-start | bytes 245768 | tf_op jit(solution)/shard_map/ppermute | solution.py:420
  36.4 0.6 collective-permute-start.14
  37.0 0.9 %collective-permute-start.13 = (bf16[80,512]{1,0:T(8,128)(2,1)S(1)}, bf16[80,512]{1,0:T(8,128)(2,1)S(1)}, u32[]{:S(2)}, u32[]{:S(2)}) collective-permute-start(bf16[80,512]{1,0:T(8,128)(2,1)S(1)} %get-tuple-element.88), channel_id=1, source_target_pairs={{0,2},{1,9},{2,0},{3,11},{4,6},{5,13},{6,4},{7,15},{8,10},{9,1},{1... | collective-permute-start | bytes 245768 | tf_op jit(solution)/shard_map/ppermute | solution.py:420
  37.9 1.4 %collective-permute-done.12.refs_1_ = bf16[80,512]{1,0:T(8,128)(2,1)S(1)} collective-permute-done((bf16[80,512]{1,0:T(8,128)(2,1)S(1)}, bf16[80,512]{1,0:T(8,128)(2,1)S(1)}, u32[]{:S(2)}, u32[]{:S(2)}) %collective-permute-start.12) | collective-permute-done | bytes 81952 | tf_op jit(solution)/shard_map/ppermute | solution.py:420
  39.5 1.4 %collective-permute-done.14.refs_2_ = bf16[80,512]{1,0:T(8,128)(2,1)S(1)} collective-permute-done((bf16[80,512]{1,0:T(8,128)(2,1)S(1)}, bf16[80,512]{1,0:T(8,128)(2,1)S(1)}, u32[]{:S(2)}, u32[]{:S(2)}) %collective-permute-start.14) | collective-permute-done | bytes 81952 | tf_op jit(solution)/shard_map/ppermute | solution.py:420
  40.9 0.5 collective-permute-done.13.refs_1_
  41.5 2.2 %collective-permute-start.17 = (bf16[80,512]{1,0:T(8,128)(2,1)S(1)}, bf16[80,512]{1,0:T(8,128)(2,1)S(1)}, u32[]{:S(2)}, u32[]{:S(2)}) collective-permute-start(bf16[80,512]{1,0:T(8,128)(2,1)S(1)} %add_piece.1.refs_0_), channel_id=1, source_target_pairs={{0,24},{1,7},{2,26},{3,5},{4,28},{5,3},{6,30},{7,1},{8,16},{9,15},... | collective-permute-start | bytes 245768 | tf_op jit(solution)/shard_map/ppermute | solution.py:420
  43.7 2.3 %collective-permute-start.15 = (bf16[80,512]{1,0:T(8,128)(2,1)S(1)}, bf16[80,512]{1,0:T(8,128)(2,1)S(1)}, u32[]{:S(2)}, u32[]{:S(2)}) collective-permute-start(bf16[80,512]{1,0:T(8,128)(2,1)S(1)} %add_piece.1.refs_0_), channel_id=1, source_target_pairs={{0,8},{1,3},{2,10},{3,1},{4,12},{5,7},{6,14},{7,5},{8,0},{9,11},{1... | collective-permute-start | bytes 245768 | tf_op jit(solution)/shard_map/ppermute | solution.py:420
  45.9 1.9 %collective-permute-done.17.refs_3_ = bf16[80,512]{1,0:T(8,128)(2,1)S(1)} collective-permute-done((bf16[80,512]{1,0:T(8,128)(2,1)S(1)}, bf16[80,512]{1,0:T(8,128)(2,1)S(1)}, u32[]{:S(2)}, u32[]{:S(2)}) %collective-permute-start.17) | collective-permute-done | bytes 81952 | tf_op jit(solution)/shard_map/ppermute | solution.py:420
  47.8 2.3 %collective-permute-done.16.refs_2_ = bf16[80,512]{1,0:T(8,128)(2,1)S(1)} collective-permute-done((bf16[80,512]{1,0:T(8,128)(2,1)S(1)}, bf16[80,512]{1,0:T(8,128)(2,1)S(1)}, u32[]{:S(2)}, u32[]{:S(2)}) %collective-permute-start.16) | collective-permute-done | bytes 81952 | tf_op jit(solution)/shard_map/ppermute | solution.py:420
  50.1 1.5 %collective-permute-start.20 = (bf16[80,512]{1,0:T(8,128)(2,1)S(1)}, bf16[80,512]{1,0:T(8,128)(2,1)S(1)}, u32[]{:S(2)}, u32[]{:S(2)}) collective-permute-start(bf16[80,512]{1,0:T(8,128)(2,1)S(1)} %add_line.1.refs_0_), channel_id=1, source_target_pairs={{0,6},{1,25},{2,4},{3,27},{4,2},{5,29},{6,0},{7,31},{8,14},{9,17},... | collective-permute-start | bytes 245768 | tf_op jit(solution)/shard_map/ppermute | solution.py:420
  51.6 1.0 %collective-permute-start.19 = (bf16[80,512]{1,0:T(8,128)(2,1)S(1)}, bf16[80,512]{1,0:T(8,128)(2,1)S(1)}, u32[]{:S(2)}, u32[]{:S(2)}) collective-permute-start(bf16[80,512]{1,0:T(8,128)(2,1)S(1)} %add_line.1.refs_0_), channel_id=1, source_target_pairs={{0,4},{1,17},{2,6},{3,19},{4,0},{5,21},{6,2},{7,23},{8,12},{9,25},... | collective-permute-start | bytes 245768 | tf_op jit(solution)/shard_map/ppermute | solution.py:420
  52.7 1.0 %collective-permute-start.18 = (bf16[80,512]{1,0:T(8,128)(2,1)S(1)}, bf16[80,512]{1,0:T(8,128)(2,1)S(1)}, u32[]{:S(2)}, u32[]{:S(2)}) collective-permute-start(bf16[80,512]{1,0:T(8,128)(2,1)S(1)} %add_line.1.refs_0_), channel_id=1, source_target_pairs={{0,2},{1,9},{2,0},{3,11},{4,6},{5,13},{6,4},{7,15},{8,10},{9,1},{1... | collective-permute-start | bytes 245768 | tf_op jit(solution)/shard_map/ppermute | solution.py:420
  53.7 1.9 %collective-permute-done.20.refs_3_ = bf16[80,512]{1,0:T(8,128)(2,1)S(1)} collective-permute-done((bf16[80,512]{1,0:T(8,128)(2,1)S(1)}, bf16[80,512]{1,0:T(8,128)(2,1)S(1)}, u32[]{:S(2)}, u32[]{:S(2)}) %collective-permute-start.20) | collective-permute-done | bytes 81952 | tf_op jit(solution)/shard_map/ppermute | solution.py:420
  55.6 0.8 %collective-permute-done.19.refs_2_ = bf16[80,512]{1,0:T(8,128)(2,1)S(1)} collective-permute-done((bf16[80,512]{1,0:T(8,128)(2,1)S(1)}, bf16[80,512]{1,0:T(8,128)(2,1)S(1)}, u32[]{:S(2)}, u32[]{:S(2)}) %collective-permute-start.19) | collective-permute-done | bytes 81952 | tf_op jit(solution)/shard_map/ppermute | solution.py:420
  56.4 0.7 %collective-permute-done.18.refs_1_ = bf16[80,512]{1,0:T(8,128)(2,1)S(1)} collective-permute-done((bf16[80,512]{1,0:T(8,128)(2,1)S(1)}, bf16[80,512]{1,0:T(8,128)(2,1)S(1)}, u32[]{:S(2)}, u32[]{:S(2)}) %collective-permute-start.18) | collective-permute-done | bytes 81952 | tf_op jit(solution)/shard_map/ppermute | solution.py:420
  57.1 0.6 collective-permute-done.23.refs_6_
  57.7 0.7 %collective-permute-done.22.refs_5_ = bf16[80,512]{1,0:T(8,128)(2,1)S(1)} collective-permute-done((bf16[80,512]{1,0:T(8,128)(2,1)S(1)}, bf16[80,512]{1,0:T(8,128)(2,1)S(1)}, u32[]{:S(2)}, u32[]{:S(2)}) %collective-permute-start.22) | collective-permute-done | bytes 81952 | tf_op jit(solution)/shard_map/ppermute | solution.py:420
  58.5 2.4 %update.1 = (f32[1,1]{1,0:T(1,128)}, f32[1,1]{1,0:T(1,128)}, f32[1,1]{1,0:T(1,128)}, f32[64,100]{1,0:T(8,128)}, f32[47,64]{1,0:T(8,128)}, /*index=5*/f32[64,100]...) custom-call(bf16[80,512]{1,0:T(8,128)(2,1)S(1)} %add_line.1.refs_0_,, ...), custom_call_target="tpu_custom_call" | custom-call | flops 2500000000 | bytes 5000000 | tf_op jit(solution)/shard_map/update/pallas_call | solution.py:49
  (73 shorter events, 2.0 us)
Async XLA Ops:
  2.4 8.4 %collective-permute-start.2 = (bf16[80,128]{1,0:T(8,128)(2,1)}, bf16[80,128]{1,0:T(8,128)(2,1)S(1)}, u32[]{:S(2)}, u32[]{:S(2)}) collective-permute-start(bf16[80,128]{1,0:T(8,128)(2,1)} %pack.1), channel_id=1, source_target_pairs={{0,24},{1,25},{2,26},{3,27},{4,28},{5,29},{6,30},{7,31},{8,16},{9,... | collective-permute-start | bytes 61448 | tf_op jit(solution)/shard_map/ppermute | solution.py:420
  7.5 4.9 %collective-permute-start.1 = (bf16[80,128]{1,0:T(8,128)(2,1)}, bf16[80,128]{1,0:T(8,128)(2,1)S(1)}, u32[]{:S(2)}, u32[]{:S(2)}) collective-permute-start(bf16[80,128]{1,0:T(8,128)(2,1)} %pack.1), channel_id=1, source_target_pairs={{0,16},{1,17},{2,18},{3,19},{4,20},{5,21},{6,22},{7,23},{8,24},{9,... | collective-permute-start | bytes 61448 | tf_op jit(solution)/shard_map/ppermute | solution.py:420
  7.5 4.9 %collective-permute-start = (bf16[80,128]{1,0:T(8,128)(2,1)}, bf16[80,128]{1,0:T(8,128)(2,1)S(1)}, u32[]{:S(2)}, u32[]{:S(2)}) collective-permute-start(bf16[80,128]{1,0:T(8,128)(2,1)} %pack.1), channel_id=1, source_target_pairs={{0,8},{1,9},{2,10},{3,11},{4,12},{5,13},{6,14},{7,15},{8,0},{9,1},... | collective-permute-start | bytes 61448 | tf_op jit(solution)/shard_map/ppermute | solution.py:420
  12.4 6.2 %collective-permute-start.5 = (bf16[80,512]{1,0:T(8,128)(2,1)S(1)}, bf16[80,512]{1,0:T(8,128)(2,1)S(1)}, u32[]{:S(2)}, u32[]{:S(2)}) collective-permute-start(bf16[80,512]{1,0:T(8,128)(2,1)S(1)} %pad_maximum_fusion.refs_2_.refs_0_), channel_id=1, source_target_pairs={{0,6},{1,7},{2,4},{3,5},{4,2},{5,3},{6,0},{7,1},{8,14},{9,15},{10,... | collective-permute-start | bytes 245768 | tf_op jit(solution)/shard_map/ppermute | solution.py:420
  14.9 4.5 %collective-permute-start.4 = (bf16[80,512]{1,0:T(8,128)(2,1)S(1)}, bf16[80,512]{1,0:T(8,128)(2,1)S(1)}, u32[]{:S(2)}, u32[]{:S(2)}) collective-permute-start(bf16[80,512]{1,0:T(8,128)(2,1)S(1)} %pad_maximum_fusion.refs_2_.refs_0_), channel_id=1, source_target_pairs={{0,4},{1,5},{2,6},{3,7},{4,0},{5,1},{6,2},{7,3},{8,12},{9,13},{10,... | collective-permute-start | bytes 245768 | tf_op jit(solution)/shard_map/ppermute | solution.py:420
  15.4 4.4 %collective-permute-start.3 = (bf16[80,512]{1,0:T(8,128)(2,1)S(1)}, bf16[80,512]{1,0:T(8,128)(2,1)S(1)}, u32[]{:S(2)}, u32[]{:S(2)}) collective-permute-start(bf16[80,512]{1,0:T(8,128)(2,1)S(1)} %pad_maximum_fusion.refs_2_.refs_0_), channel_id=1, source_target_pairs={{0,2},{1,3},{2,0},{3,1},{4,6},{5,7},{6,4},{7,5},{8,10},{9,11},{10,... | collective-permute-start | bytes 245768 | tf_op jit(solution)/shard_map/ppermute | solution.py:420
  18.5 1.4 %collective-permute-start.9 = (bf16[80,512]{1,0:T(8,128)(2,1)S(1)}, bf16[80,512]{1,0:T(8,128)(2,1)S(1)}, u32[]{:S(2)}, u32[]{:S(2)}) collective-permute-start(bf16[80,512]{1,0:T(8,128)(2,1)S(1)} %pad_maximum_fusion.refs_2_.refs_0_), channel_id=1, source_target_pairs={{0,1},{1,0},{2,3},{3,2},{4,5},{5,4},{6,7},{7,6},{8,9},{9,8},{10,11... | collective-permute-start | bytes 245768 | tf_op jit(solution)/shard_map/ppermute | solution.py:420
  18.6 2.9 %collective-permute-start.8 = (bf16[80,512]{1,0:T(8,128)(2,1)S(1)}, bf16[80,512]{1,0:T(8,128)(2,1)S(1)}, u32[]{:S(2)}, u32[]{:S(2)}) collective-permute-start(bf16[80,512]{1,0:T(8,128)(2,1)S(1)} %collective-permute-done.5.refs_2_), channel_id=1, source_target_pairs={{0,1},{1,0},{2,3},{3,2},{4,5},{5,4},{6,7},{7,6},{8,9},{9,8},{10,11... | collective-permute-start | bytes 245768 | tf_op jit(solution)/shard_map/ppermute | solution.py:420
  19.4 2.1 %collective-permute-start.7 = (bf16[80,512]{1,0:T(8,128)(2,1)S(1)}, bf16[80,512]{1,0:T(8,128)(2,1)S(1)}, u32[]{:S(2)}, u32[]{:S(2)}) collective-permute-start(bf16[80,512]{1,0:T(8,128)(2,1)S(1)} %collective-permute-done.4.refs_1_), channel_id=1, source_target_pairs={{0,1},{1,0},{2,3},{3,2},{4,5},{5,4},{6,7},{7,6},{8,9},{9,8},{10,11... | collective-permute-start | bytes 245768 | tf_op jit(solution)/shard_map/ppermute | solution.py:420
  19.8 1.7 %collective-permute-start.6 = (bf16[80,512]{1,0:T(8,128)(2,1)S(1)}, bf16[80,512]{1,0:T(8,128)(2,1)S(1)}, u32[]{:S(2)}, u32[]{:S(2)}) collective-permute-start(bf16[80,512]{1,0:T(8,128)(2,1)S(1)} %collective-permute-done.3.refs_0_), channel_id=1, source_target_pairs={{0,1},{1,0},{2,3},{3,2},{4,5},{5,4},{6,7},{7,6},{8,9},{9,8},{10,11... | collective-permute-start | bytes 245768 | tf_op jit(solution)/shard_map/ppermute | solution.py:420
  31.8 2.0 %collective-permute-start.10 = (f32[80,1536]{1,0:T(8,128)S(1)}, f32[80,1536]{1,0:T(8,128)S(1)}, u32[]{:S(2)}, u32[]{:S(2)}) collective-permute-start(f32[80,1536]{1,0:T(8,128)S(1)} %get-tuple-element.84), channel_id=1, source_target_pairs={{0,1},{1,0},{2,3},{3,2},{4,5},{5,4},{6,7},{7,6},{8,9},{9,8},{10,11... | collective-permute-start | bytes 1474568 | tf_op jit(solution)/shard_map/ppermute | solution.py:420
  33.7 2.7 %collective-permute-start.11 = (f32[80,512]{1,0:T(8,128)S(1)}, f32[80,512]{1,0:T(8,128)S(1)}, u32[]{:S(2)}, u32[]{:S(2)}) collective-permute-start(f32[80,512]{1,0:T(8,128)S(1)} %get-tuple-element.85), channel_id=1, source_target_pairs={{0,1},{1,0},{2,3},{3,2},{4,5},{5,4},{6,7},{7,6},{8,9},{9,8},{10,11... | collective-permute-start | bytes 491528 | tf_op jit(solution)/shard_map/ppermute | solution.py:420
  33.9 5.4 %collective-permute-start.12 = (bf16[80,512]{1,0:T(8,128)(2,1)S(1)}, bf16[80,512]{1,0:T(8,128)(2,1)S(1)}, u32[]{:S(2)}, u32[]{:S(2)}) collective-permute-start(bf16[80,512]{1,0:T(8,128)(2,1)S(1)} %get-tuple-element.87), channel_id=1, source_target_pairs={{0,6},{1,25},{2,4},{3,27},{4,2},{5,29},{6,0},{7,31},{8,14},{9,17},... | collective-permute-start | bytes 245768 | tf_op jit(solution)/shard_map/ppermute | solution.py:420
  36.4 4.5 %collective-permute-start.14 = (bf16[80,512]{1,0:T(8,128)(2,1)S(1)}, bf16[80,512]{1,0:T(8,128)(2,1)S(1)}, u32[]{:S(2)}, u32[]{:S(2)}) collective-permute-start(bf16[80,512]{1,0:T(8,128)(2,1)S(1)} %get-tuple-element.89), channel_id=1, source_target_pairs={{0,4},{1,17},{2,6},{3,19},{4,0},{5,21},{6,2},{7,23},{8,12},{9,25},... | collective-permute-start | bytes 245768 | tf_op jit(solution)/shard_map/ppermute | solution.py:420
  37.0 4.4 %collective-permute-start.13 = (bf16[80,512]{1,0:T(8,128)(2,1)S(1)}, bf16[80,512]{1,0:T(8,128)(2,1)S(1)}, u32[]{:S(2)}, u32[]{:S(2)}) collective-permute-start(bf16[80,512]{1,0:T(8,128)(2,1)S(1)} %get-tuple-element.88), channel_id=1, source_target_pairs={{0,2},{1,9},{2,0},{3,11},{4,6},{5,13},{6,4},{7,15},{8,10},{9,1},{1... | collective-permute-start | bytes 245768 | tf_op jit(solution)/shard_map/ppermute | solution.py:420
  39.3 19.1 %copy-start.2 = (f32[2048,64]{0,1:T(8,128)S(1)}, f32[2048,64]{0,1:T(8,128)}, u32[]{:S(2)}) copy-start(f32[2048,64]{0,1:T(8,128)} %param.33) | copy-start | bytes 1572868
  39.3 19.1 %copy-start.3 = (f32[64,2048]{1,0:T(8,128)S(1)}, f32[64,2048]{1,0:T(8,128)}, u32[]{:S(2)}) copy-start(f32[64,2048]{1,0:T(8,128)} %refs_18_.1) | copy-start | bytes 1572868
  39.3 19.1 %copy-start.6 = (f32[100,100]{1,0:T(8,128)S(1)}, f32[100,100]{1,0:T(8,128)}, u32[]{:S(2)}) copy-start(f32[100,100]{1,0:T(8,128)} %refs_12_.1) | copy-start | bytes 120004
  39.3 19.1 %copy-start.7 = (f32[100,100]{1,0:T(8,128)S(1)}, f32[100,100]{1,0:T(8,128)}, u32[]{:S(2)}) copy-start(f32[100,100]{1,0:T(8,128)} %refs_16_.3) | copy-start | bytes 120004
  39.4 19.1 %copy-start.8 = (f32[100,64]{0,1:T(8,128)S(1)}, f32[100,64]{0,1:T(8,128)}, u32[]{:S(2)}) copy-start(f32[100,64]{0,1:T(8,128)} %param.24) | copy-start | bytes 76804
  39.4 19.1 %copy-start.9 = (f32[64,47]{0,1:T(8,128)S(1)}, f32[64,47]{0,1:T(8,128)}, u32[]{:S(2)}) copy-start(f32[64,47]{0,1:T(8,128)} %param.25) | copy-start | bytes 36100
  39.4 19.1 %copy-start.10 = (f32[47,47]{1,0:T(8,128)S(1)}, f32[47,47]{1,0:T(8,128)}, u32[]{:S(2)}) copy-start(f32[47,47]{1,0:T(8,128)} %refs_15_.1) | copy-start | bytes 26512
  41.5 6.3 %collective-permute-start.17 = (bf16[80,512]{1,0:T(8,128)(2,1)S(1)}, bf16[80,512]{1,0:T(8,128)(2,1)S(1)}, u32[]{:S(2)}, u32[]{:S(2)}) collective-permute-start(bf16[80,512]{1,0:T(8,128)(2,1)S(1)} %add_piece.1.refs_0_), channel_id=1, source_target_pairs={{0,24},{1,7},{2,26},{3,5},{4,28},{5,3},{6,30},{7,1},{8,16},{9,15},... | collective-permute-start | bytes 245768 | tf_op jit(solution)/shard_map/ppermute | solution.py:420
  43.7 6.4 %collective-permute-start.16 = (bf16[80,512]{1,0:T(8,128)(2,1)S(1)}, bf16[80,512]{1,0:T(8,128)(2,1)S(1)}, u32[]{:S(2)}, u32[]{:S(2)}) collective-permute-start(bf16[80,512]{1,0:T(8,128)(2,1)S(1)} %add_piece.1.refs_0_), channel_id=1, source_target_pairs={{0,16},{1,5},{2,18},{3,7},{4,20},{5,1},{6,22},{7,3},{8,24},{9,13},... | collective-permute-start | bytes 245768 | tf_op jit(solution)/shard_map/ppermute | solution.py:420
  43.7 6.4 %collective-permute-start.15 = (bf16[80,512]{1,0:T(8,128)(2,1)S(1)}, bf16[80,512]{1,0:T(8,128)(2,1)S(1)}, u32[]{:S(2)}, u32[]{:S(2)}) collective-permute-start(bf16[80,512]{1,0:T(8,128)(2,1)S(1)} %add_piece.1.refs_0_), channel_id=1, source_target_pairs={{0,8},{1,3},{2,10},{3,1},{4,12},{5,7},{6,14},{7,5},{8,0},{9,11},{1... | collective-permute-start | bytes 245768 | tf_op jit(solution)/shard_map/ppermute | solution.py:420
  50.1 5.4 %collective-permute-start.20 = (bf16[80,512]{1,0:T(8,128)(2,1)S(1)}, bf16[80,512]{1,0:T(8,128)(2,1)S(1)}, u32[]{:S(2)}, u32[]{:S(2)}) collective-permute-start(bf16[80,512]{1,0:T(8,128)(2,1)S(1)} %add_line.1.refs_0_), channel_id=1, source_target_pairs={{0,6},{1,25},{2,4},{3,27},{4,2},{5,29},{6,0},{7,31},{8,14},{9,17},... | collective-permute-start | bytes 245768 | tf_op jit(solution)/shard_map/ppermute | solution.py:420
  51.6 4.8 %collective-permute-start.19 = (bf16[80,512]{1,0:T(8,128)(2,1)S(1)}, bf16[80,512]{1,0:T(8,128)(2,1)S(1)}, u32[]{:S(2)}, u32[]{:S(2)}) collective-permute-start(bf16[80,512]{1,0:T(8,128)(2,1)S(1)} %add_line.1.refs_0_), channel_id=1, source_target_pairs={{0,4},{1,17},{2,6},{3,19},{4,0},{5,21},{6,2},{7,23},{8,12},{9,25},... | collective-permute-start | bytes 245768 | tf_op jit(solution)/shard_map/ppermute | solution.py:420
  52.7 4.4 %collective-permute-start.18 = (bf16[80,512]{1,0:T(8,128)(2,1)S(1)}, bf16[80,512]{1,0:T(8,128)(2,1)S(1)}, u32[]{:S(2)}, u32[]{:S(2)}) collective-permute-start(bf16[80,512]{1,0:T(8,128)(2,1)S(1)} %add_line.1.refs_0_), channel_id=1, source_target_pairs={{0,2},{1,9},{2,0},{3,11},{4,6},{5,13},{6,4},{7,15},{8,10},{9,1},{1... | collective-permute-start | bytes 245768 | tf_op jit(solution)/shard_map/ppermute | solution.py:420
  53.7 3.4 %collective-permute-start.21 = (bf16[80,512]{1,0:T(8,128)(2,1)S(1)}, bf16[80,512]{1,0:T(8,128)(2,1)S(1)}, u32[]{:S(2)}, u32[]{:S(2)}) collective-permute-start(bf16[80,512]{1,0:T(8,128)(2,1)S(1)} %add_line.1.refs_0_), channel_id=1, source_target_pairs={{0,1},{1,0},{2,3},{3,2},{4,5},{5,4},{6,7},{7,6},{8,9},{9,8},{10,11... | collective-permute-start | bytes 245768 | tf_op jit(solution)/shard_map/ppermute | solution.py:420
  55.6 1.5 %collective-permute-start.24 = (bf16[80,512]{1,0:T(8,128)(2,1)S(1)}, bf16[80,512]{1,0:T(8,128)(2,1)S(1)}, u32[]{:S(2)}, u32[]{:S(2)}) collective-permute-start(bf16[80,512]{1,0:T(8,128)(2,1)S(1)} %collective-permute-done.20.refs_3_), channel_id=1, source_target_pairs={{0,1},{1,0},{2,3},{3,2},{4,5},{5,4},{6,7},{7,6},{8,9},{9,8},{10,11... | collective-permute-start | bytes 245768 | tf_op jit(solution)/shard_map/ppermute | solution.py:420
  56.4 1.3 %collective-permute-start.23 = (bf16[80,512]{1,0:T(8,128)(2,1)S(1)}, bf16[80,512]{1,0:T(8,128)(2,1)S(1)}, u32[]{:S(2)}, u32[]{:S(2)}) collective-permute-start(bf16[80,512]{1,0:T(8,128)(2,1)S(1)} %collective-permute-done.19.refs_2_), channel_id=1, source_target_pairs={{0,1},{1,0},{2,3},{3,2},{4,5},{5,4},{6,7},{7,6},{8,9},{9,8},{10,11... | collective-permute-start | bytes 245768 | tf_op jit(solution)/shard_map/ppermute | solution.py:420
  57.1 1.3 %collective-permute-start.22 = (bf16[80,512]{1,0:T(8,128)(2,1)S(1)}, bf16[80,512]{1,0:T(8,128)(2,1)S(1)}, u32[]{:S(2)}, u32[]{:S(2)}) collective-permute-start(bf16[80,512]{1,0:T(8,128)(2,1)S(1)} %collective-permute-done.18.refs_1_), channel_id=1, source_target_pairs={{0,1},{1,0},{2,3},{3,2},{4,5},{5,4},{6,7},{7,6},{8,9},{9,8},{10,11... | collective-permute-start | bytes 245768 | tf_op jit(solution)/shard_map/ppermute | solution.py:420
  (14 other events, 176.3 us)
